TPU v7x, 32 devices: a whole 2x2x4 slice. The times are simulated.
32 devices in a mesh: shard: 16 (over z, y, x), replica: 2 (over core).
Axes of the slice: x: 2, y: 2, z: 4, core: 2. Of those that a mesh axis runs over, the one named last changes fastest.
Arguments:
- grads: bfloat16 [32, 196608], P(('shard', 'replica')), may hold values from -6 to 6
- master: float32 [196608], P(('shard', 'replica')), may hold values from -120 to 120
- first_moment: float32 [196608], P(('shard', 'replica')), may hold values from -0.15625 to 0.15625
- second_moment: float32 [196608], P(('shard', 'replica')), may hold values from 1e-05 to 0.001
- owners: int32 [24], replicated, may hold values from 0 to 15, as said below
Outputs:
- new_master: float32 [196608], P(('shard', 'replica'))
- new_first: float32 [196608], P(('shard', 'replica'))
- new_second: float32 [196608], P(('shard', 'replica'))
- model_copy: bfloat16 [24, 8192], replicated
Inputs may be any that keep to these rules, and one draw needn't show every extreme that they name: owners[c] names the index along shard that owns model column c; no index owns more than 3 columns, and one owns exactly 3.
All inputs are finite; a program needn't handle non-finite values.
Results may differ from a plain program's by a relative error of at most 0.0085.
Values may be sent and summed in bfloat16 or wider, within the bound.
No kernel may reach another device: no remote copies, remote signals or barrier semaphores. Data moves between devices by JAX's collectives and lax.ppermute only.
A program may use at most 64 MiB of HBM per device.

v0:
```python
import jax
import jax.numpy as jnp
from jax import lax
from jax.sharding import PartitionSpec as P

D = 8192


learning_rate = 0.1
adam_epsilon = 1e-08
norm_epsilon = 1e-06
first_correction = 1.0 - 0.9**20
second_correction = 1.0 - 0.95**20


def adam_step(gradient, master, first_moment, second_moment):
    new_first = 0.9 * first_moment + 0.1 * gradient
    new_second = 0.95 * second_moment + 0.05 * gradient * gradient
    stepped = master - learning_rate * (new_first / first_correction) / (
        jnp.sqrt(new_second / second_correction) + adam_epsilon
    )
    return (new_first, new_second, stepped)


def flat_positions(owners):
    column_ids = jnp.arange(owners.shape[0], dtype=jnp.int32)
    ranked_below = owners[None, :] < owners[:, None]
    same_before = (owners[None, :] == owners[:, None]) & (column_ids[None, :] < column_ids[:, None])
    return jnp.sum((ranked_below | same_before).astype(jnp.int32), axis=1)


def slot_selector(owners, slots_each, shards):
    column_ids = jnp.arange(owners.shape[0], dtype=jnp.int32)
    owner_ids = jnp.arange(shards, dtype=jnp.int32)
    counts = jnp.sum((owners[None, :] == owner_ids[:, None]).astype(jnp.int32), axis=1)
    starts = jnp.sum((owners[None, :] < owner_ids[:, None]).astype(jnp.int32), axis=1)
    slot_ids = jnp.arange(slots_each, dtype=jnp.int32)
    target = starts[:, None] + slot_ids[None, :]
    usable = slot_ids[None, :] < counts[:, None]
    hits = (column_ids[None, None, :] == target[:, :, None]) & usable[:, :, None]
    return hits.astype(jnp.float32)


def on_device(grads, master, first_moment, second_moment, owners):
    flat_values = grads.reshape(-1)
    shards = lax.axis_size("shard")
    replicas = lax.axis_size("replica")
    summed = lax.psum_scatter(
        flat_values.astype(jnp.float32), ("shard", "replica"), scatter_dimension=0, tiled=True
    )
    gradient = summed / (shards * replicas)
    new_first, new_second, stepped = adam_step(gradient, master, first_moment, second_moment)
    column_total = owners.shape[0]
    matrix = stepped.reshape(-1, column_total)
    slots_each = max(2, 5 * column_total // (2 * shards))
    selector = slot_selector(owners, slots_each, shards)
    outgoing = jnp.einsum("qjc,rc->qjr", selector, matrix, precision=lax.Precision.HIGHEST)
    delivered = lax.all_to_all(outgoing, "shard", split_axis=0, concat_axis=0, tiled=True)
    squares = jnp.sum(delivered * delivered, axis=(0, 2))
    sum_squares = lax.psum(squares, "replica")
    factor = lax.rsqrt(sum_squares / D + norm_epsilon)
    returned = lax.all_to_all(
        delivered * factor[None, :, None], "shard", split_axis=0, concat_axis=0, tiled=True
    )
    normed = jnp.einsum("qjc,qjr->rc", selector, returned, precision=lax.Precision.HIGHEST)
    position = flat_positions(owners)
    column_ids = jnp.arange(column_total, dtype=jnp.int32)
    placement = (position[:, None] == column_ids[None, :]).astype(jnp.float32)
    model_rows = jnp.einsum("cj,rj->cr", placement, normed, precision=lax.Precision.HIGHEST).astype(
        jnp.bfloat16
    )
    model_copy = lax.all_gather(model_rows, ("shard", "replica"), axis=1, tiled=True)
    return (normed.reshape(-1), new_first, new_second, model_copy)


def solution(mesh):
    placed = (
        P(("shard", "replica"), None),
        P(("shard", "replica")),
        P(("shard", "replica")),
        P(("shard", "replica")),
        P(),
    )
    return jax.shard_map(
        on_device,
        mesh=mesh,
        in_specs=placed,
        out_specs=(P(("shard", "replica")), P(("shard", "replica")), P(("shard", "replica")), P()),
        check_vma=False,
    )
```

profile of v0, /device:TPU:0, one launch (start us, length us, event | category | flops | bytes accessed | tf_op | source)
XLA Modules:
  0.0 220.1 jit_solution(3856736315015643707)
XLA Ops:
  7.2 0.0 all-reduce.3.cloned.1.call-start
  7.2 2.6 %convert_element_type.26 = f32[1,196608]{1,0:T(1,128)} convert(bf16[1,196608]{1,0:T(2,128)(2,1)} %param.5) | non-fusion elementwise | flops 196608 | bytes 1179648 | tf_op jit(solution)/shard_map/convert_element_type | solution.py:49
  9.8 0.0 all-reduce.3.cloned.1.call-update
  9.8 0.0 copy-start
  9.9 0.6 copy-done.3
  10.5 0.1 convert_reduce_fusion.1
  10.6 134.3 %all-reduce.3.cloned.1.call-done = f32[196608]{0:T(1024)} async-done(((f32[196608]{0:T(1024)}), f32[196608]{0:T(1024)}) %all-reduce.3.cloned.1.call-update) | async-done | bytes 786448
  144.9 0.0 copy-done.1
  144.9 1.4 divide_subtract_fusion
  146.3 0.1 reshape.63
  146.4 0.2 fusion
  146.7 11.9 %all_to_all.10 = f32[16,3,256]{2,1,0:T(4,128)S(1)} all-to-all(f32[16,3,256]{2,1,0:T(4,128)S(1)} %copy.16), channel_id=1, replica_groups=mesh['shard'=16,'replica'=2] {'shard'}, dimensions={0} | all-to-all | bytes 98304 | tf_op jit(solution)/shard_map/all_to_all | solution.py:58
  158.6 0.1 multiply_reduce_fusion
  158.8 2.5 %psum.7 = f32[3]{0:T(128)S(1)} all-reduce(f32[3]{0:T(128)S(1)} %multiply_reduce_fusion), channel_id=1, replica_groups=mesh['shard'=16,'replica'=2] {'replica'}, use_global_device_ids=true, to_apply=%region_4.0 | all-reduce | flops 3 | bytes 24 | tf_op jit(solution)/shard_map/psum | solution.py:60
  161.3 0.7 broadcast_multiply_fusion
  162.0 3.5 %all-to-all-start.1 = ((f32[16,3,256]{2,1,0:T(4,128)}), f32[16,3,256]{2,1,0:T(4,128)S(1)}, u32[]{:S(2)}, u32[]{:S(2)}) async-start(f32[16,3,256]{2,1,0:T(4,128)} %broadcast_multiply_fusion), calls=%async_computation.1 | async-start | bytes 131072 | tf_op jit(solution)/shard_map/all_to_all | solution.py:62
  165.5 0.2 convert_reduce_fusion
  165.7 7.3 %all-to-all-done.1 = f32[16,3,256]{2,1,0:T(4,128)S(1)} async-done(((f32[16,3,256]{2,1,0:T(4,128)}), f32[16,3,256]{2,1,0:T(4,128)S(1)}, u32[]{:S(2)}, u32[]{:S(2)}) %all-to-all-start.1) | async-done | bytes 49184 | tf_op jit(solution)/shard_map/all_to_all | solution.py:62
  173.0 0.3 convolution_bitcast_fusion
  173.3 0.1 copy.18
  173.4 0.2 convolution_convert_fusion
  173.6 38.3 %all_gather.3 = bf16[24,8192]{1,0:T(8,128)(2,1)S(1)} all-gather(bf16[24,256]{1,0:T(8,128)(2,1)S(1)} %convolution_convert_fusion), channel_id=1, replica_groups=mesh['shard'=16,'replica'=2] {'shard','replica'}, dimensions={1}, use_global_device_ids=true | all-gather | bytes 405504 | tf_op jit(solution)/shard_map/all_gather | solution.py:72
  211.8 0.7 reshape.64
  212.5 0.7 copy.25
  (9 shorter events, 0.1 us)
Async XLA Ops:
  7.2 137.8 %all-reduce.3.cloned.1.call-start = ((), (), s32[]{:S(2)}) async-start(), calls=%async_computation.2 | async-start | bytes 1572864
  9.8 0.7 copy-start.3
  9.8 135.1 %copy-start.1 = (f32[6144]{0:T(1024)S(1)}, f32[6144]{0:T(1024)}, u32[]{:S(2)}) copy-start(f32[6144]{0:T(1024)} %param.7) | copy-start | bytes 73732
  9.8 135.1 %copy-start.2 = (f32[6144]{0:T(1024)S(1)}, f32[6144]{0:T(1024)}, u32[]{:S(2)}) copy-start(f32[6144]{0:T(1024)} %param.8) | copy-start | bytes 73732
  9.8 135.1 %copy-start = (f32[6144]{0:T(1024)S(1)}, f32[6144]{0:T(1024)}, u32[]{:S(2)}) copy-start(f32[6144]{0:T(1024)} %param.6) | copy-start | bytes 73732
  162.0 11.0 %all-to-all-start.1 = ((f32[16,3,256]{2,1,0:T(4,128)}), f32[16,3,256]{2,1,0:T(4,128)S(1)}, u32[]{:S(2)}, u32[]{:S(2)}) async-start(f32[16,3,256]{2,1,0:T(4,128)} %broadcast_multiply_fusion), calls=%async_computation.1 | async-start | bytes 131072 | tf_op jit(solution)/shard_map/all_to_all | solution.py:62
Sparse Core Ops, SparseCore 0:
  13.2 131.6 all-reduce.2
where the time goes:
time: 221 us; the launch traced here: 220 us
  waiting for transfers between devices  142 us (64%)
  blocking collectives  52.7 us (24%)
  between operations  14.1 us (6%)
  other arithmetic  5.14 us (2%)
  starting transfers between devices  3.54 us (2%)
  local copies, waits for them, and re-layouts  2.32 us (1%)
    unnamed x2, waiting for transfers between devices  134 us
    all_gather x1, blocking collectives, on_device(): lax.all_gather(model_rows, ('shard', 'replica'), axis=1, tiled=True)  38.3 us
    all_to_all x1, blocking collectives, on_device(): lax.all_to_all(outgoing, 'shard', split_axis=0, concat_axis=0, tiled=True)  11.9 us
    all_to_all x1, waiting for transfers between devices, on_device(): lax.all_to_all(delivered * factor[None, :, None], 'shard', split_axis=0,...  7.32 us
  transfers between devices with their start and end apart: 2, of which 2 were waited for; matrix products, arithmetic and copies ran while one was open for 0% of the time, Pallas kernels for 0%

commit v1 on v0

v1 whole, which is shorter than its diff:
```python
import jax
import jax.numpy as jnp
from jax import lax
from jax.sharding import PartitionSpec as P

D = 8192


learning_rate = 0.1
adam_epsilon = 1e-08
norm_epsilon = 1e-06
first_correction = 1.0 - 0.9**20
second_correction = 1.0 - 0.95**20
AXES = ("shard", "replica")


def adam_step(gradient, master, first_moment, second_moment):
    new_first = 0.9 * first_moment + 0.1 * gradient
    new_second = 0.95 * second_moment + 0.05 * gradient * gradient
    stepped = master - learning_rate * (new_first / first_correction) / (
        jnp.sqrt(new_second / second_correction) + adam_epsilon
    )
    return (new_first, new_second, stepped)


def flat_positions(owners):
    column_ids = jnp.arange(owners.shape[0], dtype=jnp.int32)
    ranked_below = owners[None, :] < owners[:, None]
    same_before = (owners[None, :] == owners[:, None]) & (column_ids[None, :] < column_ids[:, None])
    return jnp.sum((ranked_below | same_before).astype(jnp.int32), axis=1)


def on_device(grads, master, first_moment, second_moment, owners):
    devices = lax.axis_size("shard") * lax.axis_size("replica")
    chunk = master.shape[0]
    columns = owners.shape[0]
    pieces = lax.all_to_all(grads.reshape(devices, chunk // 128, 128), AXES, 0, 0, tiled=True)
    gradient = jnp.sum(pieces.astype(jnp.float32), axis=0).reshape(-1) / devices
    new_first, new_second, stepped = adam_step(gradient, master, first_moment, second_moment)
    matrix = stepped.reshape(-1, columns)
    position = flat_positions(owners)
    column_ids = jnp.arange(columns, dtype=jnp.int32)
    placement = (position[:, None] == column_ids[None, :]).astype(jnp.bfloat16)
    rows = jnp.einsum(
        "cj,rj->cr", placement, matrix.astype(jnp.bfloat16), preferred_element_type=jnp.float32
    ).astype(jnp.bfloat16)
    gathered = lax.all_to_all(
        jnp.broadcast_to(rows[None], (devices,) + rows.shape), AXES, 0, 0, tiled=True
    )
    wide = gathered.astype(jnp.float32)
    factor = lax.rsqrt(jnp.sum(wide * wide, axis=(0, 2)) / D + norm_epsilon)
    model_copy = jnp.transpose(wide * factor[None, :, None], (1, 0, 2)).reshape(columns, -1)
    flat_factor = jnp.sum(jnp.where(position[:, None] == column_ids[None, :], factor[:, None], 0.0), axis=0)
    new_master = (matrix * flat_factor[None, :]).reshape(-1)
    return (new_master, new_first, new_second, model_copy.astype(jnp.bfloat16))


def solution(mesh):
    placed = (P(AXES, None), P(AXES), P(AXES), P(AXES), P())
    return jax.shard_map(
        on_device,
        mesh=mesh,
        in_specs=placed,
        out_specs=(P(AXES), P(AXES), P(AXES), P()),
        check_vma=False,
    )
```

time: 221 us -> 50 us (0.23)
  waiting for transfers between devices: 142 us -> 13 us
  blocking collectives: 52.7 us -> 15.6 us
  between operations: 14.1 us -> 0.72 us
  other arithmetic: 5.14 us -> 11.9 us
  starting transfers between devices: 3.54 us -> 7.3 us
    unnamed x2 -> x0, waiting for transfers between devices: 134 us -> none
    all_gather x1 -> x0, blocking collectives: 38.3 us -> none  [on_device(): lax.all_gather(model_rows, ('shard', 'replica'), axis=1, tiled=True)]
    unnamed x0 -> x2, other arithmetic: none -> 10.1 us
    all_to_all x1, waiting for transfers between devices: 7.32 us -> 13 us  [on_device(): lax.all_to_all(grads.reshape(devices, chunk // 128, 128), AXES, 0, 0, til...]
    all_to_all x1, starting transfers between devices: 3.5 us -> 7.3 us  [on_device(): lax.all_to_all(grads.reshape(devices, chunk // 128, 128), AXES, 0, 0, til...]
    all_to_all x1, blocking collectives: 11.9 us -> 15.6 us  [on_device(): lax.all_to_all(jnp.broadcast_to(rows[None], (devices,) + rows.shape), AXE...]
    psum x1 -> x0, blocking collectives: 2.46 us -> none  [on_device(): sum_squares = lax.psum(squares, 'replica')]
  transfers between devices with their start and end apart: 2 -> 1, of which waited for: 2 -> 1; matrix products, arithmetic and copies ran while one was open for 0% -> 0% of each run, Pallas kernels for 0% -> 0%
where the time goes in v1:
time: 50 us; the launch traced here: 49.8 us
  blocking collectives  15.6 us (31%)
  waiting for transfers between devices  13 us (26%)
  other arithmetic  11.9 us (24%)
  starting transfers between devices  7.3 us (15%)
  local copies, waits for them, and re-layouts  1.09 us (2%)
  between operations  0.72 us (1%)
    all_to_all x1, blocking collectives, on_device(): lax.all_to_all(jnp.broadcast_to(rows[None], (devices,) + rows.shape), AXE...  15.6 us
    all_to_all x1, waiting for transfers between devices, on_device(): lax.all_to_all(grads.reshape(devices, chunk // 128, 128), AXES, 0, 0, til...  13 us
    unnamed x2, other arithmetic  10.1 us
    all_to_all x1, starting transfers between devices, on_device(): lax.all_to_all(grads.reshape(devices, chunk // 128, 128), AXES, 0, 0, til...  7.3 us
  transfers between devices with their start and end apart: 1, of which 1 were waited for; matrix products, arithmetic and copies ran while one was open for 0% of the time, Pallas kernels for 0%

profile of v1, /device:TPU:0, one launch (start us, length us, event | category | flops | bytes accessed | tf_op | source)
XLA Modules:
  0.0 49.8 jit_solution(14390136799042202378)
XLA Ops:
  0.6 9.9 %reduce = bf16[196608]{0:T(1024)(128)(2,1)} reduce(bf16[1,196608]{1,0:T(2,128)(2,1)} %param.5, bf16[]{:T(256)} %constant.32), dimensions={0}, to_apply=%param.5.reduce_sub_computation | reduce | bytes 786434 | tf_op args[0]
  10.5 0.0 copy-start.3
  10.5 7.3 %all-to-all-start = ((bf16[32,48,128]{2,1,0:T(8,128)(2,1)}), bf16[32,48,128]{2,1,0:T(8,128)(2,1)S(1)}, u32[]{:S(2)}, u32[]{:S(2)}) async-start(bf16[32,48,128]{2,1,0:T(8,128)(2,1)} %bitcast.3), calls=%async_computation | async-start | bytes 786432 | tf_op jit(solution)/shard_map/all_to_all | solution.py:37
  17.8 0.0 copy-done.3
  17.8 0.2 convert_reduce_fusion.1
  18.0 0.0 copy-start
  18.0 0.0 copy-start.1
  18.0 0.0 copy-start.2
  18.0 13.0 %all-to-all-done = bf16[32,48,128]{2,1,0:T(8,128)(2,1)S(1)} async-done(((bf16[32,48,128]{2,1,0:T(8,128)(2,1)}), bf16[32,48,128]{2,1,0:T(8,128)(2,1)S(1)}, u32[]{:S(2)}, u32[]{:S(2)}) %all-to-all-start) | async-done | bytes 393248 | tf_op jit(solution)/shard_map/all_to_all | solution.py:37
  31.0 0.1 convert_reduce_fusion
  31.1 0.0 copy-done
  31.1 0.0 copy-done.1
  31.1 0.0 copy-done.2
  31.1 0.6 %fusion.6 = (bf16[6144]{0:T(1024)(128)(2,1)S(1)}, f32[6144]{0:T(1024)S(1)}, f32[6144]{0:T(1024)}, f32[6144]{0:T(1024)}) fusion(f32[6144]{0:T(1024)S(1)} %copy-done, f32[48,128]{1,0:T(8,128)S(1)} %convert_reduce_fusion, f32[6144]{0:T(1024)S(1)} %copy-done.1, f32[6144]{0:T(1024)S(1)} %copy-done.2), kind=kLoop, calls=%fused_computation.18 | loop fusion | flops 86016 | bytes 184320 | tf_op jit(solution)/shard_map/convert_element_type | solution.py:45
  31.7 0.1 convert_element_type.31
  31.9 0.2 convolution_convert_fusion
  32.0 0.1 broadcast_in_dim.10
  32.1 15.6 %all_to_all.10 = bf16[32,24,256]{2,1,0:T(8,128)(2,1)S(1)} all-to-all(bf16[32,24,256]{2,1,0:T(8,128)(2,1)S(1)} %broadcast_in_dim.10), channel_id=1, replica_groups=mesh['shard'=16,'replica'=2] {'shard','replica'}, dimensions={0} | all-to-all | bytes 786432 | tf_op jit(solution)/shard_map/all_to_all | solution.py:47
  47.7 0.2 fusion
  47.9 0.1 select_reduce_fusion
  48.0 0.2 fusion.2
  48.3 0.8 %copy.11 = bf16[32,3,8,256]{3,2,0,1:T(8,128)(2,1)} copy(bf16[32,3,8,256]{3,2,1,0:T(8,128)(2,1)S(1)} %fusion.2) | data formatting | bytes 786432 | tf_op jit(solution)/shard_map/convert_element_type | solution.py:55
  49.0 0.1 mul.75
  49.2 0.6 %mul.76 = f32[6144]{0:T(1024)} multiply(f32[6144]{0:T(1024)S(1)} %get-tuple-element.5, f32[6144]{0:T(1024)S(1)} %mul.75) | non-fusion elementwise | flops 6144 | bytes 73728 | tf_op jit(solution)/shard_map/mul | solution.py:54
  (2 shorter events, 0.0 us)
Async XLA Ops:
  10.5 7.3 %copy-start.3 = (s32[24]{0:T(128)S(1)}, s32[24]{0:T(128)}, u32[]{:S(2)}) copy-start(s32[24]{0:T(128)} %param.9) | copy-start | bytes 292
  10.5 20.5 %all-to-all-start = ((bf16[32,48,128]{2,1,0:T(8,128)(2,1)}), bf16[32,48,128]{2,1,0:T(8,128)(2,1)S(1)}, u32[]{:S(2)}, u32[]{:S(2)}) async-start(bf16[32,48,128]{2,1,0:T(8,128)(2,1)} %bitcast.3), calls=%async_computation | async-start | bytes 786432 | tf_op jit(solution)/shard_map/all_to_all | solution.py:37
  18.0 13.1 %copy-start = (f32[6144]{0:T(1024)S(1)}, f32[6144]{0:T(1024)}, u32[]{:S(2)}) copy-start(f32[6144]{0:T(1024)} %param.6) | copy-start | bytes 73732
  18.0 13.1 %copy-start.1 = (f32[6144]{0:T(1024)S(1)}, f32[6144]{0:T(1024)}, u32[]{:S(2)}) copy-start(f32[6144]{0:T(1024)} %param.7) | copy-start | bytes 73732
  18.0 13.1 %copy-start.2 = (f32[6144]{0:T(1024)S(1)}, f32[6144]{0:T(1024)}, u32[]{:S(2)}) copy-start(f32[6144]{0:T(1024)} %param.8) | copy-start | bytes 73732

commit v2 on v1

--- a/solution.py
+++ b/solution.py
@@ -1,6 +1,7 @@
 import jax
 import jax.numpy as jnp
 from jax import lax
+from jax.experimental import pallas as pl
 from jax.sharding import PartitionSpec as P
 
 D = 8192
@@ -12,6 +13,7 @@
 first_correction = 1.0 - 0.9**20
 second_correction = 1.0 - 0.95**20
 AXES = ("shard", "replica")
+LANES = 128
 
 
 def adam_step(gradient, master, first_moment, second_moment):
@@ -30,11 +32,81 @@
     return jnp.sum((ranked_below | same_before).astype(jnp.int32), axis=1)
 
 
+def pack_kernel(grads_ref, out_ref):
+    devices, lines, lanes = out_ref.shape
+    for k in range(devices):
+        row = grads_ref[:, k * lines * lanes : (k + 1) * lines * lanes].astype(jnp.float32)
+        out_ref[k] = row.reshape(lines, lanes).astype(jnp.bfloat16)
+
+
+def pack(grads, devices):
+    lines = grads.shape[1] // devices // LANES
+    return pl.pallas_call(
+        pack_kernel, out_shape=jax.ShapeDtypeStruct((devices, lines, LANES), jnp.bfloat16)
+    )(grads)
+
+
+def finish_kernel(owners_ref, stepped_ref, own_ref, other_ref, master_ref, copy_ref):
+    core = lax.axis_index("replica")
+    chips, columns, width = own_ref.shape
+    total = jnp.zeros((columns, width), jnp.float32)
+    for ref in (own_ref, other_ref):
+        for c in range(chips):
+            value = ref[c].astype(jnp.float32)
+            total = total + value * value
+    factor = lax.rsqrt(jnp.sum(total, axis=1, keepdims=True) / D + norm_epsilon)
+    for ref, place in ((own_ref, core), (other_ref, 1 - core)):
+        for c in range(chips):
+            start = pl.multiple_of((2 * c + place) * width, width)
+            copy_ref[:, pl.ds(start, width)] = (ref[c].astype(jnp.float32) * factor).astype(jnp.bfloat16)
+    square = (columns, columns)
+    down = lax.broadcasted_iota(jnp.int32, square, 0)
+    along = lax.broadcasted_iota(jnp.int32, square, 1)
+    owner_row = jnp.broadcast_to(owners_ref[...].astype(jnp.float32), square)
+    owner_column = jnp.sum(jnp.where(down == along, owner_row, 0.0), axis=1, keepdims=True)
+    before = (owner_row < owner_column) | ((owner_row == owner_column) & (along < down))
+    position = jnp.sum(before.astype(jnp.float32), axis=1, keepdims=True).astype(jnp.int32)
+    period = columns // 8
+    lane = lax.broadcasted_iota(jnp.int32, (1, LANES), 1)
+    line = lax.broadcasted_iota(jnp.int32, stepped_ref.shape, 0) % period
+    spread = jnp.zeros(stepped_ref.shape, jnp.float32)
+    for p in range(period):
+        flat_column = (p * LANES + lane) % columns
+        picked = jnp.sum(jnp.where(position == flat_column, factor, 0.0), axis=0, keepdims=True)
+        spread = jnp.where(line == p, picked, spread)
+    master_ref[...] = stepped_ref[...] * spread
+
+
+def finish_narrow(owners, stepped, blocks):
+    columns = owners.shape[0]
+    blocks = blocks.astype(jnp.float32)
+    factor = lax.rsqrt(jnp.sum(blocks * blocks, axis=(0, 2)) / D + norm_epsilon)
+    scaled = jnp.transpose(blocks * factor[None, :, None], (1, 0, 2))
+    flat_factor = jnp.zeros((columns,), jnp.float32).at[flat_positions(owners)].set(factor)
+    new_master = (stepped.reshape(-1, columns) * flat_factor).reshape(stepped.shape)
+    return (new_master, scaled.reshape(columns, -1).astype(jnp.bfloat16))
+
+
+def spread(value, axes, size):
+    return lax.all_to_all(jnp.broadcast_to(value[None], (size,) + value.shape), axes, 0, 0, tiled=True)
+
+
+def finish(owners, stepped, own, other):
+    chips, columns, width = own.shape
+    return pl.pallas_call(
+        finish_kernel,
+        out_shape=(
+            jax.ShapeDtypeStruct(stepped.shape, jnp.float32),
+            jax.ShapeDtypeStruct((columns, 2 * chips * width), jnp.bfloat16),
+        ),
+    )(owners[None, :], stepped, own, other)
+
+
 def on_device(grads, master, first_moment, second_moment, owners):
-    devices = lax.axis_size("shard") * lax.axis_size("replica")
-    chunk = master.shape[0]
+    shards, replicas = lax.axis_size("shard"), lax.axis_size("replica")
+    devices = shards * replicas
     columns = owners.shape[0]
-    pieces = lax.all_to_all(grads.reshape(devices, chunk // 128, 128), AXES, 0, 0, tiled=True)
+    pieces = lax.all_to_all(pack(grads, devices), AXES, 0, 0, tiled=True)
     gradient = jnp.sum(pieces.astype(jnp.float32), axis=0).reshape(-1) / devices
     new_first, new_second, stepped = adam_step(gradient, master, first_moment, second_moment)
     matrix = stepped.reshape(-1, columns)
@@ -44,15 +116,14 @@
     rows = jnp.einsum(
         "cj,rj->cr", placement, matrix.astype(jnp.bfloat16), preferred_element_type=jnp.float32
     ).astype(jnp.bfloat16)
-    gathered = lax.all_to_all(
-        jnp.broadcast_to(rows[None], (devices,) + rows.shape), AXES, 0, 0, tiled=True
-    )
-    wide = gathered.astype(jnp.float32)
-    factor = lax.rsqrt(jnp.sum(wide * wide, axis=(0, 2)) / D + norm_epsilon)
-    model_copy = jnp.transpose(wide * factor[None, :, None], (1, 0, 2)).reshape(columns, -1)
-    flat_factor = jnp.sum(jnp.where(position[:, None] == column_ids[None, :], factor[:, None], 0.0), axis=0)
-    new_master = (matrix * flat_factor[None, :]).reshape(-1)
-    return (new_master, new_first, new_second, model_copy.astype(jnp.bfloat16))
+    flat_stepped = stepped.reshape(-1, LANES)
+    if replicas == 2 and rows.shape[1] % LANES == 0:
+        own = spread(rows, "shard", shards)
+        other = lax.ppermute(own, "replica", [(0, 1), (1, 0)])
+        new_master, model_copy = finish(owners, flat_stepped, own, other)
+    else:
+        new_master, model_copy = finish_narrow(owners, flat_stepped, spread(rows, AXES, devices))
+    return (new_master.reshape(-1), new_first, new_second, model_copy)
 
 
 def solution(mesh):

time: 50 us -> 40.6 us (0.81)
  other arithmetic: 11.9 us -> 0.88 us
  Pallas kernels: 0 us -> 4.01 us
  blocking collectives: 15.6 us -> 12.1 us
  waiting for transfers between devices: 13 us -> 14.4 us
    unnamed x2 -> x0, other arithmetic: 10.1 us -> none
    pallas_call x0 -> x2, Pallas kernels: none -> 4.01 us  [the longest x1 2.02 us: pack(): pl.pallas_call(pack_kernel, out_shape=jax.ShapeDtypeStruct((devices, line...]
    all_to_all x1, blocking collectives: 15.6 us -> 12.1 us  [spread(): lax.all_to_all(jnp.broadcast_to(value[None], (size,) + value.shape), axes...]
    ppermute x0 -> x1, waiting for transfers between devices: none -> 1.44 us  [on_device(): other = lax.ppermute(own, 'replica', [(0, 1), (1, 0)])]
    convert_element_type x1 -> x0, local copies, waits for them, and re-layouts: 0.77 us -> none  [on_device(): return (new_master, new_first, new_second, model_copy.astype(jnp.bfloat16))]
    unnamed x8 -> x12, local copies, waits for them, and re-layouts: 0.02 us -> 0.69 us
    mul x1 -> x0, other arithmetic: 0.61 us -> none  [on_device(): new_master = (matrix * flat_factor[None, :]).reshape(-1)]
  transfers between devices with their start and end apart: 1 -> 2, of which waited for: 1 -> 2; matrix products, arithmetic and copies ran while one was open for 0% -> 0% of each run, Pallas kernels for 0% -> 0%
where the time goes in v2:
time: 40.6 us; the launch traced here: 40.4 us
  waiting for transfers between devices  14.4 us (35%)
  blocking collectives  12.1 us (30%)
  starting transfers between devices  7.3 us (18%)
  Pallas kernels  4.01 us (10%)
  other arithmetic  0.88 us (2%)
  local copies, waits for them, and re-layouts  0.85 us (2%)
  between operations  0.71 us (2%)
    all_to_all x1, waiting for transfers between devices, on_device(): pieces = lax.all_to_all(pack(grads, devices), AXES, 0, 0, tiled=True)  13 us
    all_to_all x1, blocking collectives, spread(): lax.all_to_all(jnp.broadcast_to(value[None], (size,) + value.shape), axes...  12.1 us
    all_to_all x1, starting transfers between devices, on_device(): pieces = lax.all_to_all(pack(grads, devices), AXES, 0, 0, tiled=True)  7.3 us
    pallas_call x1, Pallas kernels, pack(): pl.pallas_call(pack_kernel, out_shape=jax.ShapeDtypeStruct((devices, line...  2.02 us
    pallas_call x1, Pallas kernels, finish(): pl.pallas_call(finish_kernel, out_shape=(jax.ShapeDtypeStruct(stepped.sha...  1.99 us
    ppermute x1, waiting for transfers between devices, on_device(): other = lax.ppermute(own, 'replica', [(0, 1), (1, 0)])  1.44 us
  transfers between devices with their start and end apart: 2, of which 2 were waited for; matrix products, arithmetic and copies ran while one was open for 0% of the time, Pallas kernels for 0%

profile of v2, /device:TPU:0, one launch (start us, length us, event | category | flops | bytes accessed | tf_op | source)
XLA Modules:
  0.0 40.4 jit_solution(140040257204897250)
XLA Ops:
  0.6 2.0 %shard_map.84 = bf16[32,48,128]{2,1,0:T(8,128)(2,1)} custom-call(bf16[1,196608]{1,0:T(2,128)(2,1)} %grads_ref.1), custom_call_target="tpu_custom_call" | custom-call | tf_op jit(solution)/shard_map/pallas_call | solution.py:44
  2.7 0.0 copy-start.5
  2.7 7.3 %all-to-all-start = ((bf16[32,48,128]{2,1,0:T(8,128)(2,1)}), bf16[32,48,128]{2,1,0:T(8,128)(2,1)S(1)}, u32[]{:S(2)}, u32[]{:S(2)}) async-start(bf16[32,48,128]{2,1,0:T(8,128)(2,1)} %shard_map.84), calls=%async_computation | async-start | bytes 786432 | tf_op jit(solution)/shard_map/all_to_all | solution.py:109
  10.0 0.0 copy-done.5
  10.0 0.2 convert_reduce_fusion.1
  10.2 0.0 copy-start.2
  10.2 0.0 copy-start.3
  10.2 0.0 copy-start.4
  10.2 13.0 %all-to-all-done = bf16[32,48,128]{2,1,0:T(8,128)(2,1)S(1)} async-done(((bf16[32,48,128]{2,1,0:T(8,128)(2,1)}), bf16[32,48,128]{2,1,0:T(8,128)(2,1)S(1)}, u32[]{:S(2)}, u32[]{:S(2)}) %all-to-all-start) | async-done | bytes 393248 | tf_op jit(solution)/shard_map/all_to_all | solution.py:109
  23.1 0.1 convert_reduce_fusion
  23.2 0.0 copy-done.2
  23.2 0.0 copy-done.3
  23.2 0.0 copy-done.4
  23.2 0.6 %fusion.3 = (bf16[6144]{0:T(1024)(128)(2,1)S(1)}, f32[6144]{0:T(1024)}, f32[6144]{0:T(1024)}, f32[6144]{0:T(1024)}) fusion(f32[6144]{0:T(1024)S(1)} %copy-done.2, f32[48,128]{1,0:T(8,128)S(1)} %convert_reduce_fusion, f32[6144]{0:T(1024)S(1)} %copy-done.3, f32[6144]{0:T(1024)S(1)} %copy-done.4), kind=kLoop, calls=%fused_computation.11 | loop fusion | flops 86016 | bytes 184320 | tf_op jit(solution)/shard_map/convert_element_type | solution.py:117
  23.9 0.1 convert_element_type.19
  24.0 0.2 convolution_convert_fusion
  24.2 12.1 %all_to_all.10.own_ref = bf16[16,24,256]{2,1,0:T(8,128)(2,1)S(1)} all-to-all(bf16[16,24,256]{2,1,0:T(8,128)(2,1)S(1)} %broadcast_in_dim.5), channel_id=1, replica_groups=mesh['shard'=16,'replica'=2] {'shard'}, dimensions={0} | all-to-all | bytes 393216 | tf_op jit(solution)/shard_map/all_to_all | solution.py:91
  36.3 0.0 copy-start
  36.3 0.0 collective-permute-start
  36.3 1.4 %collective-permute-done.other_ref = bf16[16,24,256]{2,1,0:T(8,128)(2,1)S(1)} collective-permute-done((bf16[16,24,256]{2,1,0:T(8,128)(2,1)S(1)}, bf16[16,24,256]{2,1,0:T(8,128)(2,1)S(1)}, u32[]{:S(2)}, u32[]{:S(2)}) %collective-permute-start) | collective-permute-done | bytes 196640 | tf_op jit(solution)/shard_map/ppermute | solution.py:122
  37.7 0.0 copy-start.1
  37.7 0.0 copy-done
  37.7 0.7 %copy-done.1 = bf16[16,24,256]{2,1,0:T(8,128)(2,1)} copy-done((bf16[16,24,256]{2,1,0:T(8,128)(2,1)}, bf16[16,24,256]{2,1,0:T(8,128)(2,1)S(1)}, u32[]{:S(2)}) %copy-start.1) | copy-done | bytes 196632
  38.4 2.0 %shard_map.85 = (f32[48,128]{1,0:T(8,128)}, bf16[24,8192]{1,0:T(8,128)(2,1)}) custom-call(s32[1,24]{1,0:T(1,128)} %bitcast.11, f32[48,128]{1,0:T(8,128)} %bitcast.10, bf16[16,24,256]{2,1,0:T(8,128)(2,1)} %copy-done, bf16[16,24,256]{2,1,0:T(8,128)(2,1)} %copy-done.1), custom_call_target="tpu_custom_call" | custom-call | tf_op jit(solution)/shard_map/pallas_call | solution.py:96
  (1 shorter events, 0.0 us)
Async XLA Ops:
  2.7 7.3 %copy-start.5 = (s32[24]{0:T(128)S(1)}, s32[24]{0:T(128)}, u32[]{:S(2)}) copy-start(s32[24]{0:T(128)} %param.9) | copy-start | bytes 292
  2.7 20.5 %all-to-all-start = ((bf16[32,48,128]{2,1,0:T(8,128)(2,1)}), bf16[32,48,128]{2,1,0:T(8,128)(2,1)S(1)}, u32[]{:S(2)}, u32[]{:S(2)}) async-start(bf16[32,48,128]{2,1,0:T(8,128)(2,1)} %shard_map.84), calls=%async_computation | async-start | bytes 786432 | tf_op jit(solution)/shard_map/all_to_all | solution.py:109
  10.2 13.1 %copy-start.2 = (f32[6144]{0:T(1024)S(1)}, f32[6144]{0:T(1024)}, u32[]{:S(2)}) copy-start(f32[6144]{0:T(1024)} %param.6) | copy-start | bytes 73732
  10.2 13.1 %copy-start.3 = (f32[6144]{0:T(1024)S(1)}, f32[6144]{0:T(1024)}, u32[]{:S(2)}) copy-start(f32[6144]{0:T(1024)} %param.7) | copy-start | bytes 73732
  10.2 13.1 %copy-start.4 = (f32[6144]{0:T(1024)S(1)}, f32[6144]{0:T(1024)}, u32[]{:S(2)}) copy-start(f32[6144]{0:T(1024)} %param.8) | copy-start | bytes 73732
  36.3 1.4 %copy-start = (bf16[16,24,256]{2,1,0:T(8,128)(2,1)}, bf16[16,24,256]{2,1,0:T(8,128)(2,1)S(1)}, u32[]{:S(2)}) copy-start(bf16[16,24,256]{2,1,0:T(8,128)(2,1)S(1)} %all_to_all.10.own_ref) | copy-start | bytes 589828
  36.3 1.4 %collective-permute-start = (bf16[16,24,256]{2,1,0:T(8,128)(2,1)S(1)}, bf16[16,24,256]{2,1,0:T(8,128)(2,1)S(1)}, u32[]{:S(2)}, u32[]{:S(2)}) collective-permute-start(bf16[16,24,256]{2,1,0:T(8,128)(2,1)S(1)} %all_to_all.10.own_ref), channel_id=1, source_target_pairs={{0,1},{1,0},{2,3},{3,2},{4,5},{5,4},{6,7},{7,6},{8,9},{9,8},{10,11... | collective-permute-start | bytes 589832 | tf_op jit(solution)/shard_map/ppermute | solution.py:122
  37.7 0.7 %copy-start.1 = (bf16[16,24,256]{2,1,0:T(8,128)(2,1)}, bf16[16,24,256]{2,1,0:T(8,128)(2,1)S(1)}, u32[]{:S(2)}) copy-start(bf16[16,24,256]{2,1,0:T(8,128)(2,1)S(1)} %collective-permute-done.other_ref) | copy-start | bytes 589828

commit v3 on v2

v3 whole, which is shorter than its diff:
```python
import jax
import jax.numpy as jnp
from jax import lax
from jax.experimental import pallas as pl
from jax.experimental.pallas import tpu as pltpu
from jax.sharding import PartitionSpec as P

D = 8192


learning_rate = 0.1
adam_epsilon = 1e-08
norm_epsilon = 1e-06
first_correction = 1.0 - 0.9**20
second_correction = 1.0 - 0.95**20
AXES = ("shard", "replica")
LANES = 128


def adam_step(gradient, master, first_moment, second_moment):
    new_first = 0.9 * first_moment + 0.1 * gradient
    new_second = 0.95 * second_moment + 0.05 * gradient * gradient
    stepped = master - learning_rate * (new_first / first_correction) / (
        jnp.sqrt(new_second / second_correction) + adam_epsilon
    )
    return (new_first, new_second, stepped)


def flat_positions(owners):
    column_ids = jnp.arange(owners.shape[0], dtype=jnp.int32)
    ranked_below = owners[None, :] < owners[:, None]
    same_before = (owners[None, :] == owners[:, None]) & (column_ids[None, :] < column_ids[:, None])
    return jnp.sum((ranked_below | same_before).astype(jnp.int32), axis=1)


def small(**more):
    return pltpu.CompilerParams(vmem_limit_bytes=6 * 2**20, **more)


def pack_kernel(grads_ref, out_ref, long_ref, wide_ref, packed_ref, in_sems, out_sems):
    parts, _, width = long_ref.shape
    devices, lines, lanes = out_ref.shape
    each = devices // parts
    row_ref = wide_ref.reshape(1, wide_ref.shape[0] * lanes)
    taken, given = [], []
    for p in range(parts):
        source = grads_ref.at[:, pl.ds(p * width, width)]
        taken.append(pltpu.make_async_copy(source, long_ref.at[p], in_sems.at[p]))
        place = pl.ds(p * each, each)
        given.append(pltpu.make_async_copy(packed_ref.at[place], out_ref.at[place], out_sems.at[p]))
        taken[p].start()
    for p in range(parts):
        taken[p].wait()
        row_ref[:, p * width : (p + 1) * width] = long_ref[p].astype(jnp.float32)
        for k in range(p * each, (p + 1) * each):
            packed_ref[k] = wide_ref[k * lines : (k + 1) * lines].astype(jnp.bfloat16)
        given[p].start()
    for copy in given:
        copy.wait()


def pack(grads, devices):
    lines = grads.shape[1] // devices // LANES
    if lines % 16:
        return grads.reshape(devices, lines, LANES)
    parts = 4
    packed = (devices, lines, LANES)
    return pl.pallas_call(
        pack_kernel,
        in_specs=[pl.BlockSpec(memory_space=pl.ANY)],
        out_specs=pl.BlockSpec(memory_space=pl.ANY),
        out_shape=jax.ShapeDtypeStruct(packed, jnp.bfloat16),
        scratch_shapes=[
            pltpu.VMEM((parts, 1, grads.shape[1] // parts), jnp.bfloat16),
            pltpu.VMEM((grads.shape[1] // LANES, LANES), jnp.float32),
            pltpu.VMEM(packed, jnp.bfloat16),
            pltpu.SemaphoreType.DMA((parts,)),
            pltpu.SemaphoreType.DMA((parts,)),
        ],
    )(grads)


def positions_column(owners_ref):
    columns = owners_ref.shape[1]
    square = (columns, columns)
    down = lax.broadcasted_iota(jnp.int32, square, 0)
    along = lax.broadcasted_iota(jnp.int32, square, 1)
    owner_row = jnp.broadcast_to(owners_ref[...].astype(jnp.float32), square)
    owner_column = jnp.sum(jnp.where(down == along, owner_row, 0.0), axis=1, keepdims=True)
    before = (owner_row < owner_column) | ((owner_row == owner_column) & (along < down))
    return jnp.sum(before.astype(jnp.float32), axis=1, keepdims=True).astype(jnp.int32)


def middle_kernel(
    owners_ref, pieces_ref, master_ref, first_ref, second_ref, gradient_ref, copies_ref, flat_ref
):
    devices = pieces_ref.shape[0]
    copies, columns, width = copies_ref.shape
    total = pieces_ref[0].astype(jnp.float32)
    for k in range(1, devices):
        total = total + pieces_ref[k].astype(jnp.float32)
    gradient = total / devices
    gradient_ref[...] = gradient
    flat_ref[...] = adam_step(gradient, master_ref[...], first_ref[...], second_ref[...])[2]
    period = columns // 8
    span = period * LANES
    group = span // columns
    lines = flat_ref.shape[0] // period
    wide = [flat_ref[pl.ds(b, lines, stride=period), :].astype(jnp.bfloat16) for b in range(period)]
    wide = jnp.concatenate(wide, axis=1)
    line = lax.broadcasted_iota(jnp.int32, (lines, width), 0)
    row = lax.broadcasted_iota(jnp.int32, (lines, width), 1)
    repeat = (row // group == line).astype(jnp.bfloat16)
    spread = lax.dot_general(wide, repeat, (((0,), (0,)), ((), ())), preferred_element_type=jnp.float32)
    entry = lax.broadcasted_iota(jnp.int32, (span, width), 0)
    row = lax.broadcasted_iota(jnp.int32, (span, width), 1)
    kept = jnp.where(entry // columns == row % group, spread, 0.0).astype(jnp.bfloat16)
    column = lax.broadcasted_iota(jnp.int32, (columns, span), 1) % columns
    pick = (column == positions_column(owners_ref)).astype(jnp.bfloat16)
    rows = jnp.dot(pick, kept, preferred_element_type=jnp.float32).astype(jnp.bfloat16)
    for k in range(copies):
        copies_ref[k] = rows


def middle(owners, pieces, master, first_moment, second_moment, copies):
    columns = owners.shape[0]
    flat = pieces.shape[1:]
    width = flat[0] * LANES // columns
    return pl.pallas_call(
        middle_kernel,
        out_shape=(
            jax.ShapeDtypeStruct(flat, jnp.float32),
            jax.ShapeDtypeStruct((copies, columns, width), jnp.bfloat16),
        ),
        scratch_shapes=[pltpu.VMEM(flat, jnp.float32)],
        compiler_params=small(),
    )(owners[None, :], pieces, *(x.reshape(flat) for x in (master, first_moment, second_moment)))


def squares_kernel(blocks_ref, total_ref):
    total = jnp.zeros(total_ref.shape, jnp.float32)
    for k in range(blocks_ref.shape[0]):
        value = blocks_ref[k].astype(jnp.float32)
        total = total + value * value
    total_ref[...] = total


def squares(blocks):
    return pl.pallas_call(
        squares_kernel,
        out_shape=jax.ShapeDtypeStruct(blocks.shape[1:], jnp.float32),
        compiler_params=small(),
        cost_estimate=pl.CostEstimate(
            flops=2 * blocks.size, bytes_accessed=2 * blocks.size, transcendentals=0
        ),
    )(blocks)


def finish_kernel(owners_ref, stepped_ref, part_ref, own_ref, other_ref, master_ref, copy_ref, scaled_ref, sems):
    core = lax.axis_index("replica")
    chips, columns, width = own_ref.shape
    total = part_ref[...]
    for k in range(chips):
        value = other_ref[k].astype(jnp.float32)
        total = total + value * value
    factor = lax.rsqrt(jnp.sum(total, axis=1, keepdims=True) / D + norm_epsilon)
    parts = sems.shape[0]
    each = chips // parts
    copies = []
    for p in range(parts):
        for k in range(p * each, (p + 1) * each):
            for ref, place in ((own_ref, core), (other_ref, 1 - core)):
                start = pl.multiple_of((2 * k + place) * width, width)
                scaled_ref[:, pl.ds(start, width)] = (ref[k].astype(jnp.float32) * factor).astype(jnp.bfloat16)
        part = pl.ds(p * 2 * each * width, 2 * each * width)
        copies.append(pltpu.make_async_copy(scaled_ref.at[:, part], copy_ref.at[:, part], sems.at[p]))
        copies[p].start()
    position = positions_column(owners_ref)
    period = columns // 8
    lane = lax.broadcasted_iota(jnp.int32, (1, LANES), 1)
    line = lax.broadcasted_iota(jnp.int32, stepped_ref.shape, 0) % period
    spread = jnp.zeros(stepped_ref.shape, jnp.float32)
    for p in range(period):
        flat_column = (p * LANES + lane) % columns
        picked = jnp.sum(jnp.where(position == flat_column, factor, 0.0), axis=0, keepdims=True)
        spread = jnp.where(line == p, picked, spread)
    master_ref[...] = stepped_ref[...] * spread
    for copy in copies:
        copy.wait()


def finish_narrow(owners, stepped, blocks):
    columns = owners.shape[0]
    blocks = blocks.astype(jnp.float32)
    factor = lax.rsqrt(jnp.sum(blocks * blocks, axis=(0, 2)) / D + norm_epsilon)
    scaled = jnp.transpose(blocks * factor[None, :, None], (1, 0, 2))
    flat_factor = jnp.zeros((columns,), jnp.float32).at[flat_positions(owners)].set(factor)
    new_master = (stepped.reshape(-1, columns) * flat_factor).reshape(stepped.shape)
    return (new_master, scaled.reshape(columns, -1).astype(jnp.bfloat16))


def spread(value, axes, size):
    return lax.all_to_all(jnp.broadcast_to(value[None], (size,) + value.shape), axes, 0, 0, tiled=True)


def finish(owners, stepped, part, own, other):
    chips, columns, width = own.shape
    wide = (columns, 2 * chips * width)
    parts = 4 if chips % 4 == 0 else 1
    whole = pl.BlockSpec(memory_space=pltpu.VMEM)
    return pl.pallas_call(
        finish_kernel,
        in_specs=[whole] * 5,
        out_specs=(whole, pl.BlockSpec(memory_space=pl.ANY)),
        out_shape=(
            jax.ShapeDtypeStruct(stepped.shape, jnp.float32),
            jax.ShapeDtypeStruct(wide, jnp.bfloat16),
        ),
        scratch_shapes=[pltpu.VMEM(wide, jnp.bfloat16), pltpu.SemaphoreType.DMA((parts,))],
        compiler_params=small(),
    )(owners[None, :], stepped, part, own, other)


def on_device(grads, master, first_moment, second_moment, owners):
    shards, replicas = lax.axis_size("shard"), lax.axis_size("replica")
    devices = shards * replicas
    columns = owners.shape[0]
    pieces = lax.all_to_all(pack(grads, devices), AXES, 0, 0, tiled=True)
    if replicas == 2 and master.shape[0] % (columns * LANES) == 0:
        gradient, copies = middle(owners, pieces, master, first_moment, second_moment, shards)
        new_first, new_second, stepped = adam_step(
            gradient.reshape(-1), master, first_moment, second_moment
        )
        own = lax.all_to_all(copies, "shard", 0, 0, tiled=True)
        other = lax.ppermute(own, "replica", [(0, 1), (1, 0)])
        new_master, model_copy = finish(owners, stepped.reshape(-1, LANES), squares(own), own, other)
        return (new_master.reshape(-1), new_first, new_second, model_copy)
    gradient = jnp.sum(pieces.astype(jnp.float32), axis=0).reshape(-1) / devices
    new_first, new_second, stepped = adam_step(gradient, master, first_moment, second_moment)
    rows = jnp.take(stepped.reshape(-1, columns), flat_positions(owners), axis=1).T.astype(jnp.bfloat16)
    new_master, model_copy = finish_narrow(owners, stepped, spread(rows, AXES, devices))
    return (new_master, new_first, new_second, model_copy)


def solution(mesh):
    placed = (P(AXES, None), P(AXES), P(AXES), P(AXES), P())
    return jax.shard_map(
        on_device,
        mesh=mesh,
        in_specs=placed,
        out_specs=(P(AXES), P(AXES), P(AXES), P()),
        check_vma=False,
    )
```

time: 40.6 us -> 39.6 us (0.975)
  blocking collectives: 12.1 us -> 32.5 us
  waiting for transfers between devices: 14.4 us -> 0.8 us
  starting transfers between devices: 7.3 us -> 0.01 us
    all_to_all x1 -> x2, blocking collectives: 12.1 us -> 32.5 us  [the longest x1 20.5 us: on_device(): pieces = lax.all_to_all(pack(grads, devices), AXES, 0, 0, tiled=True)]
    all_to_all x1 -> x0, waiting for transfers between devices: 13 us -> none  [on_device(): pieces = lax.all_to_all(pack(grads, devices), AXES, 0, 0, tiled=True)]
    all_to_all x1 -> x0, starting transfers between devices: 7.3 us -> none  [on_device(): pieces = lax.all_to_all(pack(grads, devices), AXES, 0, 0, tiled=True)]
    ppermute x1, waiting for transfers between devices: 1.44 us -> 0.8 us  [on_device(): other = lax.ppermute(own, 'replica', [(0, 1), (1, 0)])]
    convert_element_type x1 -> x0, other arithmetic: 0.63 us -> none  [on_device(): matrix.astype(jnp.bfloat16)]
    reshape x0 -> x1, other arithmetic: none -> 0.63 us  [on_device(): stepped.reshape(-1, LANES)]
    pallas_call x2 -> x4, Pallas kernels: 4.01 us -> 3.96 us  [the longest x1 1.97 us: pack(): pl.pallas_call(pack_kernel, in_specs=[pl.BlockSpec(memory_space=pl.ANY)],...]
  transfers between devices with their start and end apart: 2 -> 1, of which waited for: 2 -> 1; matrix products, arithmetic and copies ran while one was open for 0% -> 2% of each run, Pallas kernels for 0% -> 0%
where the time goes in v3:
time: 39.6 us; the launch traced here: 39.3 us
  blocking collectives  32.5 us (82%)
  Pallas kernels  3.96 us (10%)
  waiting for transfers between devices  0.8 us (2%)
  between operations  0.68 us (2%)
  local copies, waits for them, and re-layouts  0.66 us (2%)
  other arithmetic  0.63 us (2%)
    all_to_all x1, blocking collectives, on_device(): pieces = lax.all_to_all(pack(grads, devices), AXES, 0, 0, tiled=True)  20.5 us
    all_to_all x1, blocking collectives, on_device(): own = lax.all_to_all(copies, 'shard', 0, 0, tiled=True)  12.1 us
    pallas_call x1, Pallas kernels, pack(): pl.pallas_call(pack_kernel, in_specs=[pl.BlockSpec(memory_space=pl.ANY)],...  1.97 us
    pallas_call x1, Pallas kernels, finish(): pl.pallas_call(finish_kernel, in_specs=[whole] * 5, out_specs=(whole, pl....  1.52 us
    ppermute x1, waiting for transfers between devices, on_device(): other = lax.ppermute(own, 'replica', [(0, 1), (1, 0)])  0.8 us
  transfers between devices with their start and end apart: 1, of which 1 were waited for; matrix products, arithmetic and copies ran while one was open for 2% of the time, Pallas kernels for 0%

profile of v3, /device:TPU:0, one launch (start us, length us, event | category | flops | bytes accessed | tf_op | source)
XLA Modules:
  0.0 39.3 jit_solution(16152474828475309183)
XLA Ops:
  0.6 2.0 %shard_map.84 = bf16[32,48,128]{2,1,0:T(8,128)(2,1)} custom-call(bf16[1,196608]{1,0:T(2,128)(2,1)} %grads_ref.1), custom_call_target="tpu_custom_call" | custom-call | tf_op jit(solution)/shard_map/pallas_call | solution.py:68
  2.6 0.0 copy-start
  2.6 0.0 copy-start.1
  2.6 0.0 copy-start.2
  2.6 20.5 %all_to_all.10.pieces_ref = bf16[32,48,128]{2,1,0:T(8,128)(2,1)S(1)} all-to-all(bf16[32,48,128]{2,1,0:T(8,128)(2,1)} %shard_map.84), channel_id=1, replica_groups=mesh['shard'=16,'replica'=2] {'shard','replica'}, dimensions={0} | all-to-all | bytes 786432 | tf_op jit(solution)/shard_map/all_to_all | solution.py:228
  23.1 0.0 copy-start.3
  23.1 0.0 copy-done
  23.1 0.0 copy-done.1
  23.1 0.0 copy-done.2
  23.1 0.6 %copy-done.3 = s32[24]{0:T(128)S(1)} copy-done((s32[24]{0:T(128)S(1)}, s32[24]{0:T(128)}, u32[]{:S(2)}) %copy-start.3) | copy-done | bytes 120
  23.8 0.5 %shard_map.85 = (f32[48,128]{1,0:T(8,128)S(1)}, bf16[16,24,256]{2,1,0:T(8,128)(2,1)S(1)}) custom-call(s32[1,24]{1,0:T(1,128)S(1)} %bitcast.17, bf16[32,48,128]{2,1,0:T(8,128)(2,1)S(1)} %all_to_all.10.pieces_ref, f32[48,128]{1,0:T(8,128)S(1)} %bitcast.14, f32[48,128]{1,0:T(8,128)S(1)} %bitcast.15, f32[48,128]{1,0:T(8,128)S(1)} %bitcast.16), custom_call_target="tpu_custom_call" | custom-call | tf_op jit(solution)/shard_map/pallas_call | solution.py:129
  24.3 12.1 %all_to_all.11.blocks_ref.own_ref = bf16[16,24,256]{2,1,0:T(8,128)(2,1)S(1)} all-to-all(bf16[16,24,256]{2,1,0:T(8,128)(2,1)S(1)} %get-tuple-element.9), channel_id=1, replica_groups=mesh['shard'=16,'replica'=2] {'shard'}, dimensions={0} | all-to-all | bytes 393216 | tf_op jit(solution)/shard_map/all_to_all | solution.py:234
  36.3 0.0 collective-permute-start
  36.3 0.6 %subtract_bitcast_fusion = (f32[48,128]{1,0:T(8,128)S(1)}, f32[6144]{0:T(1024)}, f32[6144]{0:T(1024)}) fusion(f32[6144]{0:T(1024)S(1)} %copy-done, f32[48,128]{1,0:T(8,128)S(1)} %get-tuple-element.8, f32[6144]{0:T(1024)S(1)} %copy-done.1, f32[6144]{0:T(1024)S(1)} %copy-done.2), kind=kLoop, calls=%fused_computation.4 | loop fusion | flops 73728 | bytes 172032 | tf_op jit(solution)/shard_map/reshape | solution.py:236
  37.0 0.8 %collective-permute-done.other_ref = bf16[16,24,256]{2,1,0:T(8,128)(2,1)S(1)} collective-permute-done((bf16[16,24,256]{2,1,0:T(8,128)(2,1)S(1)}, bf16[16,24,256]{2,1,0:T(8,128)(2,1)S(1)}, u32[]{:S(2)}, u32[]{:S(2)}) %collective-permute-start) | collective-permute-done | bytes 196640 | tf_op jit(solution)/shard_map/ppermute | solution.py:235
  37.8 1.5 %shard_map.87 = (f32[48,128]{1,0:T(8,128)}, bf16[24,8192]{1,0:T(8,128)(2,1)}) custom-call(s32[1,24]{1,0:T(1,128)S(1)} %bitcast.18, f32[48,128]{1,0:T(8,128)S(1)} %get-tuple-element.12.stepped_ref, f32[24,256]{1,0:T(8,128)S(1)} %shard_map.86.part_ref, bf16[16,24,256]{2,1,0:T(8,128)(2,1)S(1)} %all_to_all.11.blocks_ref.own_ref, ...), custom_call_target="tpu_custom_call" | custom-call | tf_op jit(solution)/shard_map/pallas_call | solution.py:211
  (1 shorter events, 0.0 us)
Async XLA Ops:
  2.6 20.5 %copy-start = (f32[6144]{0:T(1024)S(1)}, f32[6144]{0:T(1024)}, u32[]{:S(2)}) copy-start(f32[6144]{0:T(1024)} %param.6) | copy-start | bytes 73732
  2.6 20.5 %copy-start.1 = (f32[6144]{0:T(1024)S(1)}, f32[6144]{0:T(1024)}, u32[]{:S(2)}) copy-start(f32[6144]{0:T(1024)} %param.7) | copy-start | bytes 73732
  2.6 20.5 %copy-start.2 = (f32[6144]{0:T(1024)S(1)}, f32[6144]{0:T(1024)}, u32[]{:S(2)}) copy-start(f32[6144]{0:T(1024)} %param.8) | copy-start | bytes 73732
  23.1 0.7 %copy-start.3 = (s32[24]{0:T(128)S(1)}, s32[24]{0:T(128)}, u32[]{:S(2)}) copy-start(s32[24]{0:T(128)} %param.9) | copy-start | bytes 292
  36.3 1.4 %collective-permute-start = (bf16[16,24,256]{2,1,0:T(8,128)(2,1)S(1)}, bf16[16,24,256]{2,1,0:T(8,128)(2,1)S(1)}, u32[]{:S(2)}, u32[]{:S(2)}) collective-permute-start(bf16[16,24,256]{2,1,0:T(8,128)(2,1)S(1)} %all_to_all.11.blocks_ref.own_ref), channel_id=1, source_target_pairs={{0,1},{1,0},{2,3},{3,2},{4,5},{5,4},{6,7},{7,6},{8,9},{9,8},{10,11... | collective-permute-start | bytes 589832 | tf_op jit(solution)/shard_map/ppermute | solution.py:235

commit v4 on v3

--- a/solution.py
+++ b/solution.py
@@ -37,62 +37,37 @@
     return pltpu.CompilerParams(vmem_limit_bytes=6 * 2**20, **more)
 
 
-def pack_kernel(grads_ref, out_ref, long_ref, wide_ref, packed_ref, in_sems, out_sems):
-    parts, _, width = long_ref.shape
+def pack_kernel(grads_ref, out_ref, wide_ref):
     devices, lines, lanes = out_ref.shape
-    each = devices // parts
     row_ref = wide_ref.reshape(1, wide_ref.shape[0] * lanes)
-    taken, given = [], []
-    for p in range(parts):
-        source = grads_ref.at[:, pl.ds(p * width, width)]
-        taken.append(pltpu.make_async_copy(source, long_ref.at[p], in_sems.at[p]))
-        place = pl.ds(p * each, each)
-        given.append(pltpu.make_async_copy(packed_ref.at[place], out_ref.at[place], out_sems.at[p]))
-        taken[p].start()
-    for p in range(parts):
-        taken[p].wait()
-        row_ref[:, p * width : (p + 1) * width] = long_ref[p].astype(jnp.float32)
-        for k in range(p * each, (p + 1) * each):
-            packed_ref[k] = wide_ref[k * lines : (k + 1) * lines].astype(jnp.bfloat16)
-        given[p].start()
-    for copy in given:
-        copy.wait()
+    width = lines * lanes
+    for k in range(devices):
+        row_ref[:, k * width : (k + 1) * width] = grads_ref[:, k * width : (k + 1) * width].astype(jnp.float32)
+        out_ref[k] = wide_ref[k * lines : (k + 1) * lines].astype(jnp.bfloat16)
 
 
 def pack(grads, devices):
     lines = grads.shape[1] // devices // LANES
     if lines % 16:
         return grads.reshape(devices, lines, LANES)
-    parts = 4
-    packed = (devices, lines, LANES)
     return pl.pallas_call(
         pack_kernel,
-        in_specs=[pl.BlockSpec(memory_space=pl.ANY)],
-        out_specs=pl.BlockSpec(memory_space=pl.ANY),
-        out_shape=jax.ShapeDtypeStruct(packed, jnp.bfloat16),
-        scratch_shapes=[
-            pltpu.VMEM((parts, 1, grads.shape[1] // parts), jnp.bfloat16),
-            pltpu.VMEM((grads.shape[1] // LANES, LANES), jnp.float32),
-            pltpu.VMEM(packed, jnp.bfloat16),
-            pltpu.SemaphoreType.DMA((parts,)),
-            pltpu.SemaphoreType.DMA((parts,)),
-        ],
+        out_shape=jax.ShapeDtypeStruct((devices, lines, LANES), jnp.bfloat16),
+        scratch_shapes=[pltpu.VMEM((grads.shape[1] // LANES, LANES), jnp.float32)],
+        compiler_params=small(),
     )(grads)
 
 
-def positions_column(owners_ref):
-    columns = owners_ref.shape[1]
+def down_column(row_ref):
+    columns = row_ref.shape[1]
     square = (columns, columns)
-    down = lax.broadcasted_iota(jnp.int32, square, 0)
-    along = lax.broadcasted_iota(jnp.int32, square, 1)
-    owner_row = jnp.broadcast_to(owners_ref[...].astype(jnp.float32), square)
-    owner_column = jnp.sum(jnp.where(down == along, owner_row, 0.0), axis=1, keepdims=True)
-    before = (owner_row < owner_column) | ((owner_row == owner_column) & (along < down))
-    return jnp.sum(before.astype(jnp.float32), axis=1, keepdims=True).astype(jnp.int32)
+    same = lax.broadcasted_iota(jnp.int32, square, 0) == lax.broadcasted_iota(jnp.int32, square, 1)
+    row = jnp.broadcast_to(row_ref[...].astype(jnp.float32), square)
+    return jnp.sum(jnp.where(same, row, 0.0), axis=1, keepdims=True).astype(jnp.int32)
 
 
 def middle_kernel(
-    owners_ref, pieces_ref, master_ref, first_ref, second_ref, gradient_ref, copies_ref, flat_ref
+    position_ref, pieces_ref, master_ref, first_ref, second_ref, gradient_ref, copies_ref, flat_ref
 ):
     devices = pieces_ref.shape[0]
     copies, columns, width = copies_ref.shape
@@ -116,14 +91,14 @@
     row = lax.broadcasted_iota(jnp.int32, (span, width), 1)
     kept = jnp.where(entry // columns == row % group, spread, 0.0).astype(jnp.bfloat16)
     column = lax.broadcasted_iota(jnp.int32, (columns, span), 1) % columns
-    pick = (column == positions_column(owners_ref)).astype(jnp.bfloat16)
+    pick = (column == down_column(position_ref)).astype(jnp.bfloat16)
     rows = jnp.dot(pick, kept, preferred_element_type=jnp.float32).astype(jnp.bfloat16)
     for k in range(copies):
         copies_ref[k] = rows
 
 
-def middle(owners, pieces, master, first_moment, second_moment, copies):
-    columns = owners.shape[0]
+def middle(position, pieces, master, first_moment, second_moment, copies):
+    columns = position.shape[0]
     flat = pieces.shape[1:]
     width = flat[0] * LANES // columns
     return pl.pallas_call(
@@ -134,35 +109,17 @@
         ),
         scratch_shapes=[pltpu.VMEM(flat, jnp.float32)],
         compiler_params=small(),
-    )(owners[None, :], pieces, *(x.reshape(flat) for x in (master, first_moment, second_moment)))
-
-
-def squares_kernel(blocks_ref, total_ref):
-    total = jnp.zeros(total_ref.shape, jnp.float32)
-    for k in range(blocks_ref.shape[0]):
-        value = blocks_ref[k].astype(jnp.float32)
-        total = total + value * value
-    total_ref[...] = total
-
-
-def squares(blocks):
-    return pl.pallas_call(
-        squares_kernel,
-        out_shape=jax.ShapeDtypeStruct(blocks.shape[1:], jnp.float32),
-        compiler_params=small(),
-        cost_estimate=pl.CostEstimate(
-            flops=2 * blocks.size, bytes_accessed=2 * blocks.size, transcendentals=0
-        ),
-    )(blocks)
-
-
-def finish_kernel(owners_ref, stepped_ref, part_ref, own_ref, other_ref, master_ref, copy_ref, scaled_ref, sems):
+    )(position[None, :], pieces, *(x.reshape(flat) for x in (master, first_moment, second_moment)))
+
+
+def finish_kernel(position_ref, stepped_ref, own_ref, other_ref, master_ref, copy_ref, scaled_ref, sems):
     core = lax.axis_index("replica")
     chips, columns, width = own_ref.shape
-    total = part_ref[...]
-    for k in range(chips):
-        value = other_ref[k].astype(jnp.float32)
-        total = total + value * value
+    total = jnp.zeros((columns, width), jnp.float32)
+    for ref in (own_ref, other_ref):
+        for k in range(chips):
+            value = ref[k].astype(jnp.float32)
+            total = total + value * value
     factor = lax.rsqrt(jnp.sum(total, axis=1, keepdims=True) / D + norm_epsilon)
     parts = sems.shape[0]
     each = chips // parts
@@ -175,7 +132,7 @@
         part = pl.ds(p * 2 * each * width, 2 * each * width)
         copies.append(pltpu.make_async_copy(scaled_ref.at[:, part], copy_ref.at[:, part], sems.at[p]))
         copies[p].start()
-    position = positions_column(owners_ref)
+    position = down_column(position_ref)
     period = columns // 8
     lane = lax.broadcasted_iota(jnp.int32, (1, LANES), 1)
     line = lax.broadcasted_iota(jnp.int32, stepped_ref.shape, 0) % period
@@ -203,14 +160,14 @@
     return lax.all_to_all(jnp.broadcast_to(value[None], (size,) + value.shape), axes, 0, 0, tiled=True)
 
 
-def finish(owners, stepped, part, own, other):
+def finish(position, stepped, own, other):
     chips, columns, width = own.shape
     wide = (columns, 2 * chips * width)
     parts = 4 if chips % 4 == 0 else 1
     whole = pl.BlockSpec(memory_space=pltpu.VMEM)
     return pl.pallas_call(
         finish_kernel,
-        in_specs=[whole] * 5,
+        in_specs=[whole] * 4,
         out_specs=(whole, pl.BlockSpec(memory_space=pl.ANY)),
         out_shape=(
             jax.ShapeDtypeStruct(stepped.shape, jnp.float32),
@@ -218,7 +175,7 @@
         ),
         scratch_shapes=[pltpu.VMEM(wide, jnp.bfloat16), pltpu.SemaphoreType.DMA((parts,))],
         compiler_params=small(),
-    )(owners[None, :], stepped, part, own, other)
+    )(position[None, :], stepped, own, other)
 
 
 def on_device(grads, master, first_moment, second_moment, owners):
@@ -227,13 +184,14 @@
     columns = owners.shape[0]
     pieces = lax.all_to_all(pack(grads, devices), AXES, 0, 0, tiled=True)
     if replicas == 2 and master.shape[0] % (columns * LANES) == 0:
-        gradient, copies = middle(owners, pieces, master, first_moment, second_moment, shards)
+        position = flat_positions(owners)
+        gradient, copies = middle(position, pieces, master, first_moment, second_moment, shards)
         new_first, new_second, stepped = adam_step(
             gradient.reshape(-1), master, first_moment, second_moment
         )
         own = lax.all_to_all(copies, "shard", 0, 0, tiled=True)
         other = lax.ppermute(own, "replica", [(0, 1), (1, 0)])
-        new_master, model_copy = finish(owners, stepped.reshape(-1, LANES), squares(own), own, other)
+        new_master, model_copy = finish(position, stepped.reshape(-1, LANES), own, other)
         return (new_master.reshape(-1), new_first, new_second, model_copy)
     gradient = jnp.sum(pieces.astype(jnp.float32), axis=0).reshape(-1) / devices
     new_first, new_second, stepped = adam_step(gradient, master, first_moment, second_moment)

time: 39.6 us -> 39 us (0.985)
  blocking collectives: 32.5 us -> 12.1 us
  waiting for transfers between devices: 0.8 us -> 13.8 us
  starting transfers between devices: 0.01 us -> 7.31 us
  Pallas kernels: 3.96 us -> 2.86 us
  local copies, waits for them, and re-layouts: 0.66 us -> 1.14 us
    all_to_all x1 -> x0, blocking collectives: 20.5 us -> none  [on_device(): pieces = lax.all_to_all(pack(grads, devices), AXES, 0, 0, tiled=True)]
    all_to_all x0 -> x1, waiting for transfers between devices: none -> 13 us  [on_device(): pieces = lax.all_to_all(pack(grads, devices), AXES, 0, 0, tiled=True)]
    all_to_all x0 -> x1, starting transfers between devices: none -> 7.3 us  [on_device(): pieces = lax.all_to_all(pack(grads, devices), AXES, 0, 0, tiled=True)]
    pallas_call x3 -> x2, Pallas kernels: 3.5 us -> 2.39 us  [the longest x1 1.5 us: finish(): pl.pallas_call(finish_kernel, in_specs=[whole] * 4, out_specs=(whole, pl....]
    unnamed x8 -> x10, local copies, waits for them, and re-layouts: 0.66 us -> 1.14 us
  transfers between devices with their start and end apart: 1 -> 2, of which waited for: 1 -> 2; matrix products, arithmetic and copies ran while one was open for 2% -> 2% of each run, Pallas kernels for 0% -> 0%
where the time goes in v4:
time: 39 us; the launch traced here: 38.6 us
  waiting for transfers between devices  13.8 us (35%)
  blocking collectives  12.1 us (31%)
  starting transfers between devices  7.31 us (19%)
  Pallas kernels  2.86 us (7%)
  local copies, waits for them, and re-layouts  1.14 us (3%)
  other arithmetic  0.81 us (2%)
  between operations  0.67 us (2%)
    all_to_all x1, waiting for transfers between devices, on_device(): pieces = lax.all_to_all(pack(grads, devices), AXES, 0, 0, tiled=True)  13 us
    all_to_all x1, blocking collectives, on_device(): own = lax.all_to_all(copies, 'shard', 0, 0, tiled=True)  12.1 us
    all_to_all x1, starting transfers between devices, on_device(): pieces = lax.all_to_all(pack(grads, devices), AXES, 0, 0, tiled=True)  7.3 us
    pallas_call x1, Pallas kernels, finish(): pl.pallas_call(finish_kernel, in_specs=[whole] * 4, out_specs=(whole, pl....  1.5 us
    unnamed x10, local copies, waits for them, and re-layouts  1.14 us
    pallas_call x1, Pallas kernels, pack(): pl.pallas_call(pack_kernel, out_shape=jax.ShapeDtypeStruct((devices, line...  0.89 us
    ppermute x1, waiting for transfers between devices, on_device(): other = lax.ppermute(own, 'replica', [(0, 1), (1, 0)])  0.81 us
  transfers between devices with their start and end apart: 2, of which 2 were waited for; matrix products, arithmetic and copies ran while one was open for 2% of the time, Pallas kernels for 0%

profile of v4, /device:TPU:0, one launch (start us, length us, event | category | flops | bytes accessed | tf_op | source)
XLA Modules:
  0.0 38.6 jit_solution(7764977086047894249)
XLA Ops:
  0.6 0.0 copy-start
  0.6 1.1 %copy-done = bf16[1,196608]{1,0:T(2,128)(2,1)S(1)} copy-done((bf16[1,196608]{1,0:T(2,128)(2,1)S(1)}, bf16[1,196608]{1,0:T(2,128)(2,1)}, u32[]{:S(2)}) %copy-start) | copy-done | bytes 393240
  1.8 0.9 %shard_map.84 = bf16[32,48,128]{2,1,0:T(8,128)(2,1)} custom-call(bf16[1,196608]{1,0:T(2,128)(2,1)S(1)} %copy-done), custom_call_target="tpu_custom_call" | custom-call | tf_op jit(solution)/shard_map/pallas_call | solution.py:53
  2.7 0.0 copy-start.4
  2.7 0.0 copy-start.1
  2.7 0.0 copy-start.2
  2.7 0.0 copy-start.3
  2.7 7.3 %all-to-all-start = ((bf16[32,48,128]{2,1,0:T(8,128)(2,1)}), bf16[32,48,128]{2,1,0:T(8,128)(2,1)S(1)}, u32[]{:S(2)}, u32[]{:S(2)}) async-start(bf16[32,48,128]{2,1,0:T(8,128)(2,1)} %shard_map.84), calls=%async_computation | async-start | bytes 786432 | tf_op jit(solution)/shard_map/all_to_all | solution.py:185
  10.0 0.0 copy-done.4
  10.0 0.2 convert_reduce_fusion
  10.2 13.0 %all-to-all-done.pieces_ref = bf16[32,48,128]{2,1,0:T(8,128)(2,1)S(1)} async-done(((bf16[32,48,128]{2,1,0:T(8,128)(2,1)}), bf16[32,48,128]{2,1,0:T(8,128)(2,1)S(1)}, u32[]{:S(2)}, u32[]{:S(2)}) %all-to-all-start) | async-done | bytes 393248 | tf_op jit(solution)/shard_map/all_to_all | solution.py:185
  23.2 0.0 copy-done.1
  23.2 0.0 copy-done.2
  23.2 0.0 copy-done.3
  23.2 0.5 %shard_map.85 = (f32[48,128]{1,0:T(8,128)S(1)}, bf16[16,24,256]{2,1,0:T(8,128)(2,1)S(1)}) custom-call(s32[1,24]{1,0:T(1,128)S(1)} %bitcast.17, bf16[32,48,128]{2,1,0:T(8,128)(2,1)S(1)} %all-to-all-done.pieces_ref, f32[48,128]{1,0:T(8,128)S(1)} %bitcast.14, f32[48,128]{1,0:T(8,128)S(1)} %bitcast.15, f32[48,128]{1,0:T(8,128)S(1)} %bitcast.16), custom_call_target="tpu_custom_call" | custom-call | tf_op jit(solution)/shard_map/pallas_call | solution.py:104
  23.6 12.1 %all_to_all.10.own_ref = bf16[16,24,256]{2,1,0:T(8,128)(2,1)S(1)} all-to-all(bf16[16,24,256]{2,1,0:T(8,128)(2,1)S(1)} %get-tuple-element.9), channel_id=1, replica_groups=mesh['shard'=16,'replica'=2] {'shard'}, dimensions={0} | all-to-all | bytes 393216 | tf_op jit(solution)/shard_map/all_to_all | solution.py:192
  35.7 0.0 collective-permute-start
  35.7 0.6 %subtract_bitcast_fusion = (f32[48,128]{1,0:T(8,128)S(1)}, f32[6144]{0:T(1024)}, f32[6144]{0:T(1024)}) fusion(f32[6144]{0:T(1024)S(1)} %copy-done.1, f32[48,128]{1,0:T(8,128)S(1)} %get-tuple-element.8, f32[6144]{0:T(1024)S(1)} %copy-done.2, f32[6144]{0:T(1024)S(1)} %copy-done.3), kind=kLoop, calls=%fused_computation.4 | loop fusion | flops 73728 | bytes 172032 | tf_op jit(solution)/shard_map/reshape | solution.py:194
  36.3 0.8 %collective-permute-done.other_ref = bf16[16,24,256]{2,1,0:T(8,128)(2,1)S(1)} collective-permute-done((bf16[16,24,256]{2,1,0:T(8,128)(2,1)S(1)}, bf16[16,24,256]{2,1,0:T(8,128)(2,1)S(1)}, u32[]{:S(2)}, u32[]{:S(2)}) %collective-permute-start) | collective-permute-done | bytes 196640 | tf_op jit(solution)/shard_map/ppermute | solution.py:193
  37.1 1.5 %shard_map.86 = (f32[48,128]{1,0:T(8,128)}, bf16[24,8192]{1,0:T(8,128)(2,1)}) custom-call(s32[1,24]{1,0:T(1,128)S(1)} %bitcast.18, f32[48,128]{1,0:T(8,128)S(1)} %get-tuple-element.12.stepped_ref, bf16[16,24,256]{2,1,0:T(8,128)(2,1)S(1)} %all_to_all.10.own_ref, bf16[16,24,256]{2,1,0:T(8,128)(2,1)S(1)} %collective-permute-done.other_ref), custom_call_target="tpu_custom_call" | custom-call | tf_op jit(solution)/shard_map/pallas_call | solution.py:168
Async XLA Ops:
  0.6 1.1 %copy-start = (bf16[1,196608]{1,0:T(2,128)(2,1)S(1)}, bf16[1,196608]{1,0:T(2,128)(2,1)}, u32[]{:S(2)}) copy-start(bf16[1,196608]{1,0:T(2,128)(2,1)} %grads_ref.1) | copy-start | bytes 1179652
  2.7 7.3 %copy-start.4 = (s32[24]{0:T(128)S(1)}, s32[24]{0:T(128)}, u32[]{:S(2)}) copy-start(s32[24]{0:T(128)} %param.9) | copy-start | bytes 292
  2.7 20.5 %copy-start.1 = (f32[6144]{0:T(1024)S(1)}, f32[6144]{0:T(1024)}, u32[]{:S(2)}) copy-start(f32[6144]{0:T(1024)} %param.6) | copy-start | bytes 73732
  2.7 20.5 %copy-start.2 = (f32[6144]{0:T(1024)S(1)}, f32[6144]{0:T(1024)}, u32[]{:S(2)}) copy-start(f32[6144]{0:T(1024)} %param.7) | copy-start | bytes 73732
  2.7 20.5 %copy-start.3 = (f32[6144]{0:T(1024)S(1)}, f32[6144]{0:T(1024)}, u32[]{:S(2)}) copy-start(f32[6144]{0:T(1024)} %param.8) | copy-start | bytes 73732
  2.7 20.5 %all-to-all-start = ((bf16[32,48,128]{2,1,0:T(8,128)(2,1)}), bf16[32,48,128]{2,1,0:T(8,128)(2,1)S(1)}, u32[]{:S(2)}, u32[]{:S(2)}) async-start(bf16[32,48,128]{2,1,0:T(8,128)(2,1)} %shard_map.84), calls=%async_computation | async-start | bytes 786432 | tf_op jit(solution)/shard_map/all_to_all | solution.py:185
  35.7 1.4 %collective-permute-start = (bf16[16,24,256]{2,1,0:T(8,128)(2,1)S(1)}, bf16[16,24,256]{2,1,0:T(8,128)(2,1)S(1)}, u32[]{:S(2)}, u32[]{:S(2)}) collective-permute-start(bf16[16,24,256]{2,1,0:T(8,128)(2,1)S(1)} %all_to_all.10.own_ref), channel_id=1, source_target_pairs={{0,1},{1,0},{2,3},{3,2},{4,5},{5,4},{6,7},{7,6},{8,9},{9,8},{10,11... | collective-permute-start | bytes 589832 | tf_op jit(solution)/shard_map/ppermute | solution.py:193

commit v5 on v4

v5 whole, which is shorter than its diff:
```python
import functools

import jax
import jax.numpy as jnp
from jax import lax
from jax.experimental import pallas as pl
from jax.experimental.pallas import tpu as pltpu
from jax.sharding import PartitionSpec as P

D = 8192


learning_rate = 0.1
adam_epsilon = 1e-08
norm_epsilon = 1e-06
first_correction = 1.0 - 0.9**20
second_correction = 1.0 - 0.95**20
AXES = ("shard", "replica")
LANES = 128


def adam_step(gradient, master, first_moment, second_moment):
    new_first = 0.9 * first_moment + 0.1 * gradient
    new_second = 0.95 * second_moment + 0.05 * gradient * gradient
    stepped = master - learning_rate * (new_first / first_correction) / (
        jnp.sqrt(new_second / second_correction) + adam_epsilon
    )
    return (new_first, new_second, stepped)


def flat_positions(owners):
    column_ids = jnp.arange(owners.shape[0], dtype=jnp.int32)
    ranked_below = owners[None, :] < owners[:, None]
    same_before = (owners[None, :] == owners[:, None]) & (column_ids[None, :] < column_ids[:, None])
    return jnp.sum((ranked_below | same_before).astype(jnp.int32), axis=1)


def small(**more):
    return pltpu.CompilerParams(vmem_limit_bytes=6 * 2**20, **more)


def pack_kernel(grads_ref, kept_ref, sent_ref, wide_ref):
    chips, lines, lanes = kept_ref.shape
    core = lax.axis_index("replica")
    row_ref = wide_ref.reshape(1, wide_ref.shape[0] * lanes)
    width = 2 * lines * lanes
    for k in range(chips):
        row_ref[:, k * width : (k + 1) * width] = grads_ref[:, k * width : (k + 1) * width].astype(jnp.float32)
        for ref, place in ((kept_ref, core), (sent_ref, 1 - core)):
            start = pl.multiple_of((2 * k + place) * lines, lines)
            ref[k] = wide_ref[pl.ds(start, lines), :].astype(jnp.bfloat16)


def pack(grads, chips, lines):
    packed = jax.ShapeDtypeStruct((chips, lines, LANES), jnp.bfloat16)
    return pl.pallas_call(
        pack_kernel,
        out_shape=(packed, packed),
        scratch_shapes=[pltpu.VMEM((grads.shape[1] // LANES, LANES), jnp.float32)],
        compiler_params=small(),
    )(grads)


def pair_kernel(kept_ref, taken_ref, *refs):
    *held, pairs_ref = refs
    pairs = kept_ref[...].astype(jnp.float32) + taken_ref[...].astype(jnp.float32)
    pairs_ref[...] = pairs.astype(jnp.bfloat16)
    for source, target in zip(held[:4], held[4:]):
        target[...] = source[...]


def add_pairs(kept, taken, position, states):
    flat = jax.ShapeDtypeStruct(kept.shape[1:], jnp.float32)
    position = position[None, :]
    small_shapes = (jax.ShapeDtypeStruct(position.shape, position.dtype), flat, flat, flat)
    return pl.pallas_call(
        pair_kernel,
        out_shape=(*small_shapes, jax.ShapeDtypeStruct(kept.shape, jnp.bfloat16)),
        compiler_params=small(),
    )(kept, taken, position, *(x.reshape(flat.shape) for x in states))


def down_column(row_ref):
    columns = row_ref.shape[1]
    square = (columns, columns)
    same = lax.broadcasted_iota(jnp.int32, square, 0) == lax.broadcasted_iota(jnp.int32, square, 1)
    row = jnp.broadcast_to(row_ref[...].astype(jnp.float32), square)
    return jnp.sum(jnp.where(same, row, 0.0), axis=1, keepdims=True).astype(jnp.int32)


def middle_kernel(
    devices, position_ref, pieces_ref, master_ref, first_ref, second_ref,
    new_first_ref, new_second_ref, stepped_ref, copies_ref,
):
    copies, columns, width = copies_ref.shape
    total = pieces_ref[0].astype(jnp.float32)
    for k in range(1, pieces_ref.shape[0]):
        total = total + pieces_ref[k].astype(jnp.float32)
    gradient = total / devices
    new_first_ref[...], new_second_ref[...], stepped_ref[...] = adam_step(
        gradient, master_ref[...], first_ref[...], second_ref[...]
    )
    period = columns // 8
    span = period * LANES
    group = span // columns
    lines = stepped_ref.shape[0] // period
    wide = [stepped_ref[pl.ds(b, lines, stride=period), :].astype(jnp.bfloat16) for b in range(period)]
    wide = jnp.concatenate(wide, axis=1)
    line = lax.broadcasted_iota(jnp.int32, (lines, width), 0)
    row = lax.broadcasted_iota(jnp.int32, (lines, width), 1)
    repeat = (row // group == line).astype(jnp.bfloat16)
    spread = lax.dot_general(wide, repeat, (((0,), (0,)), ((), ())), preferred_element_type=jnp.float32)
    entry = lax.broadcasted_iota(jnp.int32, (span, width), 0)
    row = lax.broadcasted_iota(jnp.int32, (span, width), 1)
    kept = jnp.where(entry // columns == row % group, spread, 0.0).astype(jnp.bfloat16)
    column = lax.broadcasted_iota(jnp.int32, (columns, span), 1) % columns
    pick = (column == down_column(position_ref)).astype(jnp.bfloat16)
    rows = jnp.dot(pick, kept, preferred_element_type=jnp.float32).astype(jnp.bfloat16)
    for k in range(copies):
        copies_ref[k] = rows


def middle(position, pieces, states, devices):
    columns = position.shape[1]
    flat = jax.ShapeDtypeStruct(pieces.shape[1:], jnp.float32)
    width = flat.size // columns
    return pl.pallas_call(
        functools.partial(middle_kernel, devices),
        out_shape=(flat, flat, flat, jax.ShapeDtypeStruct((pieces.shape[0], columns, width), jnp.bfloat16)),
        compiler_params=small(),
    )(position, pieces, *states)


def finish_kernel(
    position_ref, new_first_ref, new_second_ref, stepped_ref, own_ref, other_ref,
    master_out, first_out, second_out, copy_out, master_ref, scaled_ref, sems,
):
    core = lax.axis_index("replica")
    chips, columns, width = own_ref.shape
    parts = sems.shape[0] - 3
    copies = [
        pltpu.make_async_copy(new_first_ref, first_out, sems.at[0]),
        pltpu.make_async_copy(new_second_ref, second_out, sems.at[1]),
    ]
    for copy in copies:
        copy.start()
    total = jnp.zeros((columns, width), jnp.float32)
    for ref in (own_ref, other_ref):
        for k in range(chips):
            value = ref[k].astype(jnp.float32)
            total = total + value * value
    factor = lax.rsqrt(jnp.sum(total, axis=1, keepdims=True) / D + norm_epsilon)
    position = down_column(position_ref)
    period = columns // 8
    lane = lax.broadcasted_iota(jnp.int32, (1, LANES), 1)
    line = lax.broadcasted_iota(jnp.int32, stepped_ref.shape, 0) % period
    spread = jnp.zeros(stepped_ref.shape, jnp.float32)
    for p in range(period):
        flat_column = (p * LANES + lane) % columns
        picked = jnp.sum(jnp.where(position == flat_column, factor, 0.0), axis=0, keepdims=True)
        spread = jnp.where(line == p, picked, spread)
    master_ref[...] = stepped_ref[...] * spread
    copies.append(pltpu.make_async_copy(master_ref, master_out, sems.at[2]))
    copies[2].start()
    each = chips // parts
    for p in range(parts):
        for k in range(p * each, (p + 1) * each):
            for ref, place in ((own_ref, core), (other_ref, 1 - core)):
                start = pl.multiple_of((2 * k + place) * width, width)
                scaled_ref[:, pl.ds(start, width)] = (ref[k].astype(jnp.float32) * factor).astype(jnp.bfloat16)
        part = pl.ds(p * 2 * each * width, 2 * each * width)
        copies.append(pltpu.make_async_copy(scaled_ref.at[:, part], copy_out.at[:, part], sems.at[3 + p]))
        copies[3 + p].start()
    for copy in copies:
        copy.wait()


def finish(position, new_first, new_second, stepped, own, other):
    chips, columns, width = own.shape
    wide = (columns, 2 * chips * width)
    parts = 4 if chips % 4 == 0 else 1
    flat = jax.ShapeDtypeStruct(stepped.shape, jnp.float32)
    return pl.pallas_call(
        finish_kernel,
        in_specs=[pl.BlockSpec(memory_space=pltpu.VMEM)] * 6,
        out_specs=(pl.BlockSpec(memory_space=pl.ANY),) * 4,
        out_shape=(flat, flat, flat, jax.ShapeDtypeStruct(wide, jnp.bfloat16)),
        scratch_shapes=[
            pltpu.VMEM(stepped.shape, jnp.float32),
            pltpu.VMEM(wide, jnp.bfloat16),
            pltpu.SemaphoreType.DMA((3 + parts,)),
        ],
        compiler_params=small(),
    )(position, new_first, new_second, stepped, own, other)


def finish_narrow(owners, stepped, blocks):
    columns = owners.shape[0]
    blocks = blocks.astype(jnp.float32)
    factor = lax.rsqrt(jnp.sum(blocks * blocks, axis=(0, 2)) / D + norm_epsilon)
    scaled = jnp.transpose(blocks * factor[None, :, None], (1, 0, 2))
    flat_factor = jnp.zeros((columns,), jnp.float32).at[flat_positions(owners)].set(factor)
    new_master = (stepped.reshape(-1, columns) * flat_factor).reshape(stepped.shape)
    return (new_master, scaled.reshape(columns, -1).astype(jnp.bfloat16))


def spread(value, axes, size):
    return lax.all_to_all(jnp.broadcast_to(value[None], (size,) + value.shape), axes, 0, 0, tiled=True)


def on_device(grads, master, first_moment, second_moment, owners):
    shards, replicas = lax.axis_size("shard"), lax.axis_size("replica")
    devices = shards * replicas
    columns = owners.shape[0]
    if replicas == 2 and master.shape[0] // LANES % 48 == 0:
        kept, sent = pack(grads, shards, master.shape[0] // LANES)
        taken = lax.ppermute(sent, "replica", [(0, 1), (1, 0)])
        states = (master, first_moment, second_moment)
        position, *states, pairs = add_pairs(kept, taken, flat_positions(owners), states)
        pieces = lax.all_to_all(pairs, "shard", 0, 0, tiled=True)
        *updated, copies = middle(position, pieces, states, devices)
        own = lax.all_to_all(copies, "shard", 0, 0, tiled=True)
        other = lax.ppermute(own, "replica", [(0, 1), (1, 0)])
        *flat, model_copy = finish(position, *updated, own, other)
        return (*(x.reshape(-1) for x in flat), model_copy)
    pieces = lax.all_to_all(grads.reshape(devices, -1), AXES, 0, 0, tiled=True)
    gradient = jnp.sum(pieces.astype(jnp.float32), axis=0) / devices
    new_first, new_second, stepped = adam_step(gradient, master, first_moment, second_moment)
    rows = jnp.take(stepped.reshape(-1, columns), flat_positions(owners), axis=1).T.astype(jnp.bfloat16)
    new_master, model_copy = finish_narrow(owners, stepped, spread(rows, AXES, devices))
    return (new_master, new_first, new_second, model_copy)


def solution(mesh):
    placed = (P(AXES, None), P(AXES), P(AXES), P(AXES), P())
    return jax.shard_map(
        on_device,
        mesh=mesh,
        in_specs=placed,
        out_specs=(P(AXES), P(AXES), P(AXES), P()),
        check_vma=False,
    )
```

time: 39 us -> 35 us (0.90)
  blocking collectives: 12.1 us -> 28.2 us
  waiting for transfers between devices: 13.8 us -> 2.21 us
  starting transfers between devices: 7.31 us -> 0.53 us
  Pallas kernels: 2.86 us -> 1.6 us
  other arithmetic: 0.81 us -> 0.18 us
    all_to_all x0 -> x1, blocking collectives: none -> 17 us  [on_device(): pieces = lax.all_to_all(pairs, 'shard', 0, 0, tiled=True)]
    all_to_all x1 -> x0, waiting for transfers between devices: 13 us -> none  [on_device(): pieces = lax.all_to_all(pack(grads, devices), AXES, 0, 0, tiled=True)]
    all_to_all x1 -> x0, starting transfers between devices: 7.3 us -> none  [on_device(): pieces = lax.all_to_all(pack(grads, devices), AXES, 0, 0, tiled=True)]
    pallas_call x3 -> x4, Pallas kernels: 2.86 us -> 1.6 us  [the longest x1 0.93 us: finish(): pl.pallas_call(finish_kernel, in_specs=[pl.BlockSpec(memory_space=pltpu.V...]
    all_to_all x1, blocking collectives: 12.1 us -> 11.3 us  [on_device(): own = lax.all_to_all(copies, 'shard', 0, 0, tiled=True)]
    ppermute x0 -> x1, waiting for transfers between devices: none -> 0.77 us  [on_device(): taken = lax.ppermute(sent, 'replica', [(0, 1), (1, 0)])]
    ppermute x1, waiting for transfers between devices: 0.81 us -> 1.44 us  [on_device(): other = lax.ppermute(own, 'replica', [(0, 1), (1, 0)])]
    reshape x1 -> x0, other arithmetic: 0.63 us -> none  [on_device(): stepped.reshape(-1, LANES)]
  transfers between devices with their start and end apart: 2 -> 2, of which waited for: 2 -> 2; matrix products, arithmetic and copies ran while one was open for 2% -> 1% of each run, Pallas kernels for 0% -> 0%
where the time goes in v5:
time: 35 us; the launch traced here: 34.7 us
  blocking collectives  28.2 us (81%)
  waiting for transfers between devices  2.21 us (6%)
  Pallas kernels  1.6 us (5%)
  local copies, waits for them, and re-layouts  1.26 us (4%)
  between operations  0.67 us (2%)
  starting transfers between devices  0.53 us (2%)
    all_to_all x1, blocking collectives, on_device(): pieces = lax.all_to_all(pairs, 'shard', 0, 0, tiled=True)  17 us
    all_to_all x1, blocking collectives, on_device(): own = lax.all_to_all(copies, 'shard', 0, 0, tiled=True)  11.3 us
    ppermute x1, waiting for transfers between devices, on_device(): other = lax.ppermute(own, 'replica', [(0, 1), (1, 0)])  1.44 us
    unnamed x10, local copies, waits for them, and re-layouts  1.26 us
    pallas_call x1, Pallas kernels, finish(): pl.pallas_call(finish_kernel, in_specs=[pl.BlockSpec(memory_space=pltpu.V...  0.93 us
    ppermute x1, waiting for transfers between devices, on_device(): taken = lax.ppermute(sent, 'replica', [(0, 1), (1, 0)])  0.77 us
  transfers between devices with their start and end apart: 2, of which 2 were waited for; matrix products, arithmetic and copies ran while one was open for 1% of the time, Pallas kernels for 0%

profile of v5, /device:TPU:0, one launch (start us, length us, event | category | flops | bytes accessed | tf_op | source)
XLA Modules:
  0.0 34.7 jit_solution(7858778028447826592)
XLA Ops:
  0.6 0.0 copy-start
  0.6 1.1 %copy-done = bf16[1,196608]{1,0:T(2,128)(2,1)S(1)} copy-done((bf16[1,196608]{1,0:T(2,128)(2,1)S(1)}, bf16[1,196608]{1,0:T(2,128)(2,1)}, u32[]{:S(2)}) %copy-start) | copy-done | bytes 393240
  1.8 0.0 copy-start.1
  1.8 0.0 copy-start.2
  1.8 0.0 copy-start.3
  1.8 0.2 shard_map.84
  2.0 0.0 copy-start.4
  2.0 0.5 %collective-permute-start = (bf16[16,48,128]{2,1,0:T(8,128)(2,1)S(1)}, bf16[16,48,128]{2,1,0:T(8,128)(2,1)S(1)}, u32[]{:S(2)}, u32[]{:S(2)}) collective-permute-start(bf16[16,48,128]{2,1,0:T(8,128)(2,1)S(1)} %get-tuple-element.20), channel_id=1, source_target_pairs={{0,1},{1,0},{2,3},{3,2},{4,5},{5,4},{6,7},{7,6},{8,9},{9,8},{10,11... | collective-permute-start | bytes 589832 | tf_op jit(solution)/shard_map/ppermute | solution.py:217
  2.5 0.1 copy-done.4
  2.6 0.2 convert_reduce_fusion
  2.8 0.8 %collective-permute-done.taken_ref = bf16[16,48,128]{2,1,0:T(8,128)(2,1)S(1)} collective-permute-done((bf16[16,48,128]{2,1,0:T(8,128)(2,1)S(1)}, bf16[16,48,128]{2,1,0:T(8,128)(2,1)S(1)}, u32[]{:S(2)}, u32[]{:S(2)}) %collective-permute-start) | collective-permute-done | bytes 196640 | tf_op jit(solution)/shard_map/ppermute | solution.py:217
  3.6 0.0 copy-done.1
  3.6 0.0 copy-done.2
  3.6 0.0 copy-done.3
  3.6 17.0 %all_to_all.10.pieces_ref = bf16[16,48,128]{2,1,0:T(8,128)(2,1)S(1)} all-to-all(bf16[16,48,128]{2,1,0:T(8,128)(2,1)S(1)} %get-tuple-element.22), channel_id=1, replica_groups=mesh['shard'=16,'replica'=2] {'shard'}, dimensions={0} | all-to-all | bytes 393216 | tf_op jit(solution)/shard_map/all_to_all | solution.py:220
  20.6 0.4 %shard_map.86 = (f32[48,128]{1,0:T(8,128)S(1)}, f32[48,128]{1,0:T(8,128)S(1)}, f32[48,128]{1,0:T(8,128)S(1)}, bf16[16,24,256]{2,1,0:T(8,128)(2,1)S(1)}) custom-call(s32[1,24]{1,0:T(1,128)S(1)} %get-tuple-element.21.position_ref, bf16[16,48,128]{2,1,0:T(8,128)(2,1)S(1)} %all_to_all.10.pieces_ref, f32[48,128]{1,0:T(8,128)S(1)} %get-tuple-element.23.master_ref, ...), custom_call_target="tpu_custom_call" | custom-call | tf_op jit(solution)/shard_map/pallas_call | solution.py:127
  21.0 11.3 %all_to_all.11.own_ref = bf16[16,24,256]{2,1,0:T(8,128)(2,1)S(1)} all-to-all(bf16[16,24,256]{2,1,0:T(8,128)(2,1)S(1)} %get-tuple-element.29), channel_id=1, replica_groups=mesh['shard'=16,'replica'=2] {'shard'}, dimensions={0} | all-to-all | bytes 393216 | tf_op jit(solution)/shard_map/all_to_all | solution.py:222
  32.3 0.0 collective-permute-start.1
  32.3 1.4 %collective-permute-done.1.other_ref = bf16[16,24,256]{2,1,0:T(8,128)(2,1)S(1)} collective-permute-done((bf16[16,24,256]{2,1,0:T(8,128)(2,1)S(1)}, bf16[16,24,256]{2,1,0:T(8,128)(2,1)S(1)}, u32[]{:S(2)}, u32[]{:S(2)}) %collective-permute-start.1) | collective-permute-done | bytes 196640 | tf_op jit(solution)/shard_map/ppermute | solution.py:223
  33.7 0.9 %shard_map.87 = (f32[48,128]{1,0:T(8,128)}, f32[48,128]{1,0:T(8,128)}, f32[48,128]{1,0:T(8,128)}, bf16[24,8192]{1,0:T(8,128)(2,1)}) custom-call(s32[1,24]{1,0:T(1,128)S(1)} %get-tuple-element.21.position_ref, f32[48,128]{1,0:T(8,128)S(1)} %get-tuple-element.26.new_first_ref, f32[48,128]{1,0:T(8,128)S(1)} %get-tuple-element.27.new_second_ref, ...), custom_call_target="tpu_custom_call" | custom-call | tf_op jit(solution)/shard_map/pallas_call | solution.py:183
  (1 shorter events, 0.0 us)
Async XLA Ops:
  0.6 1.1 %copy-start = (bf16[1,196608]{1,0:T(2,128)(2,1)S(1)}, bf16[1,196608]{1,0:T(2,128)(2,1)}, u32[]{:S(2)}) copy-start(bf16[1,196608]{1,0:T(2,128)(2,1)} %grads_ref.1) | copy-start | bytes 1179652
  1.8 1.8 %copy-start.1 = (f32[6144]{0:T(1024)S(1)}, f32[6144]{0:T(1024)}, u32[]{:S(2)}) copy-start(f32[6144]{0:T(1024)} %param.6) | copy-start | bytes 73732
  1.8 1.8 %copy-start.2 = (f32[6144]{0:T(1024)S(1)}, f32[6144]{0:T(1024)}, u32[]{:S(2)}) copy-start(f32[6144]{0:T(1024)} %param.7) | copy-start | bytes 73732
  1.8 1.8 %copy-start.3 = (f32[6144]{0:T(1024)S(1)}, f32[6144]{0:T(1024)}, u32[]{:S(2)}) copy-start(f32[6144]{0:T(1024)} %param.8) | copy-start | bytes 73732
  2.0 0.7 %copy-start.4 = (s32[24]{0:T(128)S(1)}, s32[24]{0:T(128)}, u32[]{:S(2)}) copy-start(s32[24]{0:T(128)} %param.9) | copy-start | bytes 292
  2.0 1.6 %collective-permute-start = (bf16[16,48,128]{2,1,0:T(8,128)(2,1)S(1)}, bf16[16,48,128]{2,1,0:T(8,128)(2,1)S(1)}, u32[]{:S(2)}, u32[]{:S(2)}) collective-permute-start(bf16[16,48,128]{2,1,0:T(8,128)(2,1)S(1)} %get-tuple-element.20), channel_id=1, source_target_pairs={{0,1},{1,0},{2,3},{3,2},{4,5},{5,4},{6,7},{7,6},{8,9},{9,8},{10,11... | collective-permute-start | bytes 589832 | tf_op jit(solution)/shard_map/ppermute | solution.py:217
  32.3 1.4 %collective-permute-start.1 = (bf16[16,24,256]{2,1,0:T(8,128)(2,1)S(1)}, bf16[16,24,256]{2,1,0:T(8,128)(2,1)S(1)}, u32[]{:S(2)}, u32[]{:S(2)}) collective-permute-start(bf16[16,24,256]{2,1,0:T(8,128)(2,1)S(1)} %all_to_all.11.own_ref), channel_id=1, source_target_pairs={{0,1},{1,0},{2,3},{3,2},{4,5},{5,4},{6,7},{7,6},{8,9},{9,8},{10,11... | collective-permute-start | bytes 589832 | tf_op jit(solution)/shard_map/ppermute | solution.py:223

commit v6 on v5

v6 whole, which is shorter than its diff:
```python
import functools

import jax
import jax.numpy as jnp
from jax import lax
from jax.experimental import pallas as pl
from jax.experimental.pallas import tpu as pltpu
from jax.sharding import PartitionSpec as P

D = 8192


learning_rate = 0.1
adam_epsilon = 1e-08
norm_epsilon = 1e-06
first_correction = 1.0 - 0.9**20
second_correction = 1.0 - 0.95**20
AXES = ("shard", "replica")
HALVES = ("half", "near", "core")
LANES = 128


def adam_step(gradient, master, first_moment, second_moment):
    new_first = 0.9 * first_moment + 0.1 * gradient
    new_second = 0.95 * second_moment + 0.05 * gradient * gradient
    stepped = master - learning_rate * (new_first / first_correction) / (
        jnp.sqrt(new_second / second_correction) + adam_epsilon
    )
    return (new_first, new_second, stepped)


def flat_positions(owners):
    column_ids = jnp.arange(owners.shape[0], dtype=jnp.int32)
    ranked_below = owners[None, :] < owners[:, None]
    same_before = (owners[None, :] == owners[:, None]) & (column_ids[None, :] < column_ids[:, None])
    return jnp.sum((ranked_below | same_before).astype(jnp.int32), axis=1)


def small(**more):
    return pltpu.CompilerParams(vmem_limit_bytes=6 * 2**20, **more)


def pack_kernel(grads_ref, kept_ref, sent_ref, wide_ref):
    near, halves, lines, lanes = kept_ref.shape
    core = lax.axis_index("core")
    row_ref = wide_ref.reshape(1, wide_ref.shape[0] * lanes)
    width = 2 * lines * lanes
    for k in range(near * halves):
        row_ref[:, k * width : (k + 1) * width] = grads_ref[:, k * width : (k + 1) * width].astype(jnp.float32)
        for ref, place in ((kept_ref, core), (sent_ref, 1 - core)):
            start = pl.multiple_of((2 * k + place) * lines, lines)
            ref[k % near, k // near] = wide_ref[pl.ds(start, lines), :].astype(jnp.bfloat16)


def pack(grads, halves, near, lines):
    packed = jax.ShapeDtypeStruct((near, halves, lines, LANES), jnp.bfloat16)
    return pl.pallas_call(
        pack_kernel,
        out_shape=(packed, packed),
        scratch_shapes=[pltpu.VMEM((grads.shape[1] // LANES, LANES), jnp.float32)],
        compiler_params=small(),
    )(grads)


def pair_kernel(kept_ref, taken_ref, position_ref, pairs_ref, position_out):
    pairs = kept_ref[...].astype(jnp.float32) + taken_ref[...].astype(jnp.float32)
    pairs_ref[...] = pairs.astype(jnp.bfloat16)
    position_out[...] = position_ref[...]


def add_pairs(kept, taken, position):
    position = position[None, :]
    return pl.pallas_call(
        pair_kernel,
        out_shape=(
            jax.ShapeDtypeStruct(kept.shape, jnp.bfloat16),
            jax.ShapeDtypeStruct(position.shape, position.dtype),
        ),
        compiler_params=small(),
    )(kept, taken, position)


def partial_kernel(pieces_ref, partial_ref):
    total = pieces_ref[0].astype(jnp.float32)
    for k in range(1, pieces_ref.shape[0]):
        total = total + pieces_ref[k].astype(jnp.float32)
    partial_ref[...] = total.astype(jnp.bfloat16)


def add_pieces(pieces):
    return pl.pallas_call(
        partial_kernel,
        out_shape=jax.ShapeDtypeStruct(pieces.shape[1:], jnp.bfloat16),
        compiler_params=small(),
    )(pieces)


def down_column(row_ref):
    columns = row_ref.shape[1]
    square = (columns, columns)
    same = lax.broadcasted_iota(jnp.int32, square, 0) == lax.broadcasted_iota(jnp.int32, square, 1)
    row = jnp.broadcast_to(row_ref[...].astype(jnp.float32), square)
    return jnp.sum(jnp.where(same, row, 0.0), axis=1, keepdims=True).astype(jnp.int32)


def middle_kernel(
    devices, position_ref, partial_ref, partner_ref, mine_ref, theirs_ref,
    new_first_ref, new_second_ref, stepped_ref, copies_ref, both_ref,
):
    half = lax.axis_index("half")
    copies, halves, columns, width = copies_ref.shape
    lines = stepped_ref.shape[0]
    total = partial_ref[...].astype(jnp.float32) + partner_ref[...].astype(jnp.float32)
    swapped = jnp.concatenate([total[1], total[0]])
    gradient = jnp.where(half == 0, total.reshape(swapped.shape), swapped) / devices
    states = [jnp.concatenate([mine_ref[k], theirs_ref[k]]) for k in range(3)]
    new_first, new_second, stepped = adam_step(gradient, *states)
    new_first_ref[...] = new_first[:lines]
    new_second_ref[...] = new_second[:lines]
    stepped_ref[...] = stepped[:lines]
    both_ref[...] = stepped
    period = columns // 8
    span = period * LANES
    group = span // columns
    groups = halves * lines // period
    wide = [both_ref[pl.ds(b, groups, stride=period), :].astype(jnp.bfloat16) for b in range(period)]
    wide = jnp.concatenate(wide, axis=1)
    line = lax.broadcasted_iota(jnp.int32, (groups, halves * width), 0)
    row = lax.broadcasted_iota(jnp.int32, (groups, halves * width), 1)
    repeat = (row // group == line).astype(jnp.bfloat16)
    spread = lax.dot_general(wide, repeat, (((0,), (0,)), ((), ())), preferred_element_type=jnp.float32)
    entry = lax.broadcasted_iota(jnp.int32, (span, halves * width), 0)
    row = lax.broadcasted_iota(jnp.int32, (span, halves * width), 1)
    kept = jnp.where(entry // columns == row % group, spread, 0.0).astype(jnp.bfloat16)
    column = lax.broadcasted_iota(jnp.int32, (columns, span), 1) % columns
    pick = (column == down_column(position_ref)).astype(jnp.bfloat16)
    rows = jnp.dot(pick, kept, preferred_element_type=jnp.float32).astype(jnp.bfloat16)
    for k in range(copies):
        copies_ref[k, half] = rows[:, :width]
        copies_ref[k, 1 - half] = rows[:, width:]


def middle(position, partial, partner, mine, theirs, near, devices):
    columns = position.shape[1]
    halves, lines, lanes = partial.shape
    flat = jax.ShapeDtypeStruct((lines, lanes), jnp.float32)
    rows = (near, halves, columns, flat.size // columns)
    return pl.pallas_call(
        functools.partial(middle_kernel, devices),
        out_shape=(flat, flat, flat, jax.ShapeDtypeStruct(rows, jnp.bfloat16)),
        scratch_shapes=[pltpu.VMEM((halves * lines, lanes), jnp.float32)],
        compiler_params=small(),
    )(position, partial, partner, mine, theirs)


def finish_kernel(
    position_ref, new_first_ref, new_second_ref, stepped_ref, own_ref, other_ref,
    master_out, first_out, second_out, copy_out, master_ref, scaled_ref, sems,
):
    core = lax.axis_index("core")
    near, halves, columns, width = own_ref.shape
    chips = near * halves
    parts = sems.shape[0] - 3
    copies = [
        pltpu.make_async_copy(new_first_ref, first_out, sems.at[0]),
        pltpu.make_async_copy(new_second_ref, second_out, sems.at[1]),
    ]
    for copy in copies:
        copy.start()
    total = jnp.zeros((columns, width), jnp.float32)
    for ref in (own_ref, other_ref):
        for k in range(chips):
            value = ref[k % near, k // near].astype(jnp.float32)
            total = total + value * value
    factor = lax.rsqrt(jnp.sum(total, axis=1, keepdims=True) / D + norm_epsilon)
    position = down_column(position_ref)
    period = columns // 8
    lane = lax.broadcasted_iota(jnp.int32, (1, LANES), 1)
    line = lax.broadcasted_iota(jnp.int32, stepped_ref.shape, 0) % period
    spread = jnp.zeros(stepped_ref.shape, jnp.float32)
    for p in range(period):
        flat_column = (p * LANES + lane) % columns
        picked = jnp.sum(jnp.where(position == flat_column, factor, 0.0), axis=0, keepdims=True)
        spread = jnp.where(line == p, picked, spread)
    master_ref[...] = stepped_ref[...] * spread
    copies.append(pltpu.make_async_copy(master_ref, master_out, sems.at[2]))
    copies[2].start()
    each = chips // parts
    for p in range(parts):
        for k in range(p * each, (p + 1) * each):
            for ref, place in ((own_ref, core), (other_ref, 1 - core)):
                start = pl.multiple_of((2 * k + place) * width, width)
                scaled = ref[k % near, k // near].astype(jnp.float32) * factor
                scaled_ref[:, pl.ds(start, width)] = scaled.astype(jnp.bfloat16)
        part = pl.ds(p * 2 * each * width, 2 * each * width)
        copies.append(pltpu.make_async_copy(scaled_ref.at[:, part], copy_out.at[:, part], sems.at[3 + p]))
        copies[3 + p].start()
    for copy in copies:
        copy.wait()


def finish(position, new_first, new_second, stepped, own, other):
    near, halves, columns, width = own.shape
    chips = near * halves
    wide = (columns, 2 * chips * width)
    parts = 4 if chips % 4 == 0 else 1
    flat = jax.ShapeDtypeStruct(stepped.shape, jnp.float32)
    return pl.pallas_call(
        finish_kernel,
        in_specs=[pl.BlockSpec(memory_space=pltpu.VMEM)] * 6,
        out_specs=(pl.BlockSpec(memory_space=pl.ANY),) * 4,
        out_shape=(flat, flat, flat, jax.ShapeDtypeStruct(wide, jnp.bfloat16)),
        scratch_shapes=[
            pltpu.VMEM(stepped.shape, jnp.float32),
            pltpu.VMEM(wide, jnp.bfloat16),
            pltpu.SemaphoreType.DMA((3 + parts,)),
        ],
        compiler_params=small(),
    )(position, new_first, new_second, stepped, own, other)


def finish_narrow(owners, stepped, blocks):
    columns = owners.shape[0]
    blocks = blocks.astype(jnp.float32)
    factor = lax.rsqrt(jnp.sum(blocks * blocks, axis=(0, 2)) / D + norm_epsilon)
    scaled = jnp.transpose(blocks * factor[None, :, None], (1, 0, 2))
    flat_factor = jnp.zeros((columns,), jnp.float32).at[flat_positions(owners)].set(factor)
    new_master = (stepped.reshape(-1, columns) * flat_factor).reshape(stepped.shape)
    return (new_master, scaled.reshape(columns, -1).astype(jnp.bfloat16))


def spread(value, axes, size):
    return lax.all_to_all(jnp.broadcast_to(value[None], (size,) + value.shape), axes, 0, 0, tiled=True)


def on_halves(grads, master, first_moment, second_moment, owners):
    halves, near, cores = (lax.axis_size(axis) for axis in HALVES)
    swap = [(0, 1), (1, 0)]
    kept, sent = pack(grads, halves, near, master.shape[0] // LANES)
    mine = jnp.stack([x.reshape(-1, LANES) for x in (master, first_moment, second_moment)])
    taken = lax.ppermute(sent, "core", swap)
    theirs = lax.ppermute(mine, "half", swap)
    pairs, position = add_pairs(kept, taken, flat_positions(owners))
    partial = add_pieces(lax.all_to_all(pairs, "near", 0, 0, tiled=True))
    partner = lax.ppermute(partial, "half", swap)
    *updated, copies = middle(position, partial, partner, mine, theirs, near, halves * near * cores)
    own = lax.all_to_all(copies, "near", 0, 0, tiled=True)
    other = lax.ppermute(own, "core", swap)
    *flat, model_copy = finish(position, *updated, own, other)
    return (*(x.reshape(-1) for x in flat), model_copy)


def on_device(grads, master, first_moment, second_moment, owners):
    devices = lax.axis_size(AXES)
    columns = owners.shape[0]
    pieces = lax.all_to_all(grads.reshape(devices, -1), AXES, 0, 0, tiled=True)
    gradient = jnp.sum(pieces.astype(jnp.float32), axis=0) / devices
    new_first, new_second, stepped = adam_step(gradient, master, first_moment, second_moment)
    rows = jnp.take(stepped.reshape(-1, columns), flat_positions(owners), axis=1).T.astype(jnp.bfloat16)
    new_master, model_copy = finish_narrow(owners, stepped, spread(rows, AXES, devices))
    return (new_master, new_first, new_second, model_copy)


def solution(mesh):
    body, axes = on_device, AXES
    if mesh.shape["replica"] == 2 and mesh.shape["shard"] % 4 == 0:
        body, axes = on_halves, HALVES
        mesh = jax.sharding.Mesh(mesh.devices.reshape(2, -1, 2), HALVES)
    placed = (P(axes, None), P(axes), P(axes), P(axes), P())
    return jax.shard_map(
        body,
        mesh=mesh,
        in_specs=placed,
        out_specs=(P(axes), P(axes), P(axes), P()),
        check_vma=False,
    )
```

time: 35 us -> 35.2 us (level)
  blocking collectives: 28.2 us -> 8.76 us
  starting transfers between devices: 0.53 us -> 11.3 us
  waiting for transfers between devices: 2.21 us -> 10.2 us
  Pallas kernels: 1.6 us -> 2.36 us
    all_to_all x2 -> x1, blocking collectives: 28.2 us -> 8.76 us  [on_halves(): own = lax.all_to_all(copies, 'near', 0, 0, tiled=True)]
    all_to_all x0 -> x1, starting transfers between devices: none -> 6.23 us  [on_halves(): partial = add_pieces(lax.all_to_all(pairs, 'near', 0, 0, tiled=True))]
    all_to_all x0 -> x1, waiting for transfers between devices: none -> 5.15 us  [on_halves(): partial = add_pieces(lax.all_to_all(pairs, 'near', 0, 0, tiled=True))]
    ppermute x2 -> x4, starting transfers between devices: 0.53 us -> 5.08 us  [the longest x1 2.65 us: on_halves(): theirs = lax.ppermute(mine, 'half', swap)]
    ppermute x2 -> x4, waiting for transfers between devices: 2.21 us -> 5.09 us  [the longest x1 2.89 us: on_halves(): partner = lax.ppermute(partial, 'half', swap)]
    pallas_call x1 -> x2, Pallas kernels: 0.05 us -> 0.75 us  [the longest x1 0.72 us: add_pairs(): pl.pallas_call(pair_kernel, out_shape=(jax.ShapeDtypeStruct(kept.shape, j...]
  transfers between devices with their start and end apart: 2 -> 5, of which waited for: 2 -> 4; matrix products, arithmetic and copies ran while one was open for 1% -> 1% of each run, Pallas kernels for 0% -> 0%
where the time goes in v6:
time: 35.2 us; the launch traced here: 34.8 us
  starting transfers between devices  11.3 us (32%)
  waiting for transfers between devices  10.2 us (29%)
  blocking collectives  8.76 us (25%)
  Pallas kernels  2.36 us (7%)
  local copies, waits for them, and re-layouts  1.26 us (4%)
  between operations  0.69 us (2%)
    all_to_all x1, blocking collectives, on_halves(): own = lax.all_to_all(copies, 'near', 0, 0, tiled=True)  8.76 us
    all_to_all x1, starting transfers between devices, on_halves(): partial = add_pieces(lax.all_to_all(pairs, 'near', 0, 0, tiled=True))  6.23 us
    all_to_all x1, waiting for transfers between devices, on_halves(): partial = add_pieces(lax.all_to_all(pairs, 'near', 0, 0, tiled=True))  5.15 us
    ppermute x1, waiting for transfers between devices, on_halves(): partner = lax.ppermute(partial, 'half', swap)  2.89 us
    ppermute x1, starting transfers between devices, on_halves(): theirs = lax.ppermute(mine, 'half', swap)  2.65 us
    ppermute x1, starting transfers between devices, on_halves(): partner = lax.ppermute(partial, 'half', swap)  1.9 us
    ppermute x1, waiting for transfers between devices, on_halves(): other = lax.ppermute(own, 'core', swap)  1.44 us
    unnamed x10, local copies, waits for them, and re-layouts  1.26 us
  transfers between devices with their start and end apart: 5, of which 4 were waited for; matrix products, arithmetic and copies ran while one was open for 1% of the time, Pallas kernels for 0%

profile of v6, /device:TPU:0, one launch (start us, length us, event | category | flops | bytes accessed | tf_op | source)
XLA Modules:
  0.0 34.8 jit_solution(15430362451671042332)
XLA Ops:
  0.6 0.0 copy-start
  0.6 1.1 %copy-done = bf16[1,196608]{1,0:T(2,128)(2,1)S(1)} copy-done((bf16[1,196608]{1,0:T(2,128)(2,1)S(1)}, bf16[1,196608]{1,0:T(2,128)(2,1)}, u32[]{:S(2)}) %copy-start) | copy-done | bytes 393240
  1.8 0.2 shard_map.84
  1.9 0.0 copy-start.4
  2.0 0.5 %collective-permute-start = (bf16[8,2,48,128]{3,2,1,0:T(8,128)(2,1)S(1)}, bf16[8,2,48,128]{3,2,1,0:T(8,128)(2,1)S(1)}, u32[]{:S(2)}, u32[]{:S(2)}) collective-permute-start(bf16[8,2,48,128]{3,2,1,0:T(8,128)(2,1)S(1)} %get-tuple-element.17), channel_id=1, source_target_pairs={{0,1},{1,0},{2,3},{3,2},{4,5},{5,4},{6,7},{7,6},{8,9},{9,8},{10,11... | collective-permute-start | bytes 589832 | tf_op jit(solution)/shard_map/ppermute | solution.py:241
  2.5 0.1 copy-done.4
  2.6 0.2 convert_reduce_fusion
  2.8 0.8 %collective-permute-done.taken_ref = bf16[8,2,48,128]{3,2,1,0:T(8,128)(2,1)S(1)} collective-permute-done((bf16[8,2,48,128]{3,2,1,0:T(8,128)(2,1)S(1)}, bf16[8,2,48,128]{3,2,1,0:T(8,128)(2,1)S(1)}, u32[]{:S(2)}, u32[]{:S(2)}) %collective-permute-start) | collective-permute-done | bytes 196640 | tf_op jit(solution)/shard_map/ppermute | solution.py:241
  3.6 0.7 %shard_map.85 = (bf16[8,2,48,128]{3,2,1,0:T(8,128)(2,1)}, s32[1,24]{1,0:T(1,128)S(1)}) custom-call(bf16[8,2,48,128]{3,2,1,0:T(8,128)(2,1)S(1)} %get-tuple-element.16.kept_ref, bf16[8,2,48,128]{3,2,1,0:T(8,128)(2,1)S(1)} %collective-permute-done.taken_ref, s32[1,24]{1,0:T(1,128)S(1)} %bitcast.7), custom_call_target="tpu_custom_call" | custom-call | tf_op jit(solution)/shard_map/pallas_call | solution.py:73
  4.3 0.0 copy-start.1
  4.3 6.2 %all-to-all-start = ((bf16[8,2,48,128]{3,2,1,0:T(8,128)(2,1)}), bf16[8,2,48,128]{3,2,1,0:T(8,128)(2,1)S(1)}, u32[]{:S(2)}, u32[]{:S(2)}) async-start(bf16[8,2,48,128]{3,2,1,0:T(8,128)(2,1)} %get-tuple-element.19), calls=%async_computation | async-start | bytes 393216 | tf_op jit(solution)/shard_map/all_to_all | solution.py:244
  10.5 0.0 copy-done.1
  10.5 0.0 copy-done.2
  10.5 0.0 copy-done.3
  10.6 2.7 %collective-permute-start.2 = (f32[3,48,128]{2,1,0:T(8,128)S(1)}, f32[3,48,128]{2,1,0:T(8,128)S(1)}, u32[]{:S(2)}, u32[]{:S(2)}) collective-permute-start(f32[3,48,128]{2,1,0:T(8,128)S(1)} %pad_maximum_fusion.mine_ref), channel_id=1, source_target_pairs={{0,16},{16,0},{1,17},{17,1},{2,18},{18,2},{3,19},{19,3},{4,20},{20... | collective-permute-start | bytes 221192 | tf_op jit(solution)/shard_map/ppermute | solution.py:242
  13.2 5.1 %all-to-all-done.pieces_ref = bf16[8,2,48,128]{3,2,1,0:T(8,128)(2,1)S(1)} async-done(((bf16[8,2,48,128]{3,2,1,0:T(8,128)(2,1)}), bf16[8,2,48,128]{3,2,1,0:T(8,128)(2,1)S(1)}, u32[]{:S(2)}, u32[]{:S(2)}) %all-to-all-start) | async-done | bytes 196640 | tf_op jit(solution)/shard_map/all_to_all | solution.py:244
  18.4 1.9 %collective-permute-start.1 = (bf16[2,48,128]{2,1,0:T(8,128)(2,1)S(1)}, bf16[2,48,128]{2,1,0:T(8,128)(2,1)S(1)}, u32[]{:S(2)}, u32[]{:S(2)}) collective-permute-start(bf16[2,48,128]{2,1,0:T(8,128)(2,1)S(1)} %shard_map.86.partial_ref), channel_id=1, source_target_pairs={{0,16},{16,0},{1,17},{17,1},{2,18},{18,2},{3,19},{19,3},{4,20},{20... | collective-permute-start | bytes 73736 | tf_op jit(solution)/shard_map/ppermute | solution.py:245
  20.3 0.0 collective-permute-done.2.theirs_ref
  20.3 2.9 %collective-permute-done.1.partner_ref = bf16[2,48,128]{2,1,0:T(8,128)(2,1)S(1)} collective-permute-done((bf16[2,48,128]{2,1,0:T(8,128)(2,1)S(1)}, bf16[2,48,128]{2,1,0:T(8,128)(2,1)S(1)}, u32[]{:S(2)}, u32[]{:S(2)}) %collective-permute-start.1) | collective-permute-done | bytes 24608 | tf_op jit(solution)/shard_map/ppermute | solution.py:245
  23.2 0.5 %shard_map.87 = (f32[48,128]{1,0:T(8,128)S(1)}, f32[48,128]{1,0:T(8,128)S(1)}, f32[48,128]{1,0:T(8,128)S(1)}, bf16[8,2,24,256]{3,2,1,0:T(8,128)(2,1)S(1)}) custom-call(s32[1,24]{1,0:T(1,128)S(1)} %get-tuple-element.18.position_ref, bf16[2,48,128]{2,1,0:T(8,128)(2,1)S(1)} %shard_map.86.partial_ref, ...), custom_call_target="tpu_custom_call" | custom-call | tf_op jit(solution)/shard_map/pallas_call | solution.py:148
  23.7 8.8 %all_to_all.10.own_ref = bf16[8,2,24,256]{3,2,1,0:T(8,128)(2,1)S(1)} all-to-all(bf16[8,2,24,256]{3,2,1,0:T(8,128)(2,1)S(1)} %get-tuple-element.23), channel_id=1, replica_groups=mesh['half'=2,'near'=8,'core'=2] {'near'}, dimensions={0} | all-to-all | bytes 393216 | tf_op jit(solution)/shard_map/all_to_all | solution.py:247
  32.4 0.0 collective-permute-start.3
  32.4 1.4 %collective-permute-done.3.other_ref = bf16[8,2,24,256]{3,2,1,0:T(8,128)(2,1)S(1)} collective-permute-done((bf16[8,2,24,256]{3,2,1,0:T(8,128)(2,1)S(1)}, bf16[8,2,24,256]{3,2,1,0:T(8,128)(2,1)S(1)}, u32[]{:S(2)}, u32[]{:S(2)}) %collective-permute-start.3) | collective-permute-done | bytes 196640 | tf_op jit(solution)/shard_map/ppermute | solution.py:248
  33.9 0.9 %shard_map.88 = (f32[48,128]{1,0:T(8,128)}, f32[48,128]{1,0:T(8,128)}, f32[48,128]{1,0:T(8,128)}, bf16[24,8192]{1,0:T(8,128)(2,1)}) custom-call(s32[1,24]{1,0:T(1,128)S(1)} %get-tuple-element.18.position_ref, f32[48,128]{1,0:T(8,128)S(1)} %get-tuple-element.20.new_first_ref, f32[48,128]{1,0:T(8,128)S(1)} %get-tuple-element.21.new_second_ref, ...), custom_call_target="tpu_custom_call" | custom-call | tf_op jit(solution)/shard_map/pallas_call | solution.py:208
  (4 shorter events, 0.0 us)
Async XLA Ops:
  0.6 1.1 %copy-start = (bf16[1,196608]{1,0:T(2,128)(2,1)S(1)}, bf16[1,196608]{1,0:T(2,128)(2,1)}, u32[]{:S(2)}) copy-start(bf16[1,196608]{1,0:T(2,128)(2,1)} %grads_ref.1) | copy-start | bytes 1179652
  1.9 0.7 %copy-start.4 = (s32[24]{0:T(128)S(1)}, s32[24]{0:T(128)}, u32[]{:S(2)}) copy-start(s32[24]{0:T(128)} %param.9) | copy-start | bytes 292
  2.0 1.6 %collective-permute-start = (bf16[8,2,48,128]{3,2,1,0:T(8,128)(2,1)S(1)}, bf16[8,2,48,128]{3,2,1,0:T(8,128)(2,1)S(1)}, u32[]{:S(2)}, u32[]{:S(2)}) collective-permute-start(bf16[8,2,48,128]{3,2,1,0:T(8,128)(2,1)S(1)} %get-tuple-element.17), channel_id=1, source_target_pairs={{0,1},{1,0},{2,3},{3,2},{4,5},{5,4},{6,7},{7,6},{8,9},{9,8},{10,11... | collective-permute-start | bytes 589832 | tf_op jit(solution)/shard_map/ppermute | solution.py:241
  4.3 6.2 %copy-start.1 = (f32[6144]{0:T(1024)S(1)}, f32[6144]{0:T(1024)}, u32[]{:S(2)}) copy-start(f32[6144]{0:T(1024)} %param.8) | copy-start | bytes 73732
  4.3 6.2 %copy-start.2 = (f32[6144]{0:T(1024)S(1)}, f32[6144]{0:T(1024)}, u32[]{:S(2)}) copy-start(f32[6144]{0:T(1024)} %param.7) | copy-start | bytes 73732
  4.3 6.2 %copy-start.3 = (f32[6144]{0:T(1024)S(1)}, f32[6144]{0:T(1024)}, u32[]{:S(2)}) copy-start(f32[6144]{0:T(1024)} %param.6) | copy-start | bytes 73732
  4.3 14.1 %all-to-all-start = ((bf16[8,2,48,128]{3,2,1,0:T(8,128)(2,1)}), bf16[8,2,48,128]{3,2,1,0:T(8,128)(2,1)S(1)}, u32[]{:S(2)}, u32[]{:S(2)}) async-start(bf16[8,2,48,128]{3,2,1,0:T(8,128)(2,1)} %get-tuple-element.19), calls=%async_computation | async-start | bytes 393216 | tf_op jit(solution)/shard_map/all_to_all | solution.py:244
  10.6 9.7 %collective-permute-start.2 = (f32[3,48,128]{2,1,0:T(8,128)S(1)}, f32[3,48,128]{2,1,0:T(8,128)S(1)}, u32[]{:S(2)}, u32[]{:S(2)}) collective-permute-start(f32[3,48,128]{2,1,0:T(8,128)S(1)} %pad_maximum_fusion.mine_ref), channel_id=1, source_target_pairs={{0,16},{16,0},{1,17},{17,1},{2,18},{18,2},{3,19},{19,3},{4,20},{20... | collective-permute-start | bytes 221192 | tf_op jit(solution)/shard_map/ppermute | solution.py:242
  18.4 4.8 %collective-permute-start.1 = (bf16[2,48,128]{2,1,0:T(8,128)(2,1)S(1)}, bf16[2,48,128]{2,1,0:T(8,128)(2,1)S(1)}, u32[]{:S(2)}, u32[]{:S(2)}) collective-permute-start(bf16[2,48,128]{2,1,0:T(8,128)(2,1)S(1)} %shard_map.86.partial_ref), channel_id=1, source_target_pairs={{0,16},{16,0},{1,17},{17,1},{2,18},{18,2},{3,19},{19,3},{4,20},{20... | collective-permute-start | bytes 73736 | tf_op jit(solution)/shard_map/ppermute | solution.py:245
  32.4 1.4 %collective-permute-start.3 = (bf16[8,2,24,256]{3,2,1,0:T(8,128)(2,1)S(1)}, bf16[8,2,24,256]{3,2,1,0:T(8,128)(2,1)S(1)}, u32[]{:S(2)}, u32[]{:S(2)}) collective-permute-start(bf16[8,2,24,256]{3,2,1,0:T(8,128)(2,1)S(1)} %all_to_all.10.own_ref), channel_id=1, source_target_pairs={{0,1},{1,0},{2,3},{3,2},{4,5},{5,4},{6,7},{7,6},{8,9},{9,8},{10,11... | collective-permute-start | bytes 589832 | tf_op jit(solution)/shard_map/ppermute | solution.py:248

commit v7 on v6

--- a/solution.py
+++ b/solution.py
@@ -62,35 +62,39 @@
     )(grads)
 
 
-def pair_kernel(kept_ref, taken_ref, position_ref, pairs_ref, position_out):
+def pair_kernel(kept_ref, taken_ref, *refs):
+    *held, pairs_ref = refs
     pairs = kept_ref[...].astype(jnp.float32) + taken_ref[...].astype(jnp.float32)
     pairs_ref[...] = pairs.astype(jnp.bfloat16)
-    position_out[...] = position_ref[...]
-
-
-def add_pairs(kept, taken, position):
+    for source, target in zip(held[:4], held[4:]):
+        target[...] = source[...]
+
+
+def add_pairs(kept, taken, position, states):
+    flat = jax.ShapeDtypeStruct(kept.shape[2:], jnp.float32)
     position = position[None, :]
+    small_shapes = (jax.ShapeDtypeStruct(position.shape, position.dtype), flat, flat, flat)
     return pl.pallas_call(
         pair_kernel,
-        out_shape=(
-            jax.ShapeDtypeStruct(kept.shape, jnp.bfloat16),
-            jax.ShapeDtypeStruct(position.shape, position.dtype),
-        ),
-        compiler_params=small(),
-    )(kept, taken, position)
-
-
-def partial_kernel(pieces_ref, partial_ref):
-    total = pieces_ref[0].astype(jnp.float32)
-    for k in range(1, pieces_ref.shape[0]):
-        total = total + pieces_ref[k].astype(jnp.float32)
-    partial_ref[...] = total.astype(jnp.bfloat16)
+        out_shape=(*small_shapes, jax.ShapeDtypeStruct(kept.shape, jnp.bfloat16)),
+        compiler_params=small(),
+    )(kept, taken, position, *(x.reshape(flat.shape) for x in states))
+
+
+def partial_kernel(pieces_ref, kept_ref, sent_ref):
+    half = lax.axis_index("half")
+    for ref, place in ((kept_ref, half), (sent_ref, 1 - half)):
+        total = pieces_ref[0, place].astype(jnp.float32)
+        for k in range(1, pieces_ref.shape[0]):
+            total = total + pieces_ref[k, place].astype(jnp.float32)
+        ref[...] = total.astype(ref.dtype)
 
 
 def add_pieces(pieces):
+    shape = pieces.shape[2:]
     return pl.pallas_call(
         partial_kernel,
-        out_shape=jax.ShapeDtypeStruct(pieces.shape[1:], jnp.bfloat16),
+        out_shape=(jax.ShapeDtypeStruct(shape, jnp.float32), jax.ShapeDtypeStruct(shape, jnp.bfloat16)),
         compiler_params=small(),
     )(pieces)
 
@@ -104,53 +108,56 @@
 
 
 def middle_kernel(
-    devices, position_ref, partial_ref, partner_ref, mine_ref, theirs_ref,
-    new_first_ref, new_second_ref, stepped_ref, copies_ref, both_ref,
+    devices, position_ref, partial_ref, partner_ref, master_ref, first_ref, second_ref,
+    new_first_ref, new_second_ref, stepped_ref, rows_ref,
 ):
-    half = lax.axis_index("half")
-    copies, halves, columns, width = copies_ref.shape
-    lines = stepped_ref.shape[0]
-    total = partial_ref[...].astype(jnp.float32) + partner_ref[...].astype(jnp.float32)
-    swapped = jnp.concatenate([total[1], total[0]])
-    gradient = jnp.where(half == 0, total.reshape(swapped.shape), swapped) / devices
-    states = [jnp.concatenate([mine_ref[k], theirs_ref[k]]) for k in range(3)]
-    new_first, new_second, stepped = adam_step(gradient, *states)
-    new_first_ref[...] = new_first[:lines]
-    new_second_ref[...] = new_second[:lines]
-    stepped_ref[...] = stepped[:lines]
-    both_ref[...] = stepped
+    columns, width = rows_ref.shape
+    gradient = (partial_ref[...] + partner_ref[...].astype(jnp.float32)) / devices
+    new_first_ref[...], new_second_ref[...], stepped_ref[...] = adam_step(
+        gradient, master_ref[...], first_ref[...], second_ref[...]
+    )
     period = columns // 8
     span = period * LANES
     group = span // columns
-    groups = halves * lines // period
-    wide = [both_ref[pl.ds(b, groups, stride=period), :].astype(jnp.bfloat16) for b in range(period)]
+    groups = stepped_ref.shape[0] // period
+    wide = [stepped_ref[pl.ds(b, groups, stride=period), :].astype(jnp.bfloat16) for b in range(period)]
     wide = jnp.concatenate(wide, axis=1)
-    line = lax.broadcasted_iota(jnp.int32, (groups, halves * width), 0)
-    row = lax.broadcasted_iota(jnp.int32, (groups, halves * width), 1)
+    line = lax.broadcasted_iota(jnp.int32, (groups, width), 0)
+    row = lax.broadcasted_iota(jnp.int32, (groups, width), 1)
     repeat = (row // group == line).astype(jnp.bfloat16)
     spread = lax.dot_general(wide, repeat, (((0,), (0,)), ((), ())), preferred_element_type=jnp.float32)
-    entry = lax.broadcasted_iota(jnp.int32, (span, halves * width), 0)
-    row = lax.broadcasted_iota(jnp.int32, (span, halves * width), 1)
+    entry = lax.broadcasted_iota(jnp.int32, (span, width), 0)
+    row = lax.broadcasted_iota(jnp.int32, (span, width), 1)
     kept = jnp.where(entry // columns == row % group, spread, 0.0).astype(jnp.bfloat16)
     column = lax.broadcasted_iota(jnp.int32, (columns, span), 1) % columns
     pick = (column == down_column(position_ref)).astype(jnp.bfloat16)
-    rows = jnp.dot(pick, kept, preferred_element_type=jnp.float32).astype(jnp.bfloat16)
-    for k in range(copies):
-        copies_ref[k, half] = rows[:, :width]
-        copies_ref[k, 1 - half] = rows[:, width:]
-
-
-def middle(position, partial, partner, mine, theirs, near, devices):
+    rows_ref[...] = jnp.dot(pick, kept, preferred_element_type=jnp.float32).astype(jnp.bfloat16)
+
+
+def middle(position, partial, partner, states, devices):
     columns = position.shape[1]
-    halves, lines, lanes = partial.shape
-    flat = jax.ShapeDtypeStruct((lines, lanes), jnp.float32)
-    rows = (near, halves, columns, flat.size // columns)
+    flat = jax.ShapeDtypeStruct(partial.shape, jnp.float32)
+    rows = jax.ShapeDtypeStruct((columns, flat.size // columns), jnp.bfloat16)
     return pl.pallas_call(
         functools.partial(middle_kernel, devices),
-        out_shape=(flat, flat, flat, jax.ShapeDtypeStruct(rows, jnp.bfloat16)),
-        scratch_shapes=[pltpu.VMEM((halves * lines, lanes), jnp.float32)],
-        compiler_params=small(),
-    )(position, partial, partner, mine, theirs)
+        out_shape=(flat, flat, flat, rows),
+        compiler_params=small(),
+    )(position, partial, partner, *states)
+
+
+def copies_kernel(mine_ref, theirs_ref, copies_ref):
+    half = lax.axis_index("half")
+    for k in range(copies_ref.shape[0]):
+        copies_ref[k, half] = mine_ref[...]
+        copies_ref[k, 1 - half] = theirs_ref[...]
+
+
+def both_halves(mine, theirs, near):
+    return pl.pallas_call(
+        copies_kernel,
+        out_shape=jax.ShapeDtypeStruct((near, 2, *mine.shape), mine.dtype),
+        compiler_params=small(),
+    )(mine, theirs)
 
 
 def finish_kernel(
@@ -237,13 +244,13 @@
     halves, near, cores = (lax.axis_size(axis) for axis in HALVES)
     swap = [(0, 1), (1, 0)]
     kept, sent = pack(grads, halves, near, master.shape[0] // LANES)
-    mine = jnp.stack([x.reshape(-1, LANES) for x in (master, first_moment, second_moment)])
     taken = lax.ppermute(sent, "core", swap)
-    theirs = lax.ppermute(mine, "half", swap)
-    pairs, position = add_pairs(kept, taken, flat_positions(owners))
-    partial = add_pieces(lax.all_to_all(pairs, "near", 0, 0, tiled=True))
-    partner = lax.ppermute(partial, "half", swap)
-    *updated, copies = middle(position, partial, partner, mine, theirs, near, halves * near * cores)
+    states = (master, first_moment, second_moment)
+    position, *states, pairs = add_pairs(kept, taken, flat_positions(owners), states)
+    kept, sent = add_pieces(lax.all_to_all(pairs, "near", 0, 0, tiled=True))
+    taken = lax.ppermute(sent, "half", swap)
+    *updated, rows = middle(position, kept, taken, states, halves * near * cores)
+    copies = both_halves(rows, lax.ppermute(rows, "half", swap), near)
     own = lax.all_to_all(copies, "near", 0, 0, tiled=True)
     other = lax.ppermute(own, "core", swap)
     *flat, model_copy = finish(position, *updated, own, other)

time: 35.2 us -> 37 us (1.051)
  blocking collectives: 8.76 us -> 21 us
  starting transfers between devices: 11.3 us -> 5.79 us
  waiting for transfers between devices: 10.2 us -> 6.21 us
  Pallas kernels: 2.36 us -> 1.61 us
    all_to_all x0 -> x1, blocking collectives: none -> 12.3 us  [on_halves(): kept, sent = add_pieces(lax.all_to_all(pairs, 'near', 0, 0, tiled=True))]
    all_to_all x1 -> x0, starting transfers between devices: 6.23 us -> none  [on_halves(): partial = add_pieces(lax.all_to_all(pairs, 'near', 0, 0, tiled=True))]
    all_to_all x1 -> x0, waiting for transfers between devices: 5.15 us -> none  [on_halves(): partial = add_pieces(lax.all_to_all(pairs, 'near', 0, 0, tiled=True))]
    ppermute x2, waiting for transfers between devices: 2.89 us -> 4.01 us  [the longest x1 2 us: on_halves(): taken = lax.ppermute(sent, 'half', swap)]
    ppermute x2, starting transfers between devices: 4.56 us -> 5.26 us  [the longest x1 2.65 us: on_halves(): taken = lax.ppermute(sent, 'half', swap)]
    pallas_call x2 -> x3, Pallas kernels: 0.75 us -> 0.1 us  [the longest x1 0.05 us: add_pairs(): pl.pallas_call(pair_kernel, out_shape=(*small_shapes, jax.ShapeDtypeStruc...]
  transfers between devices with their start and end apart: 5 -> 4, of which waited for: 4 -> 4; matrix products, arithmetic and copies ran while one was open for 1% -> 0% of each run, Pallas kernels for 0% -> 0%
where the time goes in v7:
time: 37 us; the launch traced here: 36.7 us
  blocking collectives  21 us (57%)
  waiting for transfers between devices  6.21 us (17%)
  starting transfers between devices  5.79 us (16%)
  Pallas kernels  1.61 us (4%)
  local copies, waits for them, and re-layouts  1.26 us (3%)
  between operations  0.67 us (2%)
    all_to_all x1, blocking collectives, on_halves(): kept, sent = add_pieces(lax.all_to_all(pairs, 'near', 0, 0, tiled=True))  12.3 us
    all_to_all x1, blocking collectives, on_halves(): own = lax.all_to_all(copies, 'near', 0, 0, tiled=True)  8.76 us
    ppermute x1, starting transfers between devices, on_halves(): taken = lax.ppermute(sent, 'half', swap)  2.65 us
    ppermute x1, starting transfers between devices, on_halves(): copies = both_halves(rows, lax.ppermute(rows, 'half', swap), near)  2.6 us
    ppermute x1, waiting for transfers between devices, on_halves(): taken = lax.ppermute(sent, 'half', swap)  2 us
    ppermute x1, waiting for transfers between devices, on_halves(): copies = both_halves(rows, lax.ppermute(rows, 'half', swap), near)  2 us
    ppermute x1, waiting for transfers between devices, on_halves(): other = lax.ppermute(own, 'core', swap)  1.44 us
    unnamed x10, local copies, waits for them, and re-layouts  1.26 us
  transfers between devices with their start and end apart: 4, of which 4 were waited for; matrix products, arithmetic and copies ran while one was open for 0% of the time, Pallas kernels for 0%

profile of v7, /device:TPU:0, one launch (start us, length us, event | category | flops | bytes accessed | tf_op | source)
XLA Modules:
  0.0 36.7 jit_solution(2058128845634793882)
XLA Ops:
  0.6 0.0 copy-start
  0.6 1.1 %copy-done = bf16[1,196608]{1,0:T(2,128)(2,1)S(1)} copy-done((bf16[1,196608]{1,0:T(2,128)(2,1)S(1)}, bf16[1,196608]{1,0:T(2,128)(2,1)}, u32[]{:S(2)}) %copy-start) | copy-done | bytes 393240
  1.8 0.0 copy-start.1
  1.8 0.0 copy-start.2
  1.8 0.0 copy-start.3
  1.8 0.2 shard_map.84
  2.0 0.0 copy-start.4
  2.0 0.5 %collective-permute-start = (bf16[8,2,48,128]{3,2,1,0:T(8,128)(2,1)S(1)}, bf16[8,2,48,128]{3,2,1,0:T(8,128)(2,1)S(1)}, u32[]{:S(2)}, u32[]{:S(2)}) collective-permute-start(bf16[8,2,48,128]{3,2,1,0:T(8,128)(2,1)S(1)} %get-tuple-element.22), channel_id=1, source_target_pairs={{0,1},{1,0},{2,3},{3,2},{4,5},{5,4},{6,7},{7,6},{8,9},{9,8},{10,11... | collective-permute-start | bytes 589832 | tf_op jit(solution)/shard_map/ppermute | solution.py:247
  2.5 0.1 copy-done.4
  2.6 0.2 convert_reduce_fusion
  2.8 0.8 %collective-permute-done.taken_ref = bf16[8,2,48,128]{3,2,1,0:T(8,128)(2,1)S(1)} collective-permute-done((bf16[8,2,48,128]{3,2,1,0:T(8,128)(2,1)S(1)}, bf16[8,2,48,128]{3,2,1,0:T(8,128)(2,1)S(1)}, u32[]{:S(2)}, u32[]{:S(2)}) %collective-permute-start) | collective-permute-done | bytes 196640 | tf_op jit(solution)/shard_map/ppermute | solution.py:247
  3.6 0.0 copy-done.1
  3.6 0.0 copy-done.2
  3.6 0.0 copy-done.3
  3.6 12.3 %all_to_all.10.pieces_ref = bf16[8,2,48,128]{3,2,1,0:T(8,128)(2,1)S(1)} all-to-all(bf16[8,2,48,128]{3,2,1,0:T(8,128)(2,1)S(1)} %get-tuple-element.24), channel_id=1, replica_groups=mesh['half'=2,'near'=8,'core'=2] {'near'}, dimensions={0} | all-to-all | bytes 393216 | tf_op jit(solution)/shard_map/all_to_all | solution.py:250
  15.9 2.7 %collective-permute-start.1 = (bf16[48,128]{1,0:T(8,128)(2,1)S(1)}, bf16[48,128]{1,0:T(8,128)(2,1)S(1)}, u32[]{:S(2)}, u32[]{:S(2)}) collective-permute-start(bf16[48,128]{1,0:T(8,128)(2,1)S(1)} %get-tuple-element.26), channel_id=1, source_target_pairs={{0,16},{16,0},{1,17},{17,1},{2,18},{18,2},{3,19},{19,3},{4,20},{20... | collective-permute-start | bytes 36872 | tf_op jit(solution)/shard_map/ppermute | solution.py:251
  18.6 2.0 %collective-permute-done.1.partner_ref = bf16[48,128]{1,0:T(8,128)(2,1)S(1)} collective-permute-done((bf16[48,128]{1,0:T(8,128)(2,1)S(1)}, bf16[48,128]{1,0:T(8,128)(2,1)S(1)}, u32[]{:S(2)}, u32[]{:S(2)}) %collective-permute-start.1) | collective-permute-done | bytes 12320 | tf_op jit(solution)/shard_map/ppermute | solution.py:251
  20.6 0.4 %shard_map.87 = (f32[48,128]{1,0:T(8,128)S(1)}, f32[48,128]{1,0:T(8,128)S(1)}, f32[48,128]{1,0:T(8,128)S(1)}, bf16[24,256]{1,0:T(8,128)(2,1)S(1)}) custom-call(s32[1,24]{1,0:T(1,128)S(1)} %get-tuple-element.23.position_ref, f32[48,128]{1,0:T(8,128)S(1)} %get-tuple-element.25.partial_ref, bf16[48,128]{1,0:T(8,128)(2,1)S(1)} %collective-permute-done.1.partner_ref, ...), custom_call_target="tpu_custom_call" | custom-call | tf_op jit(solution)/shard_map/pallas_call | solution.py:141
  21.0 2.6 %collective-permute-start.2 = (bf16[24,256]{1,0:T(8,128)(2,1)S(1)}, bf16[24,256]{1,0:T(8,128)(2,1)S(1)}, u32[]{:S(2)}, u32[]{:S(2)}) collective-permute-start(bf16[24,256]{1,0:T(8,128)(2,1)S(1)} %get-tuple-element.33.mine_ref), channel_id=1, source_target_pairs={{0,16},{16,0},{1,17},{17,1},{2,18},{18,2},{3,19},{19,3},{4,20},{20... | collective-permute-start | bytes 36872 | tf_op jit(solution)/shard_map/ppermute | solution.py:253
  23.6 2.0 %collective-permute-done.2.theirs_ref = bf16[24,256]{1,0:T(8,128)(2,1)S(1)} collective-permute-done((bf16[24,256]{1,0:T(8,128)(2,1)S(1)}, bf16[24,256]{1,0:T(8,128)(2,1)S(1)}, u32[]{:S(2)}, u32[]{:S(2)}) %collective-permute-start.2) | collective-permute-done | bytes 12320 | tf_op jit(solution)/shard_map/ppermute | solution.py:253
  25.6 8.8 %all_to_all.11.own_ref = bf16[8,2,24,256]{3,2,1,0:T(8,128)(2,1)S(1)} all-to-all(bf16[8,2,24,256]{3,2,1,0:T(8,128)(2,1)S(1)} %shard_map.88), channel_id=1, replica_groups=mesh['half'=2,'near'=8,'core'=2] {'near'}, dimensions={0} | all-to-all | bytes 393216 | tf_op jit(solution)/shard_map/all_to_all | solution.py:254
  34.4 0.0 collective-permute-start.3
  34.4 1.4 %collective-permute-done.3.other_ref = bf16[8,2,24,256]{3,2,1,0:T(8,128)(2,1)S(1)} collective-permute-done((bf16[8,2,24,256]{3,2,1,0:T(8,128)(2,1)S(1)}, bf16[8,2,24,256]{3,2,1,0:T(8,128)(2,1)S(1)}, u32[]{:S(2)}, u32[]{:S(2)}) %collective-permute-start.3) | collective-permute-done | bytes 196640 | tf_op jit(solution)/shard_map/ppermute | solution.py:255
  35.8 0.9 %shard_map.89 = (f32[48,128]{1,0:T(8,128)}, f32[48,128]{1,0:T(8,128)}, f32[48,128]{1,0:T(8,128)}, bf16[24,8192]{1,0:T(8,128)(2,1)}) custom-call(s32[1,24]{1,0:T(1,128)S(1)} %get-tuple-element.23.position_ref, f32[48,128]{1,0:T(8,128)S(1)} %get-tuple-element.30.new_first_ref, f32[48,128]{1,0:T(8,128)S(1)} %get-tuple-element.31.new_second_ref, ...), custom_call_target="tpu_custom_call" | custom-call | tf_op jit(solution)/shard_map/pallas_call | solution.py:215
  (3 shorter events, 0.1 us)
Async XLA Ops:
  0.6 1.1 %copy-start = (bf16[1,196608]{1,0:T(2,128)(2,1)S(1)}, bf16[1,196608]{1,0:T(2,128)(2,1)}, u32[]{:S(2)}) copy-start(bf16[1,196608]{1,0:T(2,128)(2,1)} %grads_ref.1) | copy-start | bytes 1179652
  1.8 1.8 %copy-start.1 = (f32[6144]{0:T(1024)S(1)}, f32[6144]{0:T(1024)}, u32[]{:S(2)}) copy-start(f32[6144]{0:T(1024)} %param.6) | copy-start | bytes 73732
  1.8 1.8 %copy-start.2 = (f32[6144]{0:T(1024)S(1)}, f32[6144]{0:T(1024)}, u32[]{:S(2)}) copy-start(f32[6144]{0:T(1024)} %param.7) | copy-start | bytes 73732
  1.8 1.8 %copy-start.3 = (f32[6144]{0:T(1024)S(1)}, f32[6144]{0:T(1024)}, u32[]{:S(2)}) copy-start(f32[6144]{0:T(1024)} %param.8) | copy-start | bytes 73732
  2.0 0.7 %copy-start.4 = (s32[24]{0:T(128)S(1)}, s32[24]{0:T(128)}, u32[]{:S(2)}) copy-start(s32[24]{0:T(128)} %param.9) | copy-start | bytes 292
  2.0 1.6 %collective-permute-start = (bf16[8,2,48,128]{3,2,1,0:T(8,128)(2,1)S(1)}, bf16[8,2,48,128]{3,2,1,0:T(8,128)(2,1)S(1)}, u32[]{:S(2)}, u32[]{:S(2)}) collective-permute-start(bf16[8,2,48,128]{3,2,1,0:T(8,128)(2,1)S(1)} %get-tuple-element.22), channel_id=1, source_target_pairs={{0,1},{1,0},{2,3},{3,2},{4,5},{5,4},{6,7},{7,6},{8,9},{9,8},{10,11... | collective-permute-start | bytes 589832 | tf_op jit(solution)/shard_map/ppermute | solution.py:247
  15.9 4.7 %collective-permute-start.1 = (bf16[48,128]{1,0:T(8,128)(2,1)S(1)}, bf16[48,128]{1,0:T(8,128)(2,1)S(1)}, u32[]{:S(2)}, u32[]{:S(2)}) collective-permute-start(bf16[48,128]{1,0:T(8,128)(2,1)S(1)} %get-tuple-element.26), channel_id=1, source_target_pairs={{0,16},{16,0},{1,17},{17,1},{2,18},{18,2},{3,19},{19,3},{4,20},{20... | collective-permute-start | bytes 36872 | tf_op jit(solution)/shard_map/ppermute | solution.py:251
  21.0 4.6 %collective-permute-start.2 = (bf16[24,256]{1,0:T(8,128)(2,1)S(1)}, bf16[24,256]{1,0:T(8,128)(2,1)S(1)}, u32[]{:S(2)}, u32[]{:S(2)}) collective-permute-start(bf16[24,256]{1,0:T(8,128)(2,1)S(1)} %get-tuple-element.33.mine_ref), channel_id=1, source_target_pairs={{0,16},{16,0},{1,17},{17,1},{2,18},{18,2},{3,19},{19,3},{4,20},{20... | collective-permute-start | bytes 36872 | tf_op jit(solution)/shard_map/ppermute | solution.py:253
  34.4 1.4 %collective-permute-start.3 = (bf16[8,2,24,256]{3,2,1,0:T(8,128)(2,1)S(1)}, bf16[8,2,24,256]{3,2,1,0:T(8,128)(2,1)S(1)}, u32[]{:S(2)}, u32[]{:S(2)}) collective-permute-start(bf16[8,2,24,256]{3,2,1,0:T(8,128)(2,1)S(1)} %all_to_all.11.own_ref), channel_id=1, source_target_pairs={{0,1},{1,0},{2,3},{3,2},{4,5},{5,4},{6,7},{7,6},{8,9},{9,8},{10,11... | collective-permute-start | bytes 589832 | tf_op jit(solution)/shard_map/ppermute | solution.py:255

commit v8 on v5

--- a/solution.py
+++ b/solution.py
@@ -39,25 +39,36 @@
     return pltpu.CompilerParams(vmem_limit_bytes=6 * 2**20, **more)
 
 
-def pack_kernel(grads_ref, kept_ref, sent_ref, wide_ref):
-    chips, lines, lanes = kept_ref.shape
+def pack_kernel(kept, grads_ref, packed_ref, long_ref, wide_ref, sems):
+    chips, lines, lanes = packed_ref.shape
     core = lax.axis_index("replica")
-    row_ref = wide_ref.reshape(1, wide_ref.shape[0] * lanes)
-    width = 2 * lines * lanes
+    place = core if kept else 1 - core
+    width = lines * lanes
+    copies = []
     for k in range(chips):
-        row_ref[:, k * width : (k + 1) * width] = grads_ref[:, k * width : (k + 1) * width].astype(jnp.float32)
-        for ref, place in ((kept_ref, core), (sent_ref, 1 - core)):
-            start = pl.multiple_of((2 * k + place) * lines, lines)
-            ref[k] = wide_ref[pl.ds(start, lines), :].astype(jnp.bfloat16)
-
-
-def pack(grads, chips, lines):
-    packed = jax.ShapeDtypeStruct((chips, lines, LANES), jnp.bfloat16)
-    return pl.pallas_call(
-        pack_kernel,
-        out_shape=(packed, packed),
-        scratch_shapes=[pltpu.VMEM((grads.shape[1] // LANES, LANES), jnp.float32)],
-        compiler_params=small(),
+        start = pl.multiple_of((2 * k + place) * width, width)
+        source = grads_ref.at[:, pl.ds(start, width)]
+        copies.append(pltpu.make_async_copy(source, long_ref.at[k], sems.at[k]))
+        copies[k].start()
+    row_ref = wide_ref.reshape(1, chips * width)
+    for k in range(chips):
+        copies[k].wait()
+        row_ref[:, k * width : (k + 1) * width] = long_ref[k].astype(jnp.float32)
+        packed_ref[k] = wide_ref[k * lines : (k + 1) * lines].astype(jnp.bfloat16)
+
+
+def pack(kept, grads, chips, lines):
+    return pl.pallas_call(
+        functools.partial(pack_kernel, kept),
+        in_specs=[pl.BlockSpec(memory_space=pl.ANY)],
+        out_shape=jax.ShapeDtypeStruct((chips, lines, LANES), jnp.bfloat16),
+        scratch_shapes=[
+            pltpu.VMEM((chips, 1, lines * LANES), jnp.bfloat16),
+            pltpu.VMEM((chips * lines, LANES), jnp.float32),
+            pltpu.SemaphoreType.DMA((chips,)),
+        ],
+        compiler_params=pltpu.CompilerParams(vmem_limit_bytes=54736 * 2**10),
+        cost_estimate=pl.CostEstimate(flops=0, bytes_accessed=2 * grads.size, transcendentals=0),
     )(grads)
 
 
@@ -213,8 +224,9 @@
     devices = shards * replicas
     columns = owners.shape[0]
     if replicas == 2 and master.shape[0] // LANES % 48 == 0:
-        kept, sent = pack(grads, shards, master.shape[0] // LANES)
-        taken = lax.ppermute(sent, "replica", [(0, 1), (1, 0)])
+        lines = master.shape[0] // LANES
+        taken = lax.ppermute(pack(False, grads, shards, lines), "replica", [(0, 1), (1, 0)])
+        kept = pack(True, grads, shards, lines)
         states = (master, first_moment, second_moment)
         position, *states, pairs = add_pairs(kept, taken, flat_positions(owners), states)
         pieces = lax.all_to_all(pairs, "shard", 0, 0, tiled=True)

time: 35 us -> 35.1 us (level)
  Pallas kernels: 1.6 us -> 3.6 us
  local copies, waits for them, and re-layouts: 1.26 us -> 0.02 us
  waiting for transfers between devices: 2.21 us -> 1.44 us
    pallas_call x1 -> x2, Pallas kernels: 0.18 us -> 2.18 us  [pack(): pl.pallas_call(functools.partial(pack_kernel, kept), in_specs=[pl.BlockSp...]
    unnamed x10 -> x8, local copies, waits for them, and re-layouts: 1.26 us -> 0.02 us
    ppermute x1, waiting for transfers between devices: 0.77 us -> 0.01 us  [on_device(): lax.ppermute(pack(False, grads, shards, lines), 'replica', [(0, 1), (1, 0)])]
  transfers between devices with their start and end apart: 2 -> 2, of which waited for: 2 -> 1; matrix products, arithmetic and copies ran while one was open for 1% -> 1% of each run, Pallas kernels for 0% -> 3%
where the time goes in v8:
time: 35.1 us; the launch traced here: 34.7 us
  blocking collectives  28.3 us (81%)
  Pallas kernels  3.6 us (10%)
  waiting for transfers between devices  1.44 us (4%)
  between operations  0.71 us (2%)
  starting transfers between devices  0.52 us (1%)
    all_to_all x1, blocking collectives, on_device(): pieces = lax.all_to_all(pairs, 'shard', 0, 0, tiled=True)  17 us
    all_to_all x1, blocking collectives, on_device(): own = lax.all_to_all(copies, 'shard', 0, 0, tiled=True)  11.3 us
    pallas_call x2, Pallas kernels, pack(): pl.pallas_call(functools.partial(pack_kernel, kept), in_specs=[pl.BlockSp...  2.18 us
    ppermute x1, waiting for transfers between devices, on_device(): other = lax.ppermute(own, 'replica', [(0, 1), (1, 0)])  1.44 us
    pallas_call x1, Pallas kernels, finish(): pl.pallas_call(finish_kernel, in_specs=[pl.BlockSpec(memory_space=pltpu.V...  0.93 us
  transfers between devices with their start and end apart: 2, of which 1 were waited for; matrix products, arithmetic and copies ran while one was open for 1% of the time, Pallas kernels for 3%

profile of v8, /device:TPU:0, one launch (start us, length us, event | category | flops | bytes accessed | tf_op | source)
XLA Modules:
  0.0 34.7 jit_solution(12091700891513651528)
XLA Ops:
  0.6 1.1 %shard_map.85 = bf16[16,48,128]{2,1,0:T(8,128)(2,1)S(1)} custom-call(bf16[1,196608]{1,0:T(2,128)(2,1)} %grads_ref.3), custom_call_target="tpu_custom_call" | custom-call | bytes 393216 | tf_op jit(solution)/shard_map/pallas_call | solution.py:61
  1.7 0.0 copy-start.3
  1.8 0.5 %collective-permute-start = (bf16[16,48,128]{2,1,0:T(8,128)(2,1)S(1)}, bf16[16,48,128]{2,1,0:T(8,128)(2,1)S(1)}, u32[]{:S(2)}, u32[]{:S(2)}) collective-permute-start(bf16[16,48,128]{2,1,0:T(8,128)(2,1)S(1)} %shard_map.85), channel_id=1, source_target_pairs={{0,1},{1,0},{2,3},{3,2},{4,5},{5,4},{6,7},{7,6},{8,9},{9,8},{10,11... | collective-permute-start | bytes 589832 | tf_op jit(solution)/shard_map/ppermute | solution.py:228
  2.3 0.0 copy-start
  2.3 0.0 copy-start.1
  2.3 0.0 copy-start.2
  2.3 1.1 %shard_map.84.kept_ref = bf16[16,48,128]{2,1,0:T(8,128)(2,1)S(1)} custom-call(bf16[1,196608]{1,0:T(2,128)(2,1)} %grads_ref.3), custom_call_target="tpu_custom_call" | custom-call | bytes 393216 | tf_op jit(solution)/shard_map/pallas_call | solution.py:61
  3.4 0.0 copy-done.3
  3.4 0.2 convert_reduce_fusion
  3.5 0.0 collective-permute-done.taken_ref
  3.6 0.0 copy-done
  3.6 0.0 copy-done.1
  3.6 0.0 copy-done.2
  3.6 0.1 shard_map.86
  3.6 17.0 %all_to_all.10.pieces_ref = bf16[16,48,128]{2,1,0:T(8,128)(2,1)S(1)} all-to-all(bf16[16,48,128]{2,1,0:T(8,128)(2,1)S(1)} %get-tuple-element.18), channel_id=1, replica_groups=mesh['shard'=16,'replica'=2] {'shard'}, dimensions={0} | all-to-all | bytes 393216 | tf_op jit(solution)/shard_map/all_to_all | solution.py:232
  20.6 0.4 %shard_map.87 = (f32[48,128]{1,0:T(8,128)S(1)}, f32[48,128]{1,0:T(8,128)S(1)}, f32[48,128]{1,0:T(8,128)S(1)}, bf16[16,24,256]{2,1,0:T(8,128)(2,1)S(1)}) custom-call(s32[1,24]{1,0:T(1,128)S(1)} %get-tuple-element.17.position_ref, bf16[16,48,128]{2,1,0:T(8,128)(2,1)S(1)} %all_to_all.10.pieces_ref, f32[48,128]{1,0:T(8,128)S(1)} %get-tuple-element.19.master_ref, ...), custom_call_target="tpu_custom_call" | custom-call | tf_op jit(solution)/shard_map/pallas_call | solution.py:138
  21.1 11.3 %all_to_all.11.own_ref = bf16[16,24,256]{2,1,0:T(8,128)(2,1)S(1)} all-to-all(bf16[16,24,256]{2,1,0:T(8,128)(2,1)S(1)} %get-tuple-element.25), channel_id=1, replica_groups=mesh['shard'=16,'replica'=2] {'shard'}, dimensions={0} | all-to-all | bytes 393216 | tf_op jit(solution)/shard_map/all_to_all | solution.py:234
  32.4 0.0 collective-permute-start.1
  32.4 1.4 %collective-permute-done.1.other_ref = bf16[16,24,256]{2,1,0:T(8,128)(2,1)S(1)} collective-permute-done((bf16[16,24,256]{2,1,0:T(8,128)(2,1)S(1)}, bf16[16,24,256]{2,1,0:T(8,128)(2,1)S(1)}, u32[]{:S(2)}, u32[]{:S(2)}) %collective-permute-start.1) | collective-permute-done | bytes 196640 | tf_op jit(solution)/shard_map/ppermute | solution.py:235
  33.8 0.9 %shard_map.88 = (f32[48,128]{1,0:T(8,128)}, f32[48,128]{1,0:T(8,128)}, f32[48,128]{1,0:T(8,128)}, bf16[24,8192]{1,0:T(8,128)(2,1)}) custom-call(s32[1,24]{1,0:T(1,128)S(1)} %get-tuple-element.17.position_ref, f32[48,128]{1,0:T(8,128)S(1)} %get-tuple-element.22.new_first_ref, f32[48,128]{1,0:T(8,128)S(1)} %get-tuple-element.23.new_second_ref, ...), custom_call_target="tpu_custom_call" | custom-call | tf_op jit(solution)/shard_map/pallas_call | solution.py:194
Async XLA Ops:
  1.7 1.6 %copy-start.3 = (s32[24]{0:T(128)S(1)}, s32[24]{0:T(128)}, u32[]{:S(2)}) copy-start(s32[24]{0:T(128)} %param.9) | copy-start | bytes 292
  1.8 1.8 %collective-permute-start = (bf16[16,48,128]{2,1,0:T(8,128)(2,1)S(1)}, bf16[16,48,128]{2,1,0:T(8,128)(2,1)S(1)}, u32[]{:S(2)}, u32[]{:S(2)}) collective-permute-start(bf16[16,48,128]{2,1,0:T(8,128)(2,1)S(1)} %shard_map.85), channel_id=1, source_target_pairs={{0,1},{1,0},{2,3},{3,2},{4,5},{5,4},{6,7},{7,6},{8,9},{9,8},{10,11... | collective-permute-start | bytes 589832 | tf_op jit(solution)/shard_map/ppermute | solution.py:228
  2.3 1.3 %copy-start = (f32[6144]{0:T(1024)S(1)}, f32[6144]{0:T(1024)}, u32[]{:S(2)}) copy-start(f32[6144]{0:T(1024)} %param.6) | copy-start | bytes 73732
  2.3 1.3 %copy-start.1 = (f32[6144]{0:T(1024)S(1)}, f32[6144]{0:T(1024)}, u32[]{:S(2)}) copy-start(f32[6144]{0:T(1024)} %param.7) | copy-start | bytes 73732
  2.3 1.3 %copy-start.2 = (f32[6144]{0:T(1024)S(1)}, f32[6144]{0:T(1024)}, u32[]{:S(2)}) copy-start(f32[6144]{0:T(1024)} %param.8) | copy-start | bytes 73732
  32.4 1.4 %collective-permute-start.1 = (bf16[16,24,256]{2,1,0:T(8,128)(2,1)S(1)}, bf16[16,24,256]{2,1,0:T(8,128)(2,1)S(1)}, u32[]{:S(2)}, u32[]{:S(2)}) collective-permute-start(bf16[16,24,256]{2,1,0:T(8,128)(2,1)S(1)} %all_to_all.11.own_ref), channel_id=1, source_target_pairs={{0,1},{1,0},{2,3},{3,2},{4,5},{5,4},{6,7},{7,6},{8,9},{9,8},{10,11... | collective-permute-start | bytes 589832 | tf_op jit(solution)/shard_map/ppermute | solution.py:235

commit v9 on v5

--- a/solution.py
+++ b/solution.py
@@ -16,6 +16,8 @@
 first_correction = 1.0 - 0.9**20
 second_correction = 1.0 - 0.95**20
 AXES = ("shard", "replica")
+LAYERS = ("layer", "plane", "core")
+PLANE = 4
 LANES = 128
 
 
@@ -39,16 +41,20 @@
     return pltpu.CompilerParams(vmem_limit_bytes=6 * 2**20, **more)
 
 
+def slot(chip, chips):
+    return chip % PLANE * (chips // PLANE) + chip // PLANE
+
+
 def pack_kernel(grads_ref, kept_ref, sent_ref, wide_ref):
     chips, lines, lanes = kept_ref.shape
-    core = lax.axis_index("replica")
+    core = lax.axis_index("core")
     row_ref = wide_ref.reshape(1, wide_ref.shape[0] * lanes)
     width = 2 * lines * lanes
     for k in range(chips):
         row_ref[:, k * width : (k + 1) * width] = grads_ref[:, k * width : (k + 1) * width].astype(jnp.float32)
         for ref, place in ((kept_ref, core), (sent_ref, 1 - core)):
             start = pl.multiple_of((2 * k + place) * lines, lines)
-            ref[k] = wide_ref[pl.ds(start, lines), :].astype(jnp.bfloat16)
+            ref[slot(k, chips)] = wide_ref[pl.ds(start, lines), :].astype(jnp.bfloat16)
 
 
 def pack(grads, chips, lines):
@@ -135,7 +141,7 @@
     position_ref, new_first_ref, new_second_ref, stepped_ref, own_ref, other_ref,
     master_out, first_out, second_out, copy_out, master_ref, scaled_ref, sems,
 ):
-    core = lax.axis_index("replica")
+    core = lax.axis_index("core")
     chips, columns, width = own_ref.shape
     parts = sems.shape[0] - 3
     copies = [
@@ -167,7 +173,7 @@
         for k in range(p * each, (p + 1) * each):
             for ref, place in ((own_ref, core), (other_ref, 1 - core)):
                 start = pl.multiple_of((2 * k + place) * width, width)
-                scaled_ref[:, pl.ds(start, width)] = (ref[k].astype(jnp.float32) * factor).astype(jnp.bfloat16)
+                scaled_ref[:, pl.ds(start, width)] = (ref[slot(k, chips)].astype(jnp.float32) * factor).astype(jnp.bfloat16)
         part = pl.ds(p * 2 * each * width, 2 * each * width)
         copies.append(pltpu.make_async_copy(scaled_ref.at[:, part], copy_out.at[:, part], sems.at[3 + p]))
         copies[3 + p].start()
@@ -208,21 +214,24 @@
     return lax.all_to_all(jnp.broadcast_to(value[None], (size,) + value.shape), axes, 0, 0, tiled=True)
 
 
+def on_layers(grads, master, first_moment, second_moment, owners):
+    chips = lax.axis_size(("layer", "plane"))
+    swap = [(0, 1), (1, 0)]
+    kept, sent = pack(grads, chips, master.shape[0] // LANES)
+    taken = lax.ppermute(sent, "core", swap)
+    states = (master, first_moment, second_moment)
+    position, *states, pairs = add_pairs(kept, taken, flat_positions(owners), states)
+    pieces = lax.all_to_all(pairs, ("plane", "layer"), 0, 0, tiled=True)
+    *updated, copies = middle(position, pieces, states, 2 * chips)
+    own = lax.all_to_all(copies, ("plane", "layer"), 0, 0, tiled=True)
+    other = lax.ppermute(own, "core", swap)
+    *flat, model_copy = finish(position, *updated, own, other)
+    return (*(x.reshape(-1) for x in flat), model_copy)
+
+
 def on_device(grads, master, first_moment, second_moment, owners):
-    shards, replicas = lax.axis_size("shard"), lax.axis_size("replica")
-    devices = shards * replicas
+    devices = lax.axis_size(AXES)
     columns = owners.shape[0]
-    if replicas == 2 and master.shape[0] // LANES % 48 == 0:
-        kept, sent = pack(grads, shards, master.shape[0] // LANES)
-        taken = lax.ppermute(sent, "replica", [(0, 1), (1, 0)])
-        states = (master, first_moment, second_moment)
-        position, *states, pairs = add_pairs(kept, taken, flat_positions(owners), states)
-        pieces = lax.all_to_all(pairs, "shard", 0, 0, tiled=True)
-        *updated, copies = middle(position, pieces, states, devices)
-        own = lax.all_to_all(copies, "shard", 0, 0, tiled=True)
-        other = lax.ppermute(own, "replica", [(0, 1), (1, 0)])
-        *flat, model_copy = finish(position, *updated, own, other)
-        return (*(x.reshape(-1) for x in flat), model_copy)
     pieces = lax.all_to_all(grads.reshape(devices, -1), AXES, 0, 0, tiled=True)
     gradient = jnp.sum(pieces.astype(jnp.float32), axis=0) / devices
     new_first, new_second, stepped = adam_step(gradient, master, first_moment, second_moment)
@@ -232,11 +241,15 @@
 
 
 def solution(mesh):
-    placed = (P(AXES, None), P(AXES), P(AXES), P(AXES), P())
+    body, axes = on_device, AXES
+    if mesh.shape["replica"] == 2 and mesh.shape["shard"] % PLANE == 0:
+        body, axes = on_layers, LAYERS
+        mesh = jax.sharding.Mesh(mesh.devices.reshape(-1, PLANE, 2), LAYERS)
+    placed = (P(axes, None), P(axes), P(axes), P(axes), P())
     return jax.shard_map(
-        on_device,
+        body,
         mesh=mesh,
         in_specs=placed,
-        out_specs=(P(AXES), P(AXES), P(AXES), P()),
+        out_specs=(P(axes), P(axes), P(axes), P()),
         check_vma=False,
     )

time: 35 us -> 35.6 us (1.017)
  blocking collectives: 28.2 us -> 28.9 us
    all_to_all x2, blocking collectives: 28.2 us -> 28.9 us  [the longest x1 17.5 us: on_layers(): pieces = lax.all_to_all(pairs, ('plane', 'layer'), 0, 0, tiled=True)]
where the time goes in v9:
time: 35.6 us; the launch traced here: 35.3 us
  blocking collectives  28.9 us (81%)
  waiting for transfers between devices  2.21 us (6%)
  Pallas kernels  1.6 us (4%)
  local copies, waits for them, and re-layouts  1.26 us (4%)
  between operations  0.67 us (2%)
  starting transfers between devices  0.53 us (1%)
    all_to_all x1, blocking collectives, on_layers(): pieces = lax.all_to_all(pairs, ('plane', 'layer'), 0, 0, tiled=True)  17.5 us
    all_to_all x1, blocking collectives, on_layers(): own = lax.all_to_all(copies, ('plane', 'layer'), 0, 0, tiled=True)  11.4 us
    ppermute x1, waiting for transfers between devices, on_layers(): other = lax.ppermute(own, 'core', swap)  1.44 us
    unnamed x10, local copies, waits for them, and re-layouts  1.26 us
    pallas_call x1, Pallas kernels, finish(): pl.pallas_call(finish_kernel, in_specs=[pl.BlockSpec(memory_space=pltpu.V...  0.93 us
    ppermute x1, waiting for transfers between devices, on_layers(): taken = lax.ppermute(sent, 'core', swap)  0.77 us
  transfers between devices with their start and end apart: 2, of which 2 were waited for; matrix products, arithmetic and copies ran while one was open for 1% of the time, Pallas kernels for 0%

profile of v9, /device:TPU:0, one launch (start us, length us, event | category | flops | bytes accessed | tf_op | source)
XLA Modules:
  0.0 35.3 jit_solution(1814820914333792710)
XLA Ops:
  0.6 0.0 copy-start
  0.6 1.1 %copy-done = bf16[1,196608]{1,0:T(2,128)(2,1)S(1)} copy-done((bf16[1,196608]{1,0:T(2,128)(2,1)S(1)}, bf16[1,196608]{1,0:T(2,128)(2,1)}, u32[]{:S(2)}) %copy-start) | copy-done | bytes 393240
  1.8 0.0 copy-start.1
  1.8 0.0 copy-start.2
  1.8 0.0 copy-start.3
  1.8 0.2 shard_map.84
  2.0 0.0 copy-start.4
  2.0 0.5 %collective-permute-start = (bf16[16,48,128]{2,1,0:T(8,128)(2,1)S(1)}, bf16[16,48,128]{2,1,0:T(8,128)(2,1)S(1)}, u32[]{:S(2)}, u32[]{:S(2)}) collective-permute-start(bf16[16,48,128]{2,1,0:T(8,128)(2,1)S(1)} %get-tuple-element.20), channel_id=1, source_target_pairs={{0,1},{1,0},{2,3},{3,2},{4,5},{5,4},{6,7},{7,6},{8,9},{9,8},{10,11... | collective-permute-start | bytes 589832 | tf_op jit(solution)/shard_map/ppermute | solution.py:221
  2.5 0.1 copy-done.4
  2.6 0.2 convert_reduce_fusion
  2.8 0.8 %collective-permute-done.taken_ref = bf16[16,48,128]{2,1,0:T(8,128)(2,1)S(1)} collective-permute-done((bf16[16,48,128]{2,1,0:T(8,128)(2,1)S(1)}, bf16[16,48,128]{2,1,0:T(8,128)(2,1)S(1)}, u32[]{:S(2)}, u32[]{:S(2)}) %collective-permute-start) | collective-permute-done | bytes 196640 | tf_op jit(solution)/shard_map/ppermute | solution.py:221
  3.6 0.0 copy-done.1
  3.6 0.0 copy-done.2
  3.6 0.0 copy-done.3
  3.6 17.5 %all_to_all.10.pieces_ref = bf16[16,48,128]{2,1,0:T(8,128)(2,1)S(1)} all-to-all(bf16[16,48,128]{2,1,0:T(8,128)(2,1)S(1)} %get-tuple-element.22), channel_id=1, replica_groups=mesh['layer'=4,'plane'=4,'core'=2] {'plane','layer'}, dimensions={0} | all-to-all | bytes 393216 | tf_op jit(solution)/shard_map/all_to_all | solution.py:224
  21.1 0.4 %shard_map.86 = (f32[48,128]{1,0:T(8,128)S(1)}, f32[48,128]{1,0:T(8,128)S(1)}, f32[48,128]{1,0:T(8,128)S(1)}, bf16[16,24,256]{2,1,0:T(8,128)(2,1)S(1)}) custom-call(s32[1,24]{1,0:T(1,128)S(1)} %get-tuple-element.21.position_ref, bf16[16,48,128]{2,1,0:T(8,128)(2,1)S(1)} %all_to_all.10.pieces_ref, f32[48,128]{1,0:T(8,128)S(1)} %get-tuple-element.23.master_ref, ...), custom_call_target="tpu_custom_call" | custom-call | tf_op jit(solution)/shard_map/pallas_call | solution.py:133
  21.6 11.4 %all_to_all.11.own_ref = bf16[16,24,256]{2,1,0:T(8,128)(2,1)S(1)} all-to-all(bf16[16,24,256]{2,1,0:T(8,128)(2,1)S(1)} %get-tuple-element.29), channel_id=1, replica_groups=mesh['layer'=4,'plane'=4,'core'=2] {'plane','layer'}, dimensions={0} | all-to-all | bytes 393216 | tf_op jit(solution)/shard_map/all_to_all | solution.py:226
  32.9 0.0 collective-permute-start.1
  32.9 1.4 %collective-permute-done.1.other_ref = bf16[16,24,256]{2,1,0:T(8,128)(2,1)S(1)} collective-permute-done((bf16[16,24,256]{2,1,0:T(8,128)(2,1)S(1)}, bf16[16,24,256]{2,1,0:T(8,128)(2,1)S(1)}, u32[]{:S(2)}, u32[]{:S(2)}) %collective-permute-start.1) | collective-permute-done | bytes 196640 | tf_op jit(solution)/shard_map/ppermute | solution.py:227
  34.4 0.9 %shard_map.87 = (f32[48,128]{1,0:T(8,128)}, f32[48,128]{1,0:T(8,128)}, f32[48,128]{1,0:T(8,128)}, bf16[24,8192]{1,0:T(8,128)(2,1)}) custom-call(s32[1,24]{1,0:T(1,128)S(1)} %get-tuple-element.21.position_ref, f32[48,128]{1,0:T(8,128)S(1)} %get-tuple-element.26.new_first_ref, f32[48,128]{1,0:T(8,128)S(1)} %get-tuple-element.27.new_second_ref, ...), custom_call_target="tpu_custom_call" | custom-call | tf_op jit(solution)/shard_map/pallas_call | solution.py:189
  (1 shorter events, 0.0 us)
Async XLA Ops:
  0.6 1.1 %copy-start = (bf16[1,196608]{1,0:T(2,128)(2,1)S(1)}, bf16[1,196608]{1,0:T(2,128)(2,1)}, u32[]{:S(2)}) copy-start(bf16[1,196608]{1,0:T(2,128)(2,1)} %grads_ref.1) | copy-start | bytes 1179652
  1.8 1.8 %copy-start.1 = (f32[6144]{0:T(1024)S(1)}, f32[6144]{0:T(1024)}, u32[]{:S(2)}) copy-start(f32[6144]{0:T(1024)} %param.6) | copy-start | bytes 73732
  1.8 1.8 %copy-start.2 = (f32[6144]{0:T(1024)S(1)}, f32[6144]{0:T(1024)}, u32[]{:S(2)}) copy-start(f32[6144]{0:T(1024)} %param.7) | copy-start | bytes 73732
  1.8 1.8 %copy-start.3 = (f32[6144]{0:T(1024)S(1)}, f32[6144]{0:T(1024)}, u32[]{:S(2)}) copy-start(f32[6144]{0:T(1024)} %param.8) | copy-start | bytes 73732
  2.0 0.7 %copy-start.4 = (s32[24]{0:T(128)S(1)}, s32[24]{0:T(128)}, u32[]{:S(2)}) copy-start(s32[24]{0:T(128)} %param.9) | copy-start | bytes 292
  2.0 1.6 %collective-permute-start = (bf16[16,48,128]{2,1,0:T(8,128)(2,1)S(1)}, bf16[16,48,128]{2,1,0:T(8,128)(2,1)S(1)}, u32[]{:S(2)}, u32[]{:S(2)}) collective-permute-start(bf16[16,48,128]{2,1,0:T(8,128)(2,1)S(1)} %get-tuple-element.20), channel_id=1, source_target_pairs={{0,1},{1,0},{2,3},{3,2},{4,5},{5,4},{6,7},{7,6},{8,9},{9,8},{10,11... | collective-permute-start | bytes 589832 | tf_op jit(solution)/shard_map/ppermute | solution.py:221
  32.9 1.4 %collective-permute-start.1 = (bf16[16,24,256]{2,1,0:T(8,128)(2,1)S(1)}, bf16[16,24,256]{2,1,0:T(8,128)(2,1)S(1)}, u32[]{:S(2)}, u32[]{:S(2)}) collective-permute-start(bf16[16,24,256]{2,1,0:T(8,128)(2,1)S(1)} %all_to_all.11.own_ref), channel_id=1, source_target_pairs={{0,1},{1,0},{2,3},{3,2},{4,5},{5,4},{6,7},{7,6},{8,9},{9,8},{10,11... | collective-permute-start | bytes 589832 | tf_op jit(solution)/shard_map/ppermute | solution.py:227

commit v10 on v5

--- a/solution.py
+++ b/solution.py
@@ -39,26 +39,20 @@
     return pltpu.CompilerParams(vmem_limit_bytes=6 * 2**20, **more)
 
 
-def pack_kernel(grads_ref, kept_ref, sent_ref, wide_ref):
+def pack_kernel(grads_ref, kept_ref, sent_ref):
     chips, lines, lanes = kept_ref.shape
     core = lax.axis_index("replica")
-    row_ref = wide_ref.reshape(1, wide_ref.shape[0] * lanes)
-    width = 2 * lines * lanes
+    width = lines * lanes
     for k in range(chips):
-        row_ref[:, k * width : (k + 1) * width] = grads_ref[:, k * width : (k + 1) * width].astype(jnp.float32)
         for ref, place in ((kept_ref, core), (sent_ref, 1 - core)):
-            start = pl.multiple_of((2 * k + place) * lines, lines)
-            ref[k] = wide_ref[pl.ds(start, lines), :].astype(jnp.bfloat16)
+            start = pl.multiple_of((2 * k + place) * width, width)
+            row = grads_ref[:, pl.ds(start, width)].astype(jnp.float32)
+            ref[k] = row.reshape(lines, lanes).astype(jnp.bfloat16)
 
 
 def pack(grads, chips, lines):
     packed = jax.ShapeDtypeStruct((chips, lines, LANES), jnp.bfloat16)
-    return pl.pallas_call(
-        pack_kernel,
-        out_shape=(packed, packed),
-        scratch_shapes=[pltpu.VMEM((grads.shape[1] // LANES, LANES), jnp.float32)],
-        compiler_params=small(),
-    )(grads)
+    return pl.pallas_call(pack_kernel, out_shape=(packed, packed), compiler_params=small())(grads)
 
 
 def pair_kernel(kept_ref, taken_ref, *refs):
@@ -150,6 +144,15 @@
             value = ref[k].astype(jnp.float32)
             total = total + value * value
     factor = lax.rsqrt(jnp.sum(total, axis=1, keepdims=True) / D + norm_epsilon)
+    each = chips // parts
+    for p in range(parts):
+        for k in range(p * each, (p + 1) * each):
+            for ref, place in ((own_ref, core), (other_ref, 1 - core)):
+                start = pl.multiple_of((2 * k + place) * width, width)
+                scaled_ref[:, pl.ds(start, width)] = (ref[k].astype(jnp.float32) * factor).astype(jnp.bfloat16)
+        part = pl.ds(p * 2 * each * width, 2 * each * width)
+        copies.append(pltpu.make_async_copy(scaled_ref.at[:, part], copy_out.at[:, part], sems.at[3 + p]))
+        copies[-1].start()
     position = down_column(position_ref)
     period = columns // 8
     lane = lax.broadcasted_iota(jnp.int32, (1, LANES), 1)
@@ -161,16 +164,7 @@
         spread = jnp.where(line == p, picked, spread)
     master_ref[...] = stepped_ref[...] * spread
     copies.append(pltpu.make_async_copy(master_ref, master_out, sems.at[2]))
-    copies[2].start()
-    each = chips // parts
-    for p in range(parts):
-        for k in range(p * each, (p + 1) * each):
-            for ref, place in ((own_ref, core), (other_ref, 1 - core)):
-                start = pl.multiple_of((2 * k + place) * width, width)
-                scaled_ref[:, pl.ds(start, width)] = (ref[k].astype(jnp.float32) * factor).astype(jnp.bfloat16)
-        part = pl.ds(p * 2 * each * width, 2 * each * width)
-        copies.append(pltpu.make_async_copy(scaled_ref.at[:, part], copy_out.at[:, part], sems.at[3 + p]))
-        copies[3 + p].start()
+    copies[-1].start()
     for copy in copies:
         copy.wait()
 

time: 35 us -> 34.9 us (level)
  no operation moved by 1% of the time
where the time goes in v10:
time: 34.9 us; the launch traced here: 34.6 us
  blocking collectives  28.2 us (81%)
  waiting for transfers between devices  2.2 us (6%)
  Pallas kernels  1.56 us (4%)
  local copies, waits for them, and re-layouts  1.27 us (4%)
  between operations  0.67 us (2%)
  starting transfers between devices  0.52 us (1%)
    all_to_all x1, blocking collectives, on_device(): pieces = lax.all_to_all(pairs, 'shard', 0, 0, tiled=True)  17 us
    all_to_all x1, blocking collectives, on_device(): own = lax.all_to_all(copies, 'shard', 0, 0, tiled=True)  11.3 us
    ppermute x1, waiting for transfers between devices, on_device(): other = lax.ppermute(own, 'replica', [(0, 1), (1, 0)])  1.44 us
    unnamed x10, local copies, waits for them, and re-layouts  1.27 us
    pallas_call x1, Pallas kernels, finish(): pl.pallas_call(finish_kernel, in_specs=[pl.BlockSpec(memory_space=pltpu.V...  0.93 us
    ppermute x1, waiting for transfers between devices, on_device(): taken = lax.ppermute(sent, 'replica', [(0, 1), (1, 0)])  0.76 us
  transfers between devices with their start and end apart: 2, of which 2 were waited for; matrix products, arithmetic and copies ran while one was open for 1% of the time, Pallas kernels for 0%

profile of v10, /device:TPU:0, one launch (start us, length us, event | category | flops | bytes accessed | tf_op | source)
XLA Modules:
  0.0 34.6 jit_solution(11822872073330163695)
XLA Ops:
  0.6 0.0 copy-start
  0.6 1.1 %copy-done = bf16[1,196608]{1,0:T(2,128)(2,1)S(1)} copy-done((bf16[1,196608]{1,0:T(2,128)(2,1)S(1)}, bf16[1,196608]{1,0:T(2,128)(2,1)}, u32[]{:S(2)}) %copy-start) | copy-done | bytes 393240
  1.8 0.0 copy-start.1
  1.8 0.0 copy-start.2
  1.8 0.0 copy-start.3
  1.8 0.1 shard_map.84
  1.9 0.0 copy-start.4
  1.9 0.5 %collective-permute-start = (bf16[16,48,128]{2,1,0:T(8,128)(2,1)S(1)}, bf16[16,48,128]{2,1,0:T(8,128)(2,1)S(1)}, u32[]{:S(2)}, u32[]{:S(2)}) collective-permute-start(bf16[16,48,128]{2,1,0:T(8,128)(2,1)S(1)} %get-tuple-element.20), channel_id=1, source_target_pairs={{0,1},{1,0},{2,3},{3,2},{4,5},{5,4},{6,7},{7,6},{8,9},{9,8},{10,11... | collective-permute-start | bytes 589832 | tf_op jit(solution)/shard_map/ppermute | solution.py:211
  2.5 0.1 copy-done.4
  2.6 0.2 convert_reduce_fusion
  2.8 0.8 %collective-permute-done.taken_ref = bf16[16,48,128]{2,1,0:T(8,128)(2,1)S(1)} collective-permute-done((bf16[16,48,128]{2,1,0:T(8,128)(2,1)S(1)}, bf16[16,48,128]{2,1,0:T(8,128)(2,1)S(1)}, u32[]{:S(2)}, u32[]{:S(2)}) %collective-permute-start) | collective-permute-done | bytes 196640 | tf_op jit(solution)/shard_map/ppermute | solution.py:211
  3.5 0.0 copy-done.1
  3.5 0.0 copy-done.2
  3.5 0.0 copy-done.3
  3.6 17.0 %all_to_all.10.pieces_ref = bf16[16,48,128]{2,1,0:T(8,128)(2,1)S(1)} all-to-all(bf16[16,48,128]{2,1,0:T(8,128)(2,1)S(1)} %get-tuple-element.22), channel_id=1, replica_groups=mesh['shard'=16,'replica'=2] {'shard'}, dimensions={0} | all-to-all | bytes 393216 | tf_op jit(solution)/shard_map/all_to_all | solution.py:214
  20.6 0.4 %shard_map.86 = (f32[48,128]{1,0:T(8,128)S(1)}, f32[48,128]{1,0:T(8,128)S(1)}, f32[48,128]{1,0:T(8,128)S(1)}, bf16[16,24,256]{2,1,0:T(8,128)(2,1)S(1)}) custom-call(s32[1,24]{1,0:T(1,128)S(1)} %get-tuple-element.21.position_ref, bf16[16,48,128]{2,1,0:T(8,128)(2,1)S(1)} %all_to_all.10.pieces_ref, f32[48,128]{1,0:T(8,128)S(1)} %get-tuple-element.23.master_ref, ...), custom_call_target="tpu_custom_call" | custom-call | tf_op jit(solution)/shard_map/pallas_call | solution.py:121
  21.0 11.3 %all_to_all.11.own_ref = bf16[16,24,256]{2,1,0:T(8,128)(2,1)S(1)} all-to-all(bf16[16,24,256]{2,1,0:T(8,128)(2,1)S(1)} %get-tuple-element.29), channel_id=1, replica_groups=mesh['shard'=16,'replica'=2] {'shard'}, dimensions={0} | all-to-all | bytes 393216 | tf_op jit(solution)/shard_map/all_to_all | solution.py:216
  32.3 0.0 collective-permute-start.1
  32.3 1.4 %collective-permute-done.1.other_ref = bf16[16,24,256]{2,1,0:T(8,128)(2,1)S(1)} collective-permute-done((bf16[16,24,256]{2,1,0:T(8,128)(2,1)S(1)}, bf16[16,24,256]{2,1,0:T(8,128)(2,1)S(1)}, u32[]{:S(2)}, u32[]{:S(2)}) %collective-permute-start.1) | collective-permute-done | bytes 196640 | tf_op jit(solution)/shard_map/ppermute | solution.py:217
  33.7 0.9 %shard_map.87 = (f32[48,128]{1,0:T(8,128)}, f32[48,128]{1,0:T(8,128)}, f32[48,128]{1,0:T(8,128)}, bf16[24,8192]{1,0:T(8,128)(2,1)}) custom-call(s32[1,24]{1,0:T(1,128)S(1)} %get-tuple-element.21.position_ref, f32[48,128]{1,0:T(8,128)S(1)} %get-tuple-element.26.new_first_ref, f32[48,128]{1,0:T(8,128)S(1)} %get-tuple-element.27.new_second_ref, ...), custom_call_target="tpu_custom_call" | custom-call | tf_op jit(solution)/shard_map/pallas_call | solution.py:177
  (1 shorter events, 0.0 us)
Async XLA Ops:
  0.6 1.1 %copy-start = (bf16[1,196608]{1,0:T(2,128)(2,1)S(1)}, bf16[1,196608]{1,0:T(2,128)(2,1)}, u32[]{:S(2)}) copy-start(bf16[1,196608]{1,0:T(2,128)(2,1)} %grads_ref.1) | copy-start | bytes 1179652
  1.8 1.8 %copy-start.1 = (f32[6144]{0:T(1024)S(1)}, f32[6144]{0:T(1024)}, u32[]{:S(2)}) copy-start(f32[6144]{0:T(1024)} %param.6) | copy-start | bytes 73732
  1.8 1.8 %copy-start.2 = (f32[6144]{0:T(1024)S(1)}, f32[6144]{0:T(1024)}, u32[]{:S(2)}) copy-start(f32[6144]{0:T(1024)} %param.7) | copy-start | bytes 73732
  1.8 1.8 %copy-start.3 = (f32[6144]{0:T(1024)S(1)}, f32[6144]{0:T(1024)}, u32[]{:S(2)}) copy-start(f32[6144]{0:T(1024)} %param.8) | copy-start | bytes 73732
  1.9 0.7 %copy-start.4 = (s32[24]{0:T(128)S(1)}, s32[24]{0:T(128)}, u32[]{:S(2)}) copy-start(s32[24]{0:T(128)} %param.9) | copy-start | bytes 292
  1.9 1.6 %collective-permute-start = (bf16[16,48,128]{2,1,0:T(8,128)(2,1)S(1)}, bf16[16,48,128]{2,1,0:T(8,128)(2,1)S(1)}, u32[]{:S(2)}, u32[]{:S(2)}) collective-permute-start(bf16[16,48,128]{2,1,0:T(8,128)(2,1)S(1)} %get-tuple-element.20), channel_id=1, source_target_pairs={{0,1},{1,0},{2,3},{3,2},{4,5},{5,4},{6,7},{7,6},{8,9},{9,8},{10,11... | collective-permute-start | bytes 589832 | tf_op jit(solution)/shard_map/ppermute | solution.py:211
  32.3 1.4 %collective-permute-start.1 = (bf16[16,24,256]{2,1,0:T(8,128)(2,1)S(1)}, bf16[16,24,256]{2,1,0:T(8,128)(2,1)S(1)}, u32[]{:S(2)}, u32[]{:S(2)}) collective-permute-start(bf16[16,24,256]{2,1,0:T(8,128)(2,1)S(1)} %all_to_all.11.own_ref), channel_id=1, source_target_pairs={{0,1},{1,0},{2,3},{3,2},{4,5},{5,4},{6,7},{7,6},{8,9},{9,8},{10,11... | collective-permute-start | bytes 589832 | tf_op jit(solution)/shard_map/ppermute | solution.py:217

commit v11 on v10

--- a/solution.py
+++ b/solution.py
@@ -39,15 +39,25 @@
     return pltpu.CompilerParams(vmem_limit_bytes=6 * 2**20, **more)
 
 
+def far_first(chips):
+    return list(range(chips))[::-1]
+
+
+def middle_first(chips):
+    return [(k + chips // 2) % chips for k in range(chips)]
+
+
 def pack_kernel(grads_ref, kept_ref, sent_ref):
     chips, lines, lanes = kept_ref.shape
     core = lax.axis_index("replica")
     width = lines * lanes
+    order = far_first(chips)
+    slots = [order.index(k) for k in range(chips)]
     for k in range(chips):
         for ref, place in ((kept_ref, core), (sent_ref, 1 - core)):
             start = pl.multiple_of((2 * k + place) * width, width)
             row = grads_ref[:, pl.ds(start, width)].astype(jnp.float32)
-            ref[k] = row.reshape(lines, lanes).astype(jnp.bfloat16)
+            ref[slots[k]] = row.reshape(lines, lanes).astype(jnp.bfloat16)
 
 
 def pack(grads, chips, lines):
@@ -144,12 +154,14 @@
             value = ref[k].astype(jnp.float32)
             total = total + value * value
     factor = lax.rsqrt(jnp.sum(total, axis=1, keepdims=True) / D + norm_epsilon)
+    order = middle_first(chips)
+    slots = [order.index(k) for k in range(chips)]
     each = chips // parts
     for p in range(parts):
         for k in range(p * each, (p + 1) * each):
             for ref, place in ((own_ref, core), (other_ref, 1 - core)):
                 start = pl.multiple_of((2 * k + place) * width, width)
-                scaled_ref[:, pl.ds(start, width)] = (ref[k].astype(jnp.float32) * factor).astype(jnp.bfloat16)
+                scaled_ref[:, pl.ds(start, width)] = (ref[slots[k]].astype(jnp.float32) * factor).astype(jnp.bfloat16)
         part = pl.ds(p * 2 * each * width, 2 * each * width)
         copies.append(pltpu.make_async_copy(scaled_ref.at[:, part], copy_out.at[:, part], sems.at[3 + p]))
         copies[-1].start()
@@ -211,9 +223,11 @@
         taken = lax.ppermute(sent, "replica", [(0, 1), (1, 0)])
         states = (master, first_moment, second_moment)
         position, *states, pairs = add_pairs(kept, taken, flat_positions(owners), states)
-        pieces = lax.all_to_all(pairs, "shard", 0, 0, tiled=True)
+        groups = [far_first(shards)]
+        pieces = lax.all_to_all(pairs, "shard", 0, 0, tiled=True, axis_index_groups=groups)
         *updated, copies = middle(position, pieces, states, devices)
-        own = lax.all_to_all(copies, "shard", 0, 0, tiled=True)
+        groups = [middle_first(shards)]
+        own = lax.all_to_all(copies, "shard", 0, 0, tiled=True, axis_index_groups=groups)
         other = lax.ppermute(own, "replica", [(0, 1), (1, 0)])
         *flat, model_copy = finish(position, *updated, own, other)
         return (*(x.reshape(-1) for x in flat), model_copy)

time: 34.9 us -> 33 us (0.946)
  blocking collectives: 28.2 us -> 26.3 us
    all_to_all x2, blocking collectives: 28.2 us -> 26.3 us  [the longest x1 15 us: on_device(): lax.all_to_all(pairs, 'shard', 0, 0, tiled=True, axis_index_groups=groups)]
where the time goes in v11:
time: 33 us; the launch traced here: 32.8 us
  blocking collectives  26.3 us (80%)
  waiting for transfers between devices  2.2 us (7%)
  Pallas kernels  1.56 us (5%)
  local copies, waits for them, and re-layouts  1.27 us (4%)
  between operations  0.67 us (2%)
  starting transfers between devices  0.52 us (2%)
    all_to_all x1, blocking collectives, on_device(): lax.all_to_all(pairs, 'shard', 0, 0, tiled=True, axis_index_groups=groups)  15 us
    all_to_all x1, blocking collectives, on_device(): lax.all_to_all(copies, 'shard', 0, 0, tiled=True, axis_index_groups=groups)  11.4 us
    ppermute x1, waiting for transfers between devices, on_device(): other = lax.ppermute(own, 'replica', [(0, 1), (1, 0)])  1.44 us
    unnamed x10, local copies, waits for them, and re-layouts  1.27 us
    pallas_call x1, Pallas kernels, finish(): pl.pallas_call(finish_kernel, in_specs=[pl.BlockSpec(memory_space=pltpu.V...  0.93 us
    ppermute x1, waiting for transfers between devices, on_device(): taken = lax.ppermute(sent, 'replica', [(0, 1), (1, 0)])  0.76 us
  transfers between devices with their start and end apart: 2, of which 2 were waited for; matrix products, arithmetic and copies ran while one was open for 1% of the time, Pallas kernels for 0%

profile of v11, /device:TPU:0, one launch (start us, length us, event | category | flops | bytes accessed | tf_op | source)
XLA Modules:
  0.0 32.8 jit_solution(16015813190602856946)
XLA Ops:
  0.6 0.0 copy-start
  0.6 1.1 %copy-done = bf16[1,196608]{1,0:T(2,128)(2,1)S(1)} copy-done((bf16[1,196608]{1,0:T(2,128)(2,1)S(1)}, bf16[1,196608]{1,0:T(2,128)(2,1)}, u32[]{:S(2)}) %copy-start) | copy-done | bytes 393240
  1.8 0.0 copy-start.1
  1.8 0.0 copy-start.2
  1.8 0.0 copy-start.3
  1.8 0.1 shard_map.84
  1.9 0.0 copy-start.4
  1.9 0.5 %collective-permute-start = (bf16[16,48,128]{2,1,0:T(8,128)(2,1)S(1)}, bf16[16,48,128]{2,1,0:T(8,128)(2,1)S(1)}, u32[]{:S(2)}, u32[]{:S(2)}) collective-permute-start(bf16[16,48,128]{2,1,0:T(8,128)(2,1)S(1)} %get-tuple-element.20), channel_id=1, source_target_pairs={{0,1},{1,0},{2,3},{3,2},{4,5},{5,4},{6,7},{7,6},{8,9},{9,8},{10,11... | collective-permute-start | bytes 589832 | tf_op jit(solution)/shard_map/ppermute | solution.py:223
  2.5 0.1 copy-done.4
  2.6 0.2 convert_reduce_fusion
  2.8 0.8 %collective-permute-done.taken_ref = bf16[16,48,128]{2,1,0:T(8,128)(2,1)S(1)} collective-permute-done((bf16[16,48,128]{2,1,0:T(8,128)(2,1)S(1)}, bf16[16,48,128]{2,1,0:T(8,128)(2,1)S(1)}, u32[]{:S(2)}, u32[]{:S(2)}) %collective-permute-start) | collective-permute-done | bytes 196640 | tf_op jit(solution)/shard_map/ppermute | solution.py:223
  3.5 0.0 copy-done.1
  3.5 0.0 copy-done.2
  3.5 0.0 copy-done.3
  3.6 15.0 %all_to_all.10.pieces_ref = bf16[16,48,128]{2,1,0:T(8,128)(2,1)S(1)} all-to-all(bf16[16,48,128]{2,1,0:T(8,128)(2,1)S(1)} %get-tuple-element.22), channel_id=1, replica_groups={{30,28,26,24,22,20,18,16,14,12,10,8,6,4,2,0},{31,29,27,25,23,21,19,17,1..., dimensions={0} | all-to-all | bytes 393216 | tf_op jit(solution)/shard_map/all_to_all | solution.py:227
  18.6 0.4 %shard_map.86 = (f32[48,128]{1,0:T(8,128)S(1)}, f32[48,128]{1,0:T(8,128)S(1)}, f32[48,128]{1,0:T(8,128)S(1)}, bf16[16,24,256]{2,1,0:T(8,128)(2,1)S(1)}) custom-call(s32[1,24]{1,0:T(1,128)S(1)} %get-tuple-element.21.position_ref, bf16[16,48,128]{2,1,0:T(8,128)(2,1)S(1)} %all_to_all.10.pieces_ref, f32[48,128]{1,0:T(8,128)S(1)} %get-tuple-element.23.master_ref, ...), custom_call_target="tpu_custom_call" | custom-call | tf_op jit(solution)/shard_map/pallas_call | solution.py:131
  19.0 11.4 %all_to_all.11.own_ref = bf16[16,24,256]{2,1,0:T(8,128)(2,1)S(1)} all-to-all(bf16[16,24,256]{2,1,0:T(8,128)(2,1)S(1)} %get-tuple-element.29), channel_id=1, replica_groups={{16,18,20,22,24,26,28,30,0,2,4,6,8,10,12,14},{17,19,21,23,25,27,29,31,1..., dimensions={0} | all-to-all | bytes 393216 | tf_op jit(solution)/shard_map/all_to_all | solution.py:230
  30.4 0.0 collective-permute-start.1
  30.4 1.4 %collective-permute-done.1.other_ref = bf16[16,24,256]{2,1,0:T(8,128)(2,1)S(1)} collective-permute-done((bf16[16,24,256]{2,1,0:T(8,128)(2,1)S(1)}, bf16[16,24,256]{2,1,0:T(8,128)(2,1)S(1)}, u32[]{:S(2)}, u32[]{:S(2)}) %collective-permute-start.1) | collective-permute-done | bytes 196640 | tf_op jit(solution)/shard_map/ppermute | solution.py:231
  31.8 0.9 %shard_map.87 = (f32[48,128]{1,0:T(8,128)}, f32[48,128]{1,0:T(8,128)}, f32[48,128]{1,0:T(8,128)}, bf16[24,8192]{1,0:T(8,128)(2,1)}) custom-call(s32[1,24]{1,0:T(1,128)S(1)} %get-tuple-element.21.position_ref, f32[48,128]{1,0:T(8,128)S(1)} %get-tuple-element.26.new_first_ref, f32[48,128]{1,0:T(8,128)S(1)} %get-tuple-element.27.new_second_ref, ...), custom_call_target="tpu_custom_call" | custom-call | tf_op jit(solution)/shard_map/pallas_call | solution.py:189
  (1 shorter events, 0.0 us)
Async XLA Ops:
  0.6 1.1 %copy-start = (bf16[1,196608]{1,0:T(2,128)(2,1)S(1)}, bf16[1,196608]{1,0:T(2,128)(2,1)}, u32[]{:S(2)}) copy-start(bf16[1,196608]{1,0:T(2,128)(2,1)} %grads_ref.1) | copy-start | bytes 1179652
  1.8 1.8 %copy-start.1 = (f32[6144]{0:T(1024)S(1)}, f32[6144]{0:T(1024)}, u32[]{:S(2)}) copy-start(f32[6144]{0:T(1024)} %param.6) | copy-start | bytes 73732
  1.8 1.8 %copy-start.2 = (f32[6144]{0:T(1024)S(1)}, f32[6144]{0:T(1024)}, u32[]{:S(2)}) copy-start(f32[6144]{0:T(1024)} %param.7) | copy-start | bytes 73732
  1.8 1.8 %copy-start.3 = (f32[6144]{0:T(1024)S(1)}, f32[6144]{0:T(1024)}, u32[]{:S(2)}) copy-start(f32[6144]{0:T(1024)} %param.8) | copy-start | bytes 73732
  1.9 0.7 %copy-start.4 = (s32[24]{0:T(128)S(1)}, s32[24]{0:T(128)}, u32[]{:S(2)}) copy-start(s32[24]{0:T(128)} %param.9) | copy-start | bytes 292
  1.9 1.6 %collective-permute-start = (bf16[16,48,128]{2,1,0:T(8,128)(2,1)S(1)}, bf16[16,48,128]{2,1,0:T(8,128)(2,1)S(1)}, u32[]{:S(2)}, u32[]{:S(2)}) collective-permute-start(bf16[16,48,128]{2,1,0:T(8,128)(2,1)S(1)} %get-tuple-element.20), channel_id=1, source_target_pairs={{0,1},{1,0},{2,3},{3,2},{4,5},{5,4},{6,7},{7,6},{8,9},{9,8},{10,11... | collective-permute-start | bytes 589832 | tf_op jit(solution)/shard_map/ppermute | solution.py:223
  30.4 1.4 %collective-permute-start.1 = (bf16[16,24,256]{2,1,0:T(8,128)(2,1)S(1)}, bf16[16,24,256]{2,1,0:T(8,128)(2,1)S(1)}, u32[]{:S(2)}, u32[]{:S(2)}) collective-permute-start(bf16[16,24,256]{2,1,0:T(8,128)(2,1)S(1)} %all_to_all.11.own_ref), channel_id=1, source_target_pairs={{0,1},{1,0},{2,3},{3,2},{4,5},{5,4},{6,7},{7,6},{8,9},{9,8},{10,11... | collective-permute-start | bytes 589832 | tf_op jit(solution)/shard_map/ppermute | solution.py:231

commit v12 on v11

--- a/solution.py
+++ b/solution.py
@@ -41,10 +41,6 @@
 
 def far_first(chips):
     return list(range(chips))[::-1]
-
-
-def middle_first(chips):
-    return [(k + chips // 2) % chips for k in range(chips)]
 
 
 def pack_kernel(grads_ref, kept_ref, sent_ref):
@@ -154,7 +150,7 @@
             value = ref[k].astype(jnp.float32)
             total = total + value * value
     factor = lax.rsqrt(jnp.sum(total, axis=1, keepdims=True) / D + norm_epsilon)
-    order = middle_first(chips)
+    order = far_first(chips)
     slots = [order.index(k) for k in range(chips)]
     each = chips // parts
     for p in range(parts):
@@ -226,7 +222,6 @@
         groups = [far_first(shards)]
         pieces = lax.all_to_all(pairs, "shard", 0, 0, tiled=True, axis_index_groups=groups)
         *updated, copies = middle(position, pieces, states, devices)
-        groups = [middle_first(shards)]
         own = lax.all_to_all(copies, "shard", 0, 0, tiled=True, axis_index_groups=groups)
         other = lax.ppermute(own, "replica", [(0, 1), (1, 0)])
         *flat, model_copy = finish(position, *updated, own, other)

time: 33 us -> 33.1 us (level)
  no operation moved by 1% of the time
where the time goes in v12:
time: 33.1 us; the launch traced here: 32.8 us
  blocking collectives  26.4 us (80%)
  waiting for transfers between devices  2.2 us (7%)
  Pallas kernels  1.56 us (5%)
  local copies, waits for them, and re-layouts  1.27 us (4%)
  between operations  0.67 us (2%)
  starting transfers between devices  0.52 us (2%)
    all_to_all x1, blocking collectives, on_device(): lax.all_to_all(pairs, 'shard', 0, 0, tiled=True, axis_index_groups=groups)  15 us
    all_to_all x1, blocking collectives, on_device(): lax.all_to_all(copies, 'shard', 0, 0, tiled=True, axis_index_groups=groups)  11.4 us
    ppermute x1, waiting for transfers between devices, on_device(): other = lax.ppermute(own, 'replica', [(0, 1), (1, 0)])  1.44 us
    unnamed x10, local copies, waits for them, and re-layouts  1.27 us
    pallas_call x1, Pallas kernels, finish(): pl.pallas_call(finish_kernel, in_specs=[pl.BlockSpec(memory_space=pltpu.V...  0.93 us
    ppermute x1, waiting for transfers between devices, on_device(): taken = lax.ppermute(sent, 'replica', [(0, 1), (1, 0)])  0.76 us
  transfers between devices with their start and end apart: 2, of which 2 were waited for; matrix products, arithmetic and copies ran while one was open for 1% of the time, Pallas kernels for 0%

profile of v12, /device:TPU:0, one launch (start us, length us, event | category | flops | bytes accessed | tf_op | source)
XLA Modules:
  0.0 32.8 jit_solution(13242391409797842620)
XLA Ops:
  0.6 0.0 copy-start
  0.6 1.1 %copy-done = bf16[1,196608]{1,0:T(2,128)(2,1)S(1)} copy-done((bf16[1,196608]{1,0:T(2,128)(2,1)S(1)}, bf16[1,196608]{1,0:T(2,128)(2,1)}, u32[]{:S(2)}) %copy-start) | copy-done | bytes 393240
  1.8 0.0 copy-start.1
  1.8 0.0 copy-start.2
  1.8 0.0 copy-start.3
  1.8 0.1 shard_map.84
  1.9 0.0 copy-start.4
  1.9 0.5 %collective-permute-start = (bf16[16,48,128]{2,1,0:T(8,128)(2,1)S(1)}, bf16[16,48,128]{2,1,0:T(8,128)(2,1)S(1)}, u32[]{:S(2)}, u32[]{:S(2)}) collective-permute-start(bf16[16,48,128]{2,1,0:T(8,128)(2,1)S(1)} %get-tuple-element.20), channel_id=1, source_target_pairs={{0,1},{1,0},{2,3},{3,2},{4,5},{5,4},{6,7},{7,6},{8,9},{9,8},{10,11... | collective-permute-start | bytes 589832 | tf_op jit(solution)/shard_map/ppermute | solution.py:219
  2.5 0.1 copy-done.4
  2.6 0.2 convert_reduce_fusion
  2.8 0.8 %collective-permute-done.taken_ref = bf16[16,48,128]{2,1,0:T(8,128)(2,1)S(1)} collective-permute-done((bf16[16,48,128]{2,1,0:T(8,128)(2,1)S(1)}, bf16[16,48,128]{2,1,0:T(8,128)(2,1)S(1)}, u32[]{:S(2)}, u32[]{:S(2)}) %collective-permute-start) | collective-permute-done | bytes 196640 | tf_op jit(solution)/shard_map/ppermute | solution.py:219
  3.5 0.0 copy-done.1
  3.5 0.0 copy-done.2
  3.5 0.0 copy-done.3
  3.6 15.0 %all_to_all.10.pieces_ref = bf16[16,48,128]{2,1,0:T(8,128)(2,1)S(1)} all-to-all(bf16[16,48,128]{2,1,0:T(8,128)(2,1)S(1)} %get-tuple-element.22), channel_id=1, replica_groups={{30,28,26,24,22,20,18,16,14,12,10,8,6,4,2,0},{31,29,27,25,23,21,19,17,1..., dimensions={0} | all-to-all | bytes 393216 | tf_op jit(solution)/shard_map/all_to_all | solution.py:223
  18.6 0.4 %shard_map.86 = (f32[48,128]{1,0:T(8,128)S(1)}, f32[48,128]{1,0:T(8,128)S(1)}, f32[48,128]{1,0:T(8,128)S(1)}, bf16[16,24,256]{2,1,0:T(8,128)(2,1)S(1)}) custom-call(s32[1,24]{1,0:T(1,128)S(1)} %get-tuple-element.21.position_ref, bf16[16,48,128]{2,1,0:T(8,128)(2,1)S(1)} %all_to_all.10.pieces_ref, f32[48,128]{1,0:T(8,128)S(1)} %get-tuple-element.23.master_ref, ...), custom_call_target="tpu_custom_call" | custom-call | tf_op jit(solution)/shard_map/pallas_call | solution.py:127
  19.0 11.4 %all_to_all.11.own_ref = bf16[16,24,256]{2,1,0:T(8,128)(2,1)S(1)} all-to-all(bf16[16,24,256]{2,1,0:T(8,128)(2,1)S(1)} %get-tuple-element.29), channel_id=1, replica_groups={{30,28,26,24,22,20,18,16,14,12,10,8,6,4,2,0},{31,29,27,25,23,21,19,17,1..., dimensions={0} | all-to-all | bytes 393216 | tf_op jit(solution)/shard_map/all_to_all | solution.py:225
  30.5 0.0 collective-permute-start.1
  30.5 1.4 %collective-permute-done.1.other_ref = bf16[16,24,256]{2,1,0:T(8,128)(2,1)S(1)} collective-permute-done((bf16[16,24,256]{2,1,0:T(8,128)(2,1)S(1)}, bf16[16,24,256]{2,1,0:T(8,128)(2,1)S(1)}, u32[]{:S(2)}, u32[]{:S(2)}) %collective-permute-start.1) | collective-permute-done | bytes 196640 | tf_op jit(solution)/shard_map/ppermute | solution.py:226
  31.9 0.9 %shard_map.87 = (f32[48,128]{1,0:T(8,128)}, f32[48,128]{1,0:T(8,128)}, f32[48,128]{1,0:T(8,128)}, bf16[24,8192]{1,0:T(8,128)(2,1)}) custom-call(s32[1,24]{1,0:T(1,128)S(1)} %get-tuple-element.21.position_ref, f32[48,128]{1,0:T(8,128)S(1)} %get-tuple-element.26.new_first_ref, f32[48,128]{1,0:T(8,128)S(1)} %get-tuple-element.27.new_second_ref, ...), custom_call_target="tpu_custom_call" | custom-call | tf_op jit(solution)/shard_map/pallas_call | solution.py:185
  (1 shorter events, 0.0 us)
Async XLA Ops:
  0.6 1.1 %copy-start = (bf16[1,196608]{1,0:T(2,128)(2,1)S(1)}, bf16[1,196608]{1,0:T(2,128)(2,1)}, u32[]{:S(2)}) copy-start(bf16[1,196608]{1,0:T(2,128)(2,1)} %grads_ref.1) | copy-start | bytes 1179652
  1.8 1.8 %copy-start.1 = (f32[6144]{0:T(1024)S(1)}, f32[6144]{0:T(1024)}, u32[]{:S(2)}) copy-start(f32[6144]{0:T(1024)} %param.6) | copy-start | bytes 73732
  1.8 1.8 %copy-start.2 = (f32[6144]{0:T(1024)S(1)}, f32[6144]{0:T(1024)}, u32[]{:S(2)}) copy-start(f32[6144]{0:T(1024)} %param.7) | copy-start | bytes 73732
  1.8 1.8 %copy-start.3 = (f32[6144]{0:T(1024)S(1)}, f32[6144]{0:T(1024)}, u32[]{:S(2)}) copy-start(f32[6144]{0:T(1024)} %param.8) | copy-start | bytes 73732
  1.9 0.7 %copy-start.4 = (s32[24]{0:T(128)S(1)}, s32[24]{0:T(128)}, u32[]{:S(2)}) copy-start(s32[24]{0:T(128)} %param.9) | copy-start | bytes 292
  1.9 1.6 %collective-permute-start = (bf16[16,48,128]{2,1,0:T(8,128)(2,1)S(1)}, bf16[16,48,128]{2,1,0:T(8,128)(2,1)S(1)}, u32[]{:S(2)}, u32[]{:S(2)}) collective-permute-start(bf16[16,48,128]{2,1,0:T(8,128)(2,1)S(1)} %get-tuple-element.20), channel_id=1, source_target_pairs={{0,1},{1,0},{2,3},{3,2},{4,5},{5,4},{6,7},{7,6},{8,9},{9,8},{10,11... | collective-permute-start | bytes 589832 | tf_op jit(solution)/shard_map/ppermute | solution.py:219
  30.5 1.4 %collective-permute-start.1 = (bf16[16,24,256]{2,1,0:T(8,128)(2,1)S(1)}, bf16[16,24,256]{2,1,0:T(8,128)(2,1)S(1)}, u32[]{:S(2)}, u32[]{:S(2)}) collective-permute-start(bf16[16,24,256]{2,1,0:T(8,128)(2,1)S(1)} %all_to_all.11.own_ref), channel_id=1, source_target_pairs={{0,1},{1,0},{2,3},{3,2},{4,5},{5,4},{6,7},{7,6},{8,9},{9,8},{10,11... | collective-permute-start | bytes 589832 | tf_op jit(solution)/shard_map/ppermute | solution.py:226

commit v13 on v12

--- a/solution.py
+++ b/solution.py
@@ -17,6 +17,7 @@
 second_correction = 1.0 - 0.95**20
 AXES = ("shard", "replica")
 LANES = 128
+FIRST = (11, 8)
 
 
 def adam_step(gradient, master, first_moment, second_moment):
@@ -39,15 +40,16 @@
     return pltpu.CompilerParams(vmem_limit_bytes=6 * 2**20, **more)
 
 
-def far_first(chips):
-    return list(range(chips))[::-1]
+def listed(chips, first):
+    first = first % chips
+    return [k ^ first for k in range(chips)]
 
 
 def pack_kernel(grads_ref, kept_ref, sent_ref):
     chips, lines, lanes = kept_ref.shape
     core = lax.axis_index("replica")
     width = lines * lanes
-    order = far_first(chips)
+    order = listed(chips, FIRST[0])
     slots = [order.index(k) for k in range(chips)]
     for k in range(chips):
         for ref, place in ((kept_ref, core), (sent_ref, 1 - core)):
@@ -150,7 +152,7 @@
             value = ref[k].astype(jnp.float32)
             total = total + value * value
     factor = lax.rsqrt(jnp.sum(total, axis=1, keepdims=True) / D + norm_epsilon)
-    order = far_first(chips)
+    order = listed(chips, FIRST[1])
     slots = [order.index(k) for k in range(chips)]
     each = chips // parts
     for p in range(parts):
@@ -214,14 +216,15 @@
     shards, replicas = lax.axis_size("shard"), lax.axis_size("replica")
     devices = shards * replicas
     columns = owners.shape[0]
-    if replicas == 2 and master.shape[0] // LANES % 48 == 0:
+    if replicas == 2 and shards == 16 and master.shape[0] // LANES % 48 == 0:
         kept, sent = pack(grads, shards, master.shape[0] // LANES)
         taken = lax.ppermute(sent, "replica", [(0, 1), (1, 0)])
         states = (master, first_moment, second_moment)
         position, *states, pairs = add_pairs(kept, taken, flat_positions(owners), states)
-        groups = [far_first(shards)]
+        groups = [listed(shards, FIRST[0])]
         pieces = lax.all_to_all(pairs, "shard", 0, 0, tiled=True, axis_index_groups=groups)
         *updated, copies = middle(position, pieces, states, devices)
+        groups = [listed(shards, FIRST[1])]
         own = lax.all_to_all(copies, "shard", 0, 0, tiled=True, axis_index_groups=groups)
         other = lax.ppermute(own, "replica", [(0, 1), (1, 0)])
         *flat, model_copy = finish(position, *updated, own, other)

time: 33.1 us -> 32.1 us (0.970)
  blocking collectives: 26.4 us -> 25.4 us
    all_to_all x1, blocking collectives: 15 us -> 13.5 us  [on_device(): lax.all_to_all(pairs, 'shard', 0, 0, tiled=True, axis_index_groups=groups)]
    all_to_all x1, blocking collectives: 11.4 us -> 11.8 us  [on_device(): lax.all_to_all(copies, 'shard', 0, 0, tiled=True, axis_index_groups=groups)]
where the time goes in v13:
time: 32.1 us; the launch traced here: 31.8 us
  blocking collectives  25.4 us (79%)
  waiting for transfers between devices  2.2 us (7%)
  Pallas kernels  1.56 us (5%)
  local copies, waits for them, and re-layouts  1.27 us (4%)
  between operations  0.67 us (2%)
  starting transfers between devices  0.52 us (2%)
    all_to_all x1, blocking collectives, on_device(): lax.all_to_all(pairs, 'shard', 0, 0, tiled=True, axis_index_groups=groups)  13.5 us
    all_to_all x1, blocking collectives, on_device(): lax.all_to_all(copies, 'shard', 0, 0, tiled=True, axis_index_groups=groups)  11.8 us
    ppermute x1, waiting for transfers between devices, on_device(): other = lax.ppermute(own, 'replica', [(0, 1), (1, 0)])  1.44 us
    unnamed x10, local copies, waits for them, and re-layouts  1.27 us
    pallas_call x1, Pallas kernels, finish(): pl.pallas_call(finish_kernel, in_specs=[pl.BlockSpec(memory_space=pltpu.V...  0.93 us
    ppermute x1, waiting for transfers between devices, on_device(): taken = lax.ppermute(sent, 'replica', [(0, 1), (1, 0)])  0.76 us
  transfers between devices with their start and end apart: 2, of which 2 were waited for; matrix products, arithmetic and copies ran while one was open for 1% of the time, Pallas kernels for 0%

profile of v13, /device:TPU:0, one launch (start us, length us, event | category | flops | bytes accessed | tf_op | source)
XLA Modules:
  0.0 31.8 jit_solution(15916508273696007519)
XLA Ops:
  0.6 0.0 copy-start
  0.6 1.1 %copy-done = bf16[1,196608]{1,0:T(2,128)(2,1)S(1)} copy-done((bf16[1,196608]{1,0:T(2,128)(2,1)S(1)}, bf16[1,196608]{1,0:T(2,128)(2,1)}, u32[]{:S(2)}) %copy-start) | copy-done | bytes 393240
  1.8 0.0 copy-start.1
  1.8 0.0 copy-start.2
  1.8 0.0 copy-start.3
  1.8 0.1 shard_map.84
  1.9 0.0 copy-start.4
  1.9 0.5 %collective-permute-start = (bf16[16,48,128]{2,1,0:T(8,128)(2,1)S(1)}, bf16[16,48,128]{2,1,0:T(8,128)(2,1)S(1)}, u32[]{:S(2)}, u32[]{:S(2)}) collective-permute-start(bf16[16,48,128]{2,1,0:T(8,128)(2,1)S(1)} %get-tuple-element.20), channel_id=1, source_target_pairs={{0,1},{1,0},{2,3},{3,2},{4,5},{5,4},{6,7},{7,6},{8,9},{9,8},{10,11... | collective-permute-start | bytes 589832 | tf_op jit(solution)/shard_map/ppermute | solution.py:221
  2.5 0.1 copy-done.4
  2.6 0.2 convert_reduce_fusion
  2.8 0.8 %collective-permute-done.taken_ref = bf16[16,48,128]{2,1,0:T(8,128)(2,1)S(1)} collective-permute-done((bf16[16,48,128]{2,1,0:T(8,128)(2,1)S(1)}, bf16[16,48,128]{2,1,0:T(8,128)(2,1)S(1)}, u32[]{:S(2)}, u32[]{:S(2)}) %collective-permute-start) | collective-permute-done | bytes 196640 | tf_op jit(solution)/shard_map/ppermute | solution.py:221
  3.5 0.0 copy-done.1
  3.5 0.0 copy-done.2
  3.5 0.0 copy-done.3
  3.6 13.5 %all_to_all.10.pieces_ref = bf16[16,48,128]{2,1,0:T(8,128)(2,1)S(1)} all-to-all(bf16[16,48,128]{2,1,0:T(8,128)(2,1)S(1)} %get-tuple-element.22), channel_id=1, replica_groups={{22,20,18,16,30,28,26,24,6,4,2,0,14,12,10,8},{23,21,19,17,31,29,27,25,7..., dimensions={0} | all-to-all | bytes 393216 | tf_op jit(solution)/shard_map/all_to_all | solution.py:225
  17.1 0.4 %shard_map.86 = (f32[48,128]{1,0:T(8,128)S(1)}, f32[48,128]{1,0:T(8,128)S(1)}, f32[48,128]{1,0:T(8,128)S(1)}, bf16[16,24,256]{2,1,0:T(8,128)(2,1)S(1)}) custom-call(s32[1,24]{1,0:T(1,128)S(1)} %get-tuple-element.21.position_ref, bf16[16,48,128]{2,1,0:T(8,128)(2,1)S(1)} %all_to_all.10.pieces_ref, f32[48,128]{1,0:T(8,128)S(1)} %get-tuple-element.23.master_ref, ...), custom_call_target="tpu_custom_call" | custom-call | tf_op jit(solution)/shard_map/pallas_call | solution.py:129
  17.6 11.8 %all_to_all.11.own_ref = bf16[16,24,256]{2,1,0:T(8,128)(2,1)S(1)} all-to-all(bf16[16,24,256]{2,1,0:T(8,128)(2,1)S(1)} %get-tuple-element.29), channel_id=1, replica_groups={{16,18,20,22,24,26,28,30,0,2,4,6,8,10,12,14},{17,19,21,23,25,27,29,31,1..., dimensions={0} | all-to-all | bytes 393216 | tf_op jit(solution)/shard_map/all_to_all | solution.py:228
  29.4 0.0 collective-permute-start.1
  29.4 1.4 %collective-permute-done.1.other_ref = bf16[16,24,256]{2,1,0:T(8,128)(2,1)S(1)} collective-permute-done((bf16[16,24,256]{2,1,0:T(8,128)(2,1)S(1)}, bf16[16,24,256]{2,1,0:T(8,128)(2,1)S(1)}, u32[]{:S(2)}, u32[]{:S(2)}) %collective-permute-start.1) | collective-permute-done | bytes 196640 | tf_op jit(solution)/shard_map/ppermute | solution.py:229
  30.9 0.9 %shard_map.87 = (f32[48,128]{1,0:T(8,128)}, f32[48,128]{1,0:T(8,128)}, f32[48,128]{1,0:T(8,128)}, bf16[24,8192]{1,0:T(8,128)(2,1)}) custom-call(s32[1,24]{1,0:T(1,128)S(1)} %get-tuple-element.21.position_ref, f32[48,128]{1,0:T(8,128)S(1)} %get-tuple-element.26.new_first_ref, f32[48,128]{1,0:T(8,128)S(1)} %get-tuple-element.27.new_second_ref, ...), custom_call_target="tpu_custom_call" | custom-call | tf_op jit(solution)/shard_map/pallas_call | solution.py:187
  (1 shorter events, 0.0 us)
Async XLA Ops:
  0.6 1.1 %copy-start = (bf16[1,196608]{1,0:T(2,128)(2,1)S(1)}, bf16[1,196608]{1,0:T(2,128)(2,1)}, u32[]{:S(2)}) copy-start(bf16[1,196608]{1,0:T(2,128)(2,1)} %grads_ref.1) | copy-start | bytes 1179652
  1.8 1.8 %copy-start.1 = (f32[6144]{0:T(1024)S(1)}, f32[6144]{0:T(1024)}, u32[]{:S(2)}) copy-start(f32[6144]{0:T(1024)} %param.6) | copy-start | bytes 73732
  1.8 1.8 %copy-start.2 = (f32[6144]{0:T(1024)S(1)}, f32[6144]{0:T(1024)}, u32[]{:S(2)}) copy-start(f32[6144]{0:T(1024)} %param.7) | copy-start | bytes 73732
  1.8 1.8 %copy-start.3 = (f32[6144]{0:T(1024)S(1)}, f32[6144]{0:T(1024)}, u32[]{:S(2)}) copy-start(f32[6144]{0:T(1024)} %param.8) | copy-start | bytes 73732
  1.9 0.7 %copy-start.4 = (s32[24]{0:T(128)S(1)}, s32[24]{0:T(128)}, u32[]{:S(2)}) copy-start(s32[24]{0:T(128)} %param.9) | copy-start | bytes 292
  1.9 1.6 %collective-permute-start = (bf16[16,48,128]{2,1,0:T(8,128)(2,1)S(1)}, bf16[16,48,128]{2,1,0:T(8,128)(2,1)S(1)}, u32[]{:S(2)}, u32[]{:S(2)}) collective-permute-start(bf16[16,48,128]{2,1,0:T(8,128)(2,1)S(1)} %get-tuple-element.20), channel_id=1, source_target_pairs={{0,1},{1,0},{2,3},{3,2},{4,5},{5,4},{6,7},{7,6},{8,9},{9,8},{10,11... | collective-permute-start | bytes 589832 | tf_op jit(solution)/shard_map/ppermute | solution.py:221
  29.4 1.4 %collective-permute-start.1 = (bf16[16,24,256]{2,1,0:T(8,128)(2,1)S(1)}, bf16[16,24,256]{2,1,0:T(8,128)(2,1)S(1)}, u32[]{:S(2)}, u32[]{:S(2)}) collective-permute-start(bf16[16,24,256]{2,1,0:T(8,128)(2,1)S(1)} %all_to_all.11.own_ref), channel_id=1, source_target_pairs={{0,1},{1,0},{2,3},{3,2},{4,5},{5,4},{6,7},{7,6},{8,9},{9,8},{10,11... | collective-permute-start | bytes 589832 | tf_op jit(solution)/shard_map/ppermute | solution.py:229

commit v14 on v13

--- a/solution.py
+++ b/solution.py
@@ -17,7 +17,7 @@
 second_correction = 1.0 - 0.95**20
 AXES = ("shard", "replica")
 LANES = 128
-FIRST = (11, 8)
+FIRST = (11, 11)
 
 
 def adam_step(gradient, master, first_moment, second_moment):

time: 32.1 us -> 30.8 us (0.960)
  blocking collectives: 25.4 us -> 24.1 us
    all_to_all x1, blocking collectives: 11.8 us -> 10.5 us  [on_device(): lax.all_to_all(copies, 'shard', 0, 0, tiled=True, axis_index_groups=groups)]
where the time goes in v14:
time: 30.8 us; the launch traced here: 30.5 us
  blocking collectives  24.1 us (78%)
  waiting for transfers between devices  2.2 us (7%)
  Pallas kernels  1.56 us (5%)
  local copies, waits for them, and re-layouts  1.27 us (4%)
  between operations  0.67 us (2%)
  starting transfers between devices  0.52 us (2%)
    all_to_all x1, blocking collectives, on_device(): lax.all_to_all(pairs, 'shard', 0, 0, tiled=True, axis_index_groups=groups)  13.5 us
    all_to_all x1, blocking collectives, on_device(): lax.all_to_all(copies, 'shard', 0, 0, tiled=True, axis_index_groups=groups)  10.5 us
    ppermute x1, waiting for transfers between devices, on_device(): other = lax.ppermute(own, 'replica', [(0, 1), (1, 0)])  1.44 us
    unnamed x10, local copies, waits for them, and re-layouts  1.27 us
    pallas_call x1, Pallas kernels, finish(): pl.pallas_call(finish_kernel, in_specs=[pl.BlockSpec(memory_space=pltpu.V...  0.93 us
    ppermute x1, waiting for transfers between devices, on_device(): taken = lax.ppermute(sent, 'replica', [(0, 1), (1, 0)])  0.76 us
  transfers between devices with their start and end apart: 2, of which 2 were waited for; matrix products, arithmetic and copies ran while one was open for 1% of the time, Pallas kernels for 0%

profile of v14, /device:TPU:0, one launch (start us, length us, event | category | flops | bytes accessed | tf_op | source)
XLA Modules:
  0.0 30.5 jit_solution(3786444441786410354)
XLA Ops:
  0.6 0.0 copy-start
  0.6 1.1 %copy-done = bf16[1,196608]{1,0:T(2,128)(2,1)S(1)} copy-done((bf16[1,196608]{1,0:T(2,128)(2,1)S(1)}, bf16[1,196608]{1,0:T(2,128)(2,1)}, u32[]{:S(2)}) %copy-start) | copy-done | bytes 393240
  1.8 0.0 copy-start.1
  1.8 0.0 copy-start.2
  1.8 0.0 copy-start.3
  1.8 0.1 shard_map.84
  1.9 0.0 copy-start.4
  1.9 0.5 %collective-permute-start = (bf16[16,48,128]{2,1,0:T(8,128)(2,1)S(1)}, bf16[16,48,128]{2,1,0:T(8,128)(2,1)S(1)}, u32[]{:S(2)}, u32[]{:S(2)}) collective-permute-start(bf16[16,48,128]{2,1,0:T(8,128)(2,1)S(1)} %get-tuple-element.20), channel_id=1, source_target_pairs={{0,1},{1,0},{2,3},{3,2},{4,5},{5,4},{6,7},{7,6},{8,9},{9,8},{10,11... | collective-permute-start | bytes 589832 | tf_op jit(solution)/shard_map/ppermute | solution.py:221
  2.5 0.1 copy-done.4
  2.6 0.2 convert_reduce_fusion
  2.8 0.8 %collective-permute-done.taken_ref = bf16[16,48,128]{2,1,0:T(8,128)(2,1)S(1)} collective-permute-done((bf16[16,48,128]{2,1,0:T(8,128)(2,1)S(1)}, bf16[16,48,128]{2,1,0:T(8,128)(2,1)S(1)}, u32[]{:S(2)}, u32[]{:S(2)}) %collective-permute-start) | collective-permute-done | bytes 196640 | tf_op jit(solution)/shard_map/ppermute | solution.py:221
  3.5 0.0 copy-done.1
  3.5 0.0 copy-done.2
  3.5 0.0 copy-done.3
  3.6 13.5 %all_to_all.10.pieces_ref = bf16[16,48,128]{2,1,0:T(8,128)(2,1)S(1)} all-to-all(bf16[16,48,128]{2,1,0:T(8,128)(2,1)S(1)} %get-tuple-element.22), channel_id=1, replica_groups={{22,20,18,16,30,28,26,24,6,4,2,0,14,12,10,8},{23,21,19,17,31,29,27,25,7..., dimensions={0} | all-to-all | bytes 393216 | tf_op jit(solution)/shard_map/all_to_all | solution.py:225
  17.1 0.4 %shard_map.86 = (f32[48,128]{1,0:T(8,128)S(1)}, f32[48,128]{1,0:T(8,128)S(1)}, f32[48,128]{1,0:T(8,128)S(1)}, bf16[16,24,256]{2,1,0:T(8,128)(2,1)S(1)}) custom-call(s32[1,24]{1,0:T(1,128)S(1)} %get-tuple-element.21.position_ref, bf16[16,48,128]{2,1,0:T(8,128)(2,1)S(1)} %all_to_all.10.pieces_ref, f32[48,128]{1,0:T(8,128)S(1)} %get-tuple-element.23.master_ref, ...), custom_call_target="tpu_custom_call" | custom-call | tf_op jit(solution)/shard_map/pallas_call | solution.py:129
  17.6 10.5 %all_to_all.11.own_ref = bf16[16,24,256]{2,1,0:T(8,128)(2,1)S(1)} all-to-all(bf16[16,24,256]{2,1,0:T(8,128)(2,1)S(1)} %get-tuple-element.29), channel_id=1, replica_groups={{22,20,18,16,30,28,26,24,6,4,2,0,14,12,10,8},{23,21,19,17,31,29,27,25,7..., dimensions={0} | all-to-all | bytes 393216 | tf_op jit(solution)/shard_map/all_to_all | solution.py:228
  28.1 0.0 collective-permute-start.1
  28.1 1.4 %collective-permute-done.1.other_ref = bf16[16,24,256]{2,1,0:T(8,128)(2,1)S(1)} collective-permute-done((bf16[16,24,256]{2,1,0:T(8,128)(2,1)S(1)}, bf16[16,24,256]{2,1,0:T(8,128)(2,1)S(1)}, u32[]{:S(2)}, u32[]{:S(2)}) %collective-permute-start.1) | collective-permute-done | bytes 196640 | tf_op jit(solution)/shard_map/ppermute | solution.py:229
  29.6 0.9 %shard_map.87 = (f32[48,128]{1,0:T(8,128)}, f32[48,128]{1,0:T(8,128)}, f32[48,128]{1,0:T(8,128)}, bf16[24,8192]{1,0:T(8,128)(2,1)}) custom-call(s32[1,24]{1,0:T(1,128)S(1)} %get-tuple-element.21.position_ref, f32[48,128]{1,0:T(8,128)S(1)} %get-tuple-element.26.new_first_ref, f32[48,128]{1,0:T(8,128)S(1)} %get-tuple-element.27.new_second_ref, ...), custom_call_target="tpu_custom_call" | custom-call | tf_op jit(solution)/shard_map/pallas_call | solution.py:187
  (1 shorter events, 0.0 us)
Async XLA Ops:
  0.6 1.1 %copy-start = (bf16[1,196608]{1,0:T(2,128)(2,1)S(1)}, bf16[1,196608]{1,0:T(2,128)(2,1)}, u32[]{:S(2)}) copy-start(bf16[1,196608]{1,0:T(2,128)(2,1)} %grads_ref.1) | copy-start | bytes 1179652
  1.8 1.8 %copy-start.1 = (f32[6144]{0:T(1024)S(1)}, f32[6144]{0:T(1024)}, u32[]{:S(2)}) copy-start(f32[6144]{0:T(1024)} %param.6) | copy-start | bytes 73732
  1.8 1.8 %copy-start.2 = (f32[6144]{0:T(1024)S(1)}, f32[6144]{0:T(1024)}, u32[]{:S(2)}) copy-start(f32[6144]{0:T(1024)} %param.7) | copy-start | bytes 73732
  1.8 1.8 %copy-start.3 = (f32[6144]{0:T(1024)S(1)}, f32[6144]{0:T(1024)}, u32[]{:S(2)}) copy-start(f32[6144]{0:T(1024)} %param.8) | copy-start | bytes 73732
  1.9 0.7 %copy-start.4 = (s32[24]{0:T(128)S(1)}, s32[24]{0:T(128)}, u32[]{:S(2)}) copy-start(s32[24]{0:T(128)} %param.9) | copy-start | bytes 292
  1.9 1.6 %collective-permute-start = (bf16[16,48,128]{2,1,0:T(8,128)(2,1)S(1)}, bf16[16,48,128]{2,1,0:T(8,128)(2,1)S(1)}, u32[]{:S(2)}, u32[]{:S(2)}) collective-permute-start(bf16[16,48,128]{2,1,0:T(8,128)(2,1)S(1)} %get-tuple-element.20), channel_id=1, source_target_pairs={{0,1},{1,0},{2,3},{3,2},{4,5},{5,4},{6,7},{7,6},{8,9},{9,8},{10,11... | collective-permute-start | bytes 589832 | tf_op jit(solution)/shard_map/ppermute | solution.py:221
  28.1 1.4 %collective-permute-start.1 = (bf16[16,24,256]{2,1,0:T(8,128)(2,1)S(1)}, bf16[16,24,256]{2,1,0:T(8,128)(2,1)S(1)}, u32[]{:S(2)}, u32[]{:S(2)}) collective-permute-start(bf16[16,24,256]{2,1,0:T(8,128)(2,1)S(1)} %all_to_all.11.own_ref), channel_id=1, source_target_pairs={{0,1},{1,0},{2,3},{3,2},{4,5},{5,4},{6,7},{7,6},{8,9},{9,8},{10,11... | collective-permute-start | bytes 589832 | tf_op jit(solution)/shard_map/ppermute | solution.py:229

commit v15 on v10

--- a/solution.py
+++ b/solution.py
@@ -17,6 +17,7 @@
 second_correction = 1.0 - 0.95**20
 AXES = ("shard", "replica")
 LANES = 128
+FIRST = ((11, 15), (11, 15))
 
 
 def adam_step(gradient, master, first_moment, second_moment):
@@ -37,6 +38,14 @@
 
 def small(**more):
     return pltpu.CompilerParams(vmem_limit_bytes=6 * 2**20, **more)
+
+
+def groups(chips, firsts):
+    return [[2 * (k ^ first) + core for k in range(chips)] for core, first in enumerate(firsts)]
+
+
+def slot(chip, core, firsts):
+    return jnp.bitwise_xor(chip, jnp.where(core == 0, firsts[0], firsts[1]))
 
 
 def pack_kernel(grads_ref, kept_ref, sent_ref):
@@ -47,7 +56,7 @@
         for ref, place in ((kept_ref, core), (sent_ref, 1 - core)):
             start = pl.multiple_of((2 * k + place) * width, width)
             row = grads_ref[:, pl.ds(start, width)].astype(jnp.float32)
-            ref[k] = row.reshape(lines, lanes).astype(jnp.bfloat16)
+            ref[slot(k, place, FIRST[0])] = row.reshape(lines, lanes).astype(jnp.bfloat16)
 
 
 def pack(grads, chips, lines):
@@ -149,7 +158,8 @@
         for k in range(p * each, (p + 1) * each):
             for ref, place in ((own_ref, core), (other_ref, 1 - core)):
                 start = pl.multiple_of((2 * k + place) * width, width)
-                scaled_ref[:, pl.ds(start, width)] = (ref[k].astype(jnp.float32) * factor).astype(jnp.bfloat16)
+                scaled = ref[slot(k, place, FIRST[1])].astype(jnp.float32) * factor
+                scaled_ref[:, pl.ds(start, width)] = scaled.astype(jnp.bfloat16)
         part = pl.ds(p * 2 * each * width, 2 * each * width)
         copies.append(pltpu.make_async_copy(scaled_ref.at[:, part], copy_out.at[:, part], sems.at[3 + p]))
         copies[-1].start()
@@ -206,14 +216,18 @@
     shards, replicas = lax.axis_size("shard"), lax.axis_size("replica")
     devices = shards * replicas
     columns = owners.shape[0]
-    if replicas == 2 and master.shape[0] // LANES % 48 == 0:
+    if replicas == 2 and shards == 16 and master.shape[0] // LANES % 48 == 0:
         kept, sent = pack(grads, shards, master.shape[0] // LANES)
         taken = lax.ppermute(sent, "replica", [(0, 1), (1, 0)])
         states = (master, first_moment, second_moment)
         position, *states, pairs = add_pairs(kept, taken, flat_positions(owners), states)
-        pieces = lax.all_to_all(pairs, "shard", 0, 0, tiled=True)
+        pieces = lax.all_to_all(
+            pairs, AXES, 0, 0, tiled=True, axis_index_groups=groups(shards, FIRST[0])
+        )
         *updated, copies = middle(position, pieces, states, devices)
-        own = lax.all_to_all(copies, "shard", 0, 0, tiled=True)
+        own = lax.all_to_all(
+            copies, AXES, 0, 0, tiled=True, axis_index_groups=groups(shards, FIRST[1])
+        )
         other = lax.ppermute(own, "replica", [(0, 1), (1, 0)])
         *flat, model_copy = finish(position, *updated, own, other)
         return (*(x.reshape(-1) for x in flat), model_copy)

time: 34.9 us -> 33.1 us (0.948)
  blocking collectives: 28.2 us -> 26.4 us
    all_to_all x2, blocking collectives: 28.2 us -> 26.4 us  [the longest x1 14.5 us: on_device(): lax.all_to_all(pairs, AXES, 0, 0, tiled=True, axis_index_groups=groups(sh...]
where the time goes in v15:
time: 33.1 us; the launch traced here: 32.8 us
  blocking collectives  26.4 us (80%)
  waiting for transfers between devices  2.09 us (6%)
  Pallas kernels  1.57 us (5%)
  local copies, waits for them, and re-layouts  1.27 us (4%)
  between operations  0.67 us (2%)
  starting transfers between devices  0.63 us (2%)
    all_to_all x1, blocking collectives, on_device(): lax.all_to_all(pairs, AXES, 0, 0, tiled=True, axis_index_groups=groups(sh...  14.5 us
    all_to_all x1, blocking collectives, on_device(): lax.all_to_all(copies, AXES, 0, 0, tiled=True, axis_index_groups=groups(s...  11.9 us
    ppermute x1, waiting for transfers between devices, on_device(): other = lax.ppermute(own, 'replica', [(0, 1), (1, 0)])  1.33 us
    unnamed x10, local copies, waits for them, and re-layouts  1.27 us
    pallas_call x1, Pallas kernels, finish(): pl.pallas_call(finish_kernel, in_specs=[pl.BlockSpec(memory_space=pltpu.V...  0.93 us
    ppermute x1, waiting for transfers between devices, on_device(): taken = lax.ppermute(sent, 'replica', [(0, 1), (1, 0)])  0.76 us
  transfers between devices with their start and end apart: 2, of which 2 were waited for; matrix products, arithmetic and copies ran while one was open for 1% of the time, Pallas kernels for 0%

profile of v15, /device:TPU:0, one launch (start us, length us, event | category | flops | bytes accessed | tf_op | source)
XLA Modules:
  0.0 32.8 jit_solution(2408770095415617156)
XLA Ops:
  0.6 0.0 copy-start
  0.6 1.1 %copy-done = bf16[1,196608]{1,0:T(2,128)(2,1)S(1)} copy-done((bf16[1,196608]{1,0:T(2,128)(2,1)S(1)}, bf16[1,196608]{1,0:T(2,128)(2,1)}, u32[]{:S(2)}) %copy-start) | copy-done | bytes 393240
  1.8 0.0 copy-start.1
  1.8 0.0 copy-start.2
  1.8 0.0 copy-start.3
  1.8 0.1 shard_map.84
  1.9 0.0 copy-start.4
  1.9 0.5 %collective-permute-start = (bf16[16,48,128]{2,1,0:T(8,128)(2,1)S(1)}, bf16[16,48,128]{2,1,0:T(8,128)(2,1)S(1)}, u32[]{:S(2)}, u32[]{:S(2)}) collective-permute-start(bf16[16,48,128]{2,1,0:T(8,128)(2,1)S(1)} %get-tuple-element.20), channel_id=1, source_target_pairs={{0,1},{1,0},{2,3},{3,2},{4,5},{5,4},{6,7},{7,6},{8,9},{9,8},{10,11... | collective-permute-start | bytes 589832 | tf_op jit(solution)/shard_map/ppermute | solution.py:221
  2.5 0.1 copy-done.4
  2.6 0.2 convert_reduce_fusion
  2.8 0.8 %collective-permute-done.taken_ref = bf16[16,48,128]{2,1,0:T(8,128)(2,1)S(1)} collective-permute-done((bf16[16,48,128]{2,1,0:T(8,128)(2,1)S(1)}, bf16[16,48,128]{2,1,0:T(8,128)(2,1)S(1)}, u32[]{:S(2)}, u32[]{:S(2)}) %collective-permute-start) | collective-permute-done | bytes 196640 | tf_op jit(solution)/shard_map/ppermute | solution.py:221
  3.5 0.0 copy-done.1
  3.5 0.0 copy-done.2
  3.5 0.0 copy-done.3
  3.6 14.5 %all_to_all.10.pieces_ref = bf16[16,48,128]{2,1,0:T(8,128)(2,1)S(1)} all-to-all(bf16[16,48,128]{2,1,0:T(8,128)(2,1)S(1)} %get-tuple-element.22), channel_id=1, replica_groups={{22,20,18,16,30,28,26,24,6,4,2,0,14,12,10,8},{31,29,27,25,23,21,19,17,1..., dimensions={0} | all-to-all | bytes 393216 | tf_op jit(solution)/shard_map/all_to_all | solution.py:224
  18.1 0.4 %shard_map.86 = (f32[48,128]{1,0:T(8,128)S(1)}, f32[48,128]{1,0:T(8,128)S(1)}, f32[48,128]{1,0:T(8,128)S(1)}, bf16[16,24,256]{2,1,0:T(8,128)(2,1)S(1)}) custom-call(s32[1,24]{1,0:T(1,128)S(1)} %get-tuple-element.21.position_ref, bf16[16,48,128]{2,1,0:T(8,128)(2,1)S(1)} %all_to_all.10.pieces_ref, f32[48,128]{1,0:T(8,128)S(1)} %get-tuple-element.23.master_ref, ...), custom_call_target="tpu_custom_call" | custom-call | tf_op jit(solution)/shard_map/pallas_call | solution.py:130
  18.5 11.9 %all_to_all.11.own_ref = bf16[16,24,256]{2,1,0:T(8,128)(2,1)S(1)} all-to-all(bf16[16,24,256]{2,1,0:T(8,128)(2,1)S(1)} %get-tuple-element.29), channel_id=1, replica_groups={{22,20,18,16,30,28,26,24,6,4,2,0,14,12,10,8},{31,29,27,25,23,21,19,17,1..., dimensions={0} | all-to-all | bytes 393216 | tf_op jit(solution)/shard_map/all_to_all | solution.py:228
  30.5 0.1 collective-permute-start.1
  30.6 1.3 %collective-permute-done.1.other_ref = bf16[16,24,256]{2,1,0:T(8,128)(2,1)S(1)} collective-permute-done((bf16[16,24,256]{2,1,0:T(8,128)(2,1)S(1)}, bf16[16,24,256]{2,1,0:T(8,128)(2,1)S(1)}, u32[]{:S(2)}, u32[]{:S(2)}) %collective-permute-start.1) | collective-permute-done | bytes 196640 | tf_op jit(solution)/shard_map/ppermute | solution.py:231
  31.9 0.9 %shard_map.87 = (f32[48,128]{1,0:T(8,128)}, f32[48,128]{1,0:T(8,128)}, f32[48,128]{1,0:T(8,128)}, bf16[24,8192]{1,0:T(8,128)(2,1)}) custom-call(s32[1,24]{1,0:T(1,128)S(1)} %get-tuple-element.21.position_ref, f32[48,128]{1,0:T(8,128)S(1)} %get-tuple-element.26.new_first_ref, f32[48,128]{1,0:T(8,128)S(1)} %get-tuple-element.27.new_second_ref, ...), custom_call_target="tpu_custom_call" | custom-call | tf_op jit(solution)/shard_map/pallas_call | solution.py:187
  (1 shorter events, 0.0 us)
Async XLA Ops:
  0.6 1.1 %copy-start = (bf16[1,196608]{1,0:T(2,128)(2,1)S(1)}, bf16[1,196608]{1,0:T(2,128)(2,1)}, u32[]{:S(2)}) copy-start(bf16[1,196608]{1,0:T(2,128)(2,1)} %grads_ref.1) | copy-start | bytes 1179652
  1.8 1.8 %copy-start.1 = (f32[6144]{0:T(1024)S(1)}, f32[6144]{0:T(1024)}, u32[]{:S(2)}) copy-start(f32[6144]{0:T(1024)} %param.6) | copy-start | bytes 73732
  1.8 1.8 %copy-start.2 = (f32[6144]{0:T(1024)S(1)}, f32[6144]{0:T(1024)}, u32[]{:S(2)}) copy-start(f32[6144]{0:T(1024)} %param.7) | copy-start | bytes 73732
  1.8 1.8 %copy-start.3 = (f32[6144]{0:T(1024)S(1)}, f32[6144]{0:T(1024)}, u32[]{:S(2)}) copy-start(f32[6144]{0:T(1024)} %param.8) | copy-start | bytes 73732
  1.9 0.7 %copy-start.4 = (s32[24]{0:T(128)S(1)}, s32[24]{0:T(128)}, u32[]{:S(2)}) copy-start(s32[24]{0:T(128)} %param.9) | copy-start | bytes 292
  1.9 1.6 %collective-permute-start = (bf16[16,48,128]{2,1,0:T(8,128)(2,1)S(1)}, bf16[16,48,128]{2,1,0:T(8,128)(2,1)S(1)}, u32[]{:S(2)}, u32[]{:S(2)}) collective-permute-start(bf16[16,48,128]{2,1,0:T(8,128)(2,1)S(1)} %get-tuple-element.20), channel_id=1, source_target_pairs={{0,1},{1,0},{2,3},{3,2},{4,5},{5,4},{6,7},{7,6},{8,9},{9,8},{10,11... | collective-permute-start | bytes 589832 | tf_op jit(solution)/shard_map/ppermute | solution.py:221
  30.5 1.4 %collective-permute-start.1 = (bf16[16,24,256]{2,1,0:T(8,128)(2,1)S(1)}, bf16[16,24,256]{2,1,0:T(8,128)(2,1)S(1)}, u32[]{:S(2)}, u32[]{:S(2)}) collective-permute-start(bf16[16,24,256]{2,1,0:T(8,128)(2,1)S(1)} %all_to_all.11.own_ref), channel_id=1, source_target_pairs={{0,1},{1,0},{2,3},{3,2},{4,5},{5,4},{6,7},{7,6},{8,9},{9,8},{10,11... | collective-permute-start | bytes 589832 | tf_op jit(solution)/shard_map/ppermute | solution.py:231

commit v16 on v10

--- a/solution.py
+++ b/solution.py
@@ -17,6 +17,8 @@
 second_correction = 1.0 - 0.95**20
 AXES = ("shard", "replica")
 LANES = 128
+FIRST = 11
+PLANE = 4
 
 
 def adam_step(gradient, master, first_moment, second_moment):
@@ -37,6 +39,24 @@
 
 def small(**more):
     return pltpu.CompilerParams(vmem_limit_bytes=6 * 2**20, **more)
+
+
+def place_of(chip):
+    by_layer = chip ^ FIRST
+    return by_layer, by_layer % PLANE * PLANE + by_layer // PLANE
+
+
+def groups(chips):
+    lists = [[0] * chips, [0] * chips]
+    for chip in range(chips):
+        for core, place in enumerate(place_of(chip)):
+            lists[core][place] = 2 * chip + core
+    return lists
+
+
+def slot(chip, core):
+    places = place_of(chip)
+    return jnp.where(core == 0, places[0], places[1])
 
 
 def pack_kernel(grads_ref, kept_ref, sent_ref):
@@ -47,7 +67,7 @@
         for ref, place in ((kept_ref, core), (sent_ref, 1 - core)):
             start = pl.multiple_of((2 * k + place) * width, width)
             row = grads_ref[:, pl.ds(start, width)].astype(jnp.float32)
-            ref[k] = row.reshape(lines, lanes).astype(jnp.bfloat16)
+            ref[slot(k, place)] = row.reshape(lines, lanes).astype(jnp.bfloat16)
 
 
 def pack(grads, chips, lines):
@@ -149,7 +169,8 @@
         for k in range(p * each, (p + 1) * each):
             for ref, place in ((own_ref, core), (other_ref, 1 - core)):
                 start = pl.multiple_of((2 * k + place) * width, width)
-                scaled_ref[:, pl.ds(start, width)] = (ref[k].astype(jnp.float32) * factor).astype(jnp.bfloat16)
+                scaled = ref[slot(k, place)].astype(jnp.float32) * factor
+                scaled_ref[:, pl.ds(start, width)] = scaled.astype(jnp.bfloat16)
         part = pl.ds(p * 2 * each * width, 2 * each * width)
         copies.append(pltpu.make_async_copy(scaled_ref.at[:, part], copy_out.at[:, part], sems.at[3 + p]))
         copies[-1].start()
@@ -206,14 +227,14 @@
     shards, replicas = lax.axis_size("shard"), lax.axis_size("replica")
     devices = shards * replicas
     columns = owners.shape[0]
-    if replicas == 2 and master.shape[0] // LANES % 48 == 0:
+    if replicas == 2 and shards == 16 and master.shape[0] // LANES % 48 == 0:
         kept, sent = pack(grads, shards, master.shape[0] // LANES)
         taken = lax.ppermute(sent, "replica", [(0, 1), (1, 0)])
         states = (master, first_moment, second_moment)
         position, *states, pairs = add_pairs(kept, taken, flat_positions(owners), states)
-        pieces = lax.all_to_all(pairs, "shard", 0, 0, tiled=True)
+        pieces = lax.all_to_all(pairs, AXES, 0, 0, tiled=True, axis_index_groups=groups(shards))
         *updated, copies = middle(position, pieces, states, devices)
-        own = lax.all_to_all(copies, "shard", 0, 0, tiled=True)
+        own = lax.all_to_all(copies, AXES, 0, 0, tiled=True, axis_index_groups=groups(shards))
         other = lax.ppermute(own, "replica", [(0, 1), (1, 0)])
         *flat, model_copy = finish(position, *updated, own, other)
         return (*(x.reshape(-1) for x in flat), model_copy)

time: 34.9 us -> 30.7 us (0.88)
  blocking collectives: 28.2 us -> 24 us
    all_to_all x2, blocking collectives: 28.2 us -> 24 us  [the longest x1 13.6 us: on_device(): lax.all_to_all(pairs, AXES, 0, 0, tiled=True, axis_index_groups=groups(sh...]
where the time goes in v16:
time: 30.7 us; the launch traced here: 30.4 us
  blocking collectives  24 us (78%)
  waiting for transfers between devices  2.2 us (7%)
  Pallas kernels  1.57 us (5%)
  local copies, waits for them, and re-layouts  1.27 us (4%)
  between operations  0.67 us (2%)
  starting transfers between devices  0.52 us (2%)
    all_to_all x1, blocking collectives, on_device(): lax.all_to_all(pairs, AXES, 0, 0, tiled=True, axis_index_groups=groups(sh...  13.6 us
    all_to_all x1, blocking collectives, on_device(): lax.all_to_all(copies, AXES, 0, 0, tiled=True, axis_index_groups=groups(s...  10.4 us
    ppermute x1, waiting for transfers between devices, on_device(): other = lax.ppermute(own, 'replica', [(0, 1), (1, 0)])  1.44 us
    unnamed x10, local copies, waits for them, and re-layouts  1.27 us
    pallas_call x1, Pallas kernels, finish(): pl.pallas_call(finish_kernel, in_specs=[pl.BlockSpec(memory_space=pltpu.V...  0.93 us
    ppermute x1, waiting for transfers between devices, on_device(): taken = lax.ppermute(sent, 'replica', [(0, 1), (1, 0)])  0.76 us
  transfers between devices with their start and end apart: 2, of which 2 were waited for; matrix products, arithmetic and copies ran while one was open for 1% of the time, Pallas kernels for 0%

profile of v16, /device:TPU:0, one launch (start us, length us, event | category | flops | bytes accessed | tf_op | source)
XLA Modules:
  0.0 30.4 jit_solution(15929753820397322990)
XLA Ops:
  0.6 0.0 copy-start
  0.6 1.1 %copy-done = bf16[1,196608]{1,0:T(2,128)(2,1)S(1)} copy-done((bf16[1,196608]{1,0:T(2,128)(2,1)S(1)}, bf16[1,196608]{1,0:T(2,128)(2,1)}, u32[]{:S(2)}) %copy-start) | copy-done | bytes 393240
  1.8 0.0 copy-start.1
  1.8 0.0 copy-start.2
  1.8 0.0 copy-start.3
  1.8 0.1 shard_map.84
  1.9 0.0 copy-start.4
  1.9 0.5 %collective-permute-start = (bf16[16,48,128]{2,1,0:T(8,128)(2,1)S(1)}, bf16[16,48,128]{2,1,0:T(8,128)(2,1)S(1)}, u32[]{:S(2)}, u32[]{:S(2)}) collective-permute-start(bf16[16,48,128]{2,1,0:T(8,128)(2,1)S(1)} %get-tuple-element.20), channel_id=1, source_target_pairs={{0,1},{1,0},{2,3},{3,2},{4,5},{5,4},{6,7},{7,6},{8,9},{9,8},{10,11... | collective-permute-start | bytes 589832 | tf_op jit(solution)/shard_map/ppermute | solution.py:232
  2.5 0.1 copy-done.4
  2.6 0.2 convert_reduce_fusion
  2.8 0.8 %collective-permute-done.taken_ref = bf16[16,48,128]{2,1,0:T(8,128)(2,1)S(1)} collective-permute-done((bf16[16,48,128]{2,1,0:T(8,128)(2,1)S(1)}, bf16[16,48,128]{2,1,0:T(8,128)(2,1)S(1)}, u32[]{:S(2)}, u32[]{:S(2)}) %collective-permute-start) | collective-permute-done | bytes 196640 | tf_op jit(solution)/shard_map/ppermute | solution.py:232
  3.5 0.0 copy-done.1
  3.5 0.0 copy-done.2
  3.5 0.0 copy-done.3
  3.6 13.6 %all_to_all.10.pieces_ref = bf16[16,48,128]{2,1,0:T(8,128)(2,1)S(1)} all-to-all(bf16[16,48,128]{2,1,0:T(8,128)(2,1)S(1)} %get-tuple-element.22), channel_id=1, replica_groups={{22,20,18,16,30,28,26,24,6,4,2,0,14,12,10,8},{23,31,7,15,21,29,5,13,19,..., dimensions={0} | all-to-all | bytes 393216 | tf_op jit(solution)/shard_map/all_to_all | solution.py:235
  17.2 0.4 %shard_map.86 = (f32[48,128]{1,0:T(8,128)S(1)}, f32[48,128]{1,0:T(8,128)S(1)}, f32[48,128]{1,0:T(8,128)S(1)}, bf16[16,24,256]{2,1,0:T(8,128)(2,1)S(1)}) custom-call(s32[1,24]{1,0:T(1,128)S(1)} %get-tuple-element.21.position_ref, bf16[16,48,128]{2,1,0:T(8,128)(2,1)S(1)} %all_to_all.10.pieces_ref, f32[48,128]{1,0:T(8,128)S(1)} %get-tuple-element.23.master_ref, ...), custom_call_target="tpu_custom_call" | custom-call | tf_op jit(solution)/shard_map/pallas_call | solution.py:141
  17.6 10.4 %all_to_all.11.own_ref = bf16[16,24,256]{2,1,0:T(8,128)(2,1)S(1)} all-to-all(bf16[16,24,256]{2,1,0:T(8,128)(2,1)S(1)} %get-tuple-element.29), channel_id=1, replica_groups={{22,20,18,16,30,28,26,24,6,4,2,0,14,12,10,8},{23,31,7,15,21,29,5,13,19,..., dimensions={0} | all-to-all | bytes 393216 | tf_op jit(solution)/shard_map/all_to_all | solution.py:237
  28.1 0.0 collective-permute-start.1
  28.1 1.4 %collective-permute-done.1.other_ref = bf16[16,24,256]{2,1,0:T(8,128)(2,1)S(1)} collective-permute-done((bf16[16,24,256]{2,1,0:T(8,128)(2,1)S(1)}, bf16[16,24,256]{2,1,0:T(8,128)(2,1)S(1)}, u32[]{:S(2)}, u32[]{:S(2)}) %collective-permute-start.1) | collective-permute-done | bytes 196640 | tf_op jit(solution)/shard_map/ppermute | solution.py:238
  29.5 0.9 %shard_map.87 = (f32[48,128]{1,0:T(8,128)}, f32[48,128]{1,0:T(8,128)}, f32[48,128]{1,0:T(8,128)}, bf16[24,8192]{1,0:T(8,128)(2,1)}) custom-call(s32[1,24]{1,0:T(1,128)S(1)} %get-tuple-element.21.position_ref, f32[48,128]{1,0:T(8,128)S(1)} %get-tuple-element.26.new_first_ref, f32[48,128]{1,0:T(8,128)S(1)} %get-tuple-element.27.new_second_ref, ...), custom_call_target="tpu_custom_call" | custom-call | tf_op jit(solution)/shard_map/pallas_call | solution.py:198
  (1 shorter events, 0.0 us)
Async XLA Ops:
  0.6 1.1 %copy-start = (bf16[1,196608]{1,0:T(2,128)(2,1)S(1)}, bf16[1,196608]{1,0:T(2,128)(2,1)}, u32[]{:S(2)}) copy-start(bf16[1,196608]{1,0:T(2,128)(2,1)} %grads_ref.1) | copy-start | bytes 1179652
  1.8 1.8 %copy-start.1 = (f32[6144]{0:T(1024)S(1)}, f32[6144]{0:T(1024)}, u32[]{:S(2)}) copy-start(f32[6144]{0:T(1024)} %param.6) | copy-start | bytes 73732
  1.8 1.8 %copy-start.2 = (f32[6144]{0:T(1024)S(1)}, f32[6144]{0:T(1024)}, u32[]{:S(2)}) copy-start(f32[6144]{0:T(1024)} %param.7) | copy-start | bytes 73732
  1.8 1.8 %copy-start.3 = (f32[6144]{0:T(1024)S(1)}, f32[6144]{0:T(1024)}, u32[]{:S(2)}) copy-start(f32[6144]{0:T(1024)} %param.8) | copy-start | bytes 73732
  1.9 0.7 %copy-start.4 = (s32[24]{0:T(128)S(1)}, s32[24]{0:T(128)}, u32[]{:S(2)}) copy-start(s32[24]{0:T(128)} %param.9) | copy-start | bytes 292
  1.9 1.6 %collective-permute-start = (bf16[16,48,128]{2,1,0:T(8,128)(2,1)S(1)}, bf16[16,48,128]{2,1,0:T(8,128)(2,1)S(1)}, u32[]{:S(2)}, u32[]{:S(2)}) collective-permute-start(bf16[16,48,128]{2,1,0:T(8,128)(2,1)S(1)} %get-tuple-element.20), channel_id=1, source_target_pairs={{0,1},{1,0},{2,3},{3,2},{4,5},{5,4},{6,7},{7,6},{8,9},{9,8},{10,11... | collective-permute-start | bytes 589832 | tf_op jit(solution)/shard_map/ppermute | solution.py:232
  28.1 1.4 %collective-permute-start.1 = (bf16[16,24,256]{2,1,0:T(8,128)(2,1)S(1)}, bf16[16,24,256]{2,1,0:T(8,128)(2,1)S(1)}, u32[]{:S(2)}, u32[]{:S(2)}) collective-permute-start(bf16[16,24,256]{2,1,0:T(8,128)(2,1)S(1)} %all_to_all.11.own_ref), channel_id=1, source_target_pairs={{0,1},{1,0},{2,3},{3,2},{4,5},{5,4},{6,7},{7,6},{8,9},{9,8},{10,11... | collective-permute-start | bytes 589832 | tf_op jit(solution)/shard_map/ppermute | solution.py:238

commit v17 on v16

--- a/solution.py
+++ b/solution.py
@@ -43,7 +43,8 @@
 
 def place_of(chip):
     by_layer = chip ^ FIRST
-    return by_layer, by_layer % PLANE * PLANE + by_layer // PLANE
+    by_column = by_layer % PLANE * PLANE + by_layer // PLANE
+    return by_column, by_column
 
 
 def groups(chips):

time: 30.7 us -> 31 us (level)
  blocking collectives: 24 us -> 24.4 us
    all_to_all x1, blocking collectives: 13.6 us -> 14 us  [on_device(): lax.all_to_all(pairs, AXES, 0, 0, tiled=True, axis_index_groups=groups(sh...]
where the time goes in v17:
time: 31 us; the launch traced here: 30.8 us
  blocking collectives  24.4 us (79%)
  waiting for transfers between devices  2.2 us (7%)
  Pallas kernels  1.56 us (5%)
  local copies, waits for them, and re-layouts  1.27 us (4%)
  between operations  0.67 us (2%)
  starting transfers between devices  0.52 us (2%)
    all_to_all x1, blocking collectives, on_device(): lax.all_to_all(pairs, AXES, 0, 0, tiled=True, axis_index_groups=groups(sh...  14 us
    all_to_all x1, blocking collectives, on_device(): lax.all_to_all(copies, AXES, 0, 0, tiled=True, axis_index_groups=groups(s...  10.3 us
    ppermute x1, waiting for transfers between devices, on_device(): other = lax.ppermute(own, 'replica', [(0, 1), (1, 0)])  1.44 us
    unnamed x10, local copies, waits for them, and re-layouts  1.27 us
    pallas_call x1, Pallas kernels, finish(): pl.pallas_call(finish_kernel, in_specs=[pl.BlockSpec(memory_space=pltpu.V...  0.93 us
    ppermute x1, waiting for transfers between devices, on_device(): taken = lax.ppermute(sent, 'replica', [(0, 1), (1, 0)])  0.76 us
  transfers between devices with their start and end apart: 2, of which 2 were waited for; matrix products, arithmetic and copies ran while one was open for 1% of the time, Pallas kernels for 0%

profile of v17, /device:TPU:0, one launch (start us, length us, event | category | flops | bytes accessed | tf_op | source)
XLA Modules:
  0.0 30.8 jit_solution(11618934885145699938)
XLA Ops:
  0.6 0.0 copy-start
  0.6 1.1 %copy-done = bf16[1,196608]{1,0:T(2,128)(2,1)S(1)} copy-done((bf16[1,196608]{1,0:T(2,128)(2,1)S(1)}, bf16[1,196608]{1,0:T(2,128)(2,1)}, u32[]{:S(2)}) %copy-start) | copy-done | bytes 393240
  1.8 0.0 copy-start.1
  1.8 0.0 copy-start.2
  1.8 0.0 copy-start.3
  1.8 0.1 shard_map.84
  1.9 0.0 copy-start.4
  1.9 0.5 %collective-permute-start = (bf16[16,48,128]{2,1,0:T(8,128)(2,1)S(1)}, bf16[16,48,128]{2,1,0:T(8,128)(2,1)S(1)}, u32[]{:S(2)}, u32[]{:S(2)}) collective-permute-start(bf16[16,48,128]{2,1,0:T(8,128)(2,1)S(1)} %get-tuple-element.20), channel_id=1, source_target_pairs={{0,1},{1,0},{2,3},{3,2},{4,5},{5,4},{6,7},{7,6},{8,9},{9,8},{10,11... | collective-permute-start | bytes 589832 | tf_op jit(solution)/shard_map/ppermute | solution.py:233
  2.5 0.1 copy-done.4
  2.6 0.2 convert_reduce_fusion
  2.8 0.8 %collective-permute-done.taken_ref = bf16[16,48,128]{2,1,0:T(8,128)(2,1)S(1)} collective-permute-done((bf16[16,48,128]{2,1,0:T(8,128)(2,1)S(1)}, bf16[16,48,128]{2,1,0:T(8,128)(2,1)S(1)}, u32[]{:S(2)}, u32[]{:S(2)}) %collective-permute-start) | collective-permute-done | bytes 196640 | tf_op jit(solution)/shard_map/ppermute | solution.py:233
  3.5 0.0 copy-done.1
  3.5 0.0 copy-done.2
  3.5 0.0 copy-done.3
  3.6 14.0 %all_to_all.10.pieces_ref = bf16[16,48,128]{2,1,0:T(8,128)(2,1)S(1)} all-to-all(bf16[16,48,128]{2,1,0:T(8,128)(2,1)S(1)} %get-tuple-element.22), channel_id=1, replica_groups={{22,30,6,14,20,28,4,12,18,26,2,10,16,24,0,8},{23,31,7,15,21,29,5,13,19,..., dimensions={0} | all-to-all | bytes 393216 | tf_op jit(solution)/shard_map/all_to_all | solution.py:236
  17.6 0.4 %shard_map.86 = (f32[48,128]{1,0:T(8,128)S(1)}, f32[48,128]{1,0:T(8,128)S(1)}, f32[48,128]{1,0:T(8,128)S(1)}, bf16[16,24,256]{2,1,0:T(8,128)(2,1)S(1)}) custom-call(s32[1,24]{1,0:T(1,128)S(1)} %get-tuple-element.21.position_ref, bf16[16,48,128]{2,1,0:T(8,128)(2,1)S(1)} %all_to_all.10.pieces_ref, f32[48,128]{1,0:T(8,128)S(1)} %get-tuple-element.23.master_ref, ...), custom_call_target="tpu_custom_call" | custom-call | tf_op jit(solution)/shard_map/pallas_call | solution.py:142
  18.0 10.3 %all_to_all.11.own_ref = bf16[16,24,256]{2,1,0:T(8,128)(2,1)S(1)} all-to-all(bf16[16,24,256]{2,1,0:T(8,128)(2,1)S(1)} %get-tuple-element.29), channel_id=1, replica_groups={{22,30,6,14,20,28,4,12,18,26,2,10,16,24,0,8},{23,31,7,15,21,29,5,13,19,..., dimensions={0} | all-to-all | bytes 393216 | tf_op jit(solution)/shard_map/all_to_all | solution.py:238
  28.4 0.0 collective-permute-start.1
  28.4 1.4 %collective-permute-done.1.other_ref = bf16[16,24,256]{2,1,0:T(8,128)(2,1)S(1)} collective-permute-done((bf16[16,24,256]{2,1,0:T(8,128)(2,1)S(1)}, bf16[16,24,256]{2,1,0:T(8,128)(2,1)S(1)}, u32[]{:S(2)}, u32[]{:S(2)}) %collective-permute-start.1) | collective-permute-done | bytes 196640 | tf_op jit(solution)/shard_map/ppermute | solution.py:239
  29.8 0.9 %shard_map.87 = (f32[48,128]{1,0:T(8,128)}, f32[48,128]{1,0:T(8,128)}, f32[48,128]{1,0:T(8,128)}, bf16[24,8192]{1,0:T(8,128)(2,1)}) custom-call(s32[1,24]{1,0:T(1,128)S(1)} %get-tuple-element.21.position_ref, f32[48,128]{1,0:T(8,128)S(1)} %get-tuple-element.26.new_first_ref, f32[48,128]{1,0:T(8,128)S(1)} %get-tuple-element.27.new_second_ref, ...), custom_call_target="tpu_custom_call" | custom-call | tf_op jit(solution)/shard_map/pallas_call | solution.py:199
  (1 shorter events, 0.0 us)
Async XLA Ops:
  0.6 1.1 %copy-start = (bf16[1,196608]{1,0:T(2,128)(2,1)S(1)}, bf16[1,196608]{1,0:T(2,128)(2,1)}, u32[]{:S(2)}) copy-start(bf16[1,196608]{1,0:T(2,128)(2,1)} %grads_ref.1) | copy-start | bytes 1179652
  1.8 1.8 %copy-start.1 = (f32[6144]{0:T(1024)S(1)}, f32[6144]{0:T(1024)}, u32[]{:S(2)}) copy-start(f32[6144]{0:T(1024)} %param.6) | copy-start | bytes 73732
  1.8 1.8 %copy-start.2 = (f32[6144]{0:T(1024)S(1)}, f32[6144]{0:T(1024)}, u32[]{:S(2)}) copy-start(f32[6144]{0:T(1024)} %param.7) | copy-start | bytes 73732
  1.8 1.8 %copy-start.3 = (f32[6144]{0:T(1024)S(1)}, f32[6144]{0:T(1024)}, u32[]{:S(2)}) copy-start(f32[6144]{0:T(1024)} %param.8) | copy-start | bytes 73732
  1.9 0.7 %copy-start.4 = (s32[24]{0:T(128)S(1)}, s32[24]{0:T(128)}, u32[]{:S(2)}) copy-start(s32[24]{0:T(128)} %param.9) | copy-start | bytes 292
  1.9 1.6 %collective-permute-start = (bf16[16,48,128]{2,1,0:T(8,128)(2,1)S(1)}, bf16[16,48,128]{2,1,0:T(8,128)(2,1)S(1)}, u32[]{:S(2)}, u32[]{:S(2)}) collective-permute-start(bf16[16,48,128]{2,1,0:T(8,128)(2,1)S(1)} %get-tuple-element.20), channel_id=1, source_target_pairs={{0,1},{1,0},{2,3},{3,2},{4,5},{5,4},{6,7},{7,6},{8,9},{9,8},{10,11... | collective-permute-start | bytes 589832 | tf_op jit(solution)/shard_map/ppermute | solution.py:233
  28.4 1.4 %collective-permute-start.1 = (bf16[16,24,256]{2,1,0:T(8,128)(2,1)S(1)}, bf16[16,24,256]{2,1,0:T(8,128)(2,1)S(1)}, u32[]{:S(2)}, u32[]{:S(2)}) collective-permute-start(bf16[16,24,256]{2,1,0:T(8,128)(2,1)S(1)} %all_to_all.11.own_ref), channel_id=1, source_target_pairs={{0,1},{1,0},{2,3},{3,2},{4,5},{5,4},{6,7},{7,6},{8,9},{9,8},{10,11... | collective-permute-start | bytes 589832 | tf_op jit(solution)/shard_map/ppermute | solution.py:239

commit v18 on v16

--- a/solution.py
+++ b/solution.py
@@ -17,7 +17,7 @@
 second_correction = 1.0 - 0.95**20
 AXES = ("shard", "replica")
 LANES = 128
-FIRST = 11
+FIRST = (11, 7)
 PLANE = 4
 
 
@@ -41,21 +41,21 @@
     return pltpu.CompilerParams(vmem_limit_bytes=6 * 2**20, **more)
 
 
-def place_of(chip):
-    by_layer = chip ^ FIRST
+def place_of(chip, first):
+    by_layer = chip ^ first
     return by_layer, by_layer % PLANE * PLANE + by_layer // PLANE
 
 
-def groups(chips):
+def groups(chips, first):
     lists = [[0] * chips, [0] * chips]
     for chip in range(chips):
-        for core, place in enumerate(place_of(chip)):
+        for core, place in enumerate(place_of(chip, first)):
             lists[core][place] = 2 * chip + core
     return lists
 
 
-def slot(chip, core):
-    places = place_of(chip)
+def slot(chip, core, first):
+    places = place_of(chip, first)
     return jnp.where(core == 0, places[0], places[1])
 
 
@@ -67,7 +67,7 @@
         for ref, place in ((kept_ref, core), (sent_ref, 1 - core)):
             start = pl.multiple_of((2 * k + place) * width, width)
             row = grads_ref[:, pl.ds(start, width)].astype(jnp.float32)
-            ref[slot(k, place)] = row.reshape(lines, lanes).astype(jnp.bfloat16)
+            ref[slot(k, place, FIRST[0])] = row.reshape(lines, lanes).astype(jnp.bfloat16)
 
 
 def pack(grads, chips, lines):
@@ -169,7 +169,7 @@
         for k in range(p * each, (p + 1) * each):
             for ref, place in ((own_ref, core), (other_ref, 1 - core)):
                 start = pl.multiple_of((2 * k + place) * width, width)
-                scaled = ref[slot(k, place)].astype(jnp.float32) * factor
+                scaled = ref[slot(k, place, FIRST[1])].astype(jnp.float32) * factor
                 scaled_ref[:, pl.ds(start, width)] = scaled.astype(jnp.bfloat16)
         part = pl.ds(p * 2 * each * width, 2 * each * width)
         copies.append(pltpu.make_async_copy(scaled_ref.at[:, part], copy_out.at[:, part], sems.at[3 + p]))
@@ -232,9 +232,11 @@
         taken = lax.ppermute(sent, "replica", [(0, 1), (1, 0)])
         states = (master, first_moment, second_moment)
         position, *states, pairs = add_pairs(kept, taken, flat_positions(owners), states)
-        pieces = lax.all_to_all(pairs, AXES, 0, 0, tiled=True, axis_index_groups=groups(shards))
+        lists = groups(shards, FIRST[0])
+        pieces = lax.all_to_all(pairs, AXES, 0, 0, tiled=True, axis_index_groups=lists)
         *updated, copies = middle(position, pieces, states, devices)
-        own = lax.all_to_all(copies, AXES, 0, 0, tiled=True, axis_index_groups=groups(shards))
+        lists = groups(shards, FIRST[1])
+        own = lax.all_to_all(copies, AXES, 0, 0, tiled=True, axis_index_groups=lists)
         other = lax.ppermute(own, "replica", [(0, 1), (1, 0)])
         *flat, model_copy = finish(position, *updated, own, other)
         return (*(x.reshape(-1) for x in flat), model_copy)

time: 30.7 us -> 32.2 us (1.049)
  blocking collectives: 24 us -> 25.5 us
    all_to_all x2, blocking collectives: 24 us -> 25.5 us  [the longest x1 13.6 us: on_device(): lax.all_to_all(pairs, AXES, 0, 0, tiled=True, axis_index_groups=lists)]
where the time goes in v18:
time: 32.2 us; the launch traced here: 31.9 us
  blocking collectives  25.5 us (79%)
  waiting for transfers between devices  2.2 us (7%)
  Pallas kernels  1.57 us (5%)
  local copies, waits for them, and re-layouts  1.27 us (4%)
  between operations  0.67 us (2%)
  starting transfers between devices  0.52 us (2%)
    all_to_all x1, blocking collectives, on_device(): lax.all_to_all(pairs, AXES, 0, 0, tiled=True, axis_index_groups=lists)  13.6 us
    all_to_all x1, blocking collectives, on_device(): lax.all_to_all(copies, AXES, 0, 0, tiled=True, axis_index_groups=lists)  11.9 us
    ppermute x1, waiting for transfers between devices, on_device(): other = lax.ppermute(own, 'replica', [(0, 1), (1, 0)])  1.44 us
    unnamed x10, local copies, waits for them, and re-layouts  1.27 us
    pallas_call x1, Pallas kernels, finish(): pl.pallas_call(finish_kernel, in_specs=[pl.BlockSpec(memory_space=pltpu.V...  0.93 us
    ppermute x1, waiting for transfers between devices, on_device(): taken = lax.ppermute(sent, 'replica', [(0, 1), (1, 0)])  0.76 us
  transfers between devices with their start and end apart: 2, of which 2 were waited for; matrix products, arithmetic and copies ran while one was open for 1% of the time, Pallas kernels for 0%

profile of v18, /device:TPU:0, one launch (start us, length us, event | category | flops | bytes accessed | tf_op | source)
XLA Modules:
  0.0 31.9 jit_solution(832979141168648574)
XLA Ops:
  0.6 0.0 copy-start
  0.6 1.1 %copy-done = bf16[1,196608]{1,0:T(2,128)(2,1)S(1)} copy-done((bf16[1,196608]{1,0:T(2,128)(2,1)S(1)}, bf16[1,196608]{1,0:T(2,128)(2,1)}, u32[]{:S(2)}) %copy-start) | copy-done | bytes 393240
  1.8 0.0 copy-start.1
  1.8 0.0 copy-start.2
  1.8 0.0 copy-start.3
  1.8 0.1 shard_map.84
  1.9 0.0 copy-start.4
  1.9 0.5 %collective-permute-start = (bf16[16,48,128]{2,1,0:T(8,128)(2,1)S(1)}, bf16[16,48,128]{2,1,0:T(8,128)(2,1)S(1)}, u32[]{:S(2)}, u32[]{:S(2)}) collective-permute-start(bf16[16,48,128]{2,1,0:T(8,128)(2,1)S(1)} %get-tuple-element.20), channel_id=1, source_target_pairs={{0,1},{1,0},{2,3},{3,2},{4,5},{5,4},{6,7},{7,6},{8,9},{9,8},{10,11... | collective-permute-start | bytes 589832 | tf_op jit(solution)/shard_map/ppermute | solution.py:232
  2.5 0.1 copy-done.4
  2.6 0.2 convert_reduce_fusion
  2.8 0.8 %collective-permute-done.taken_ref = bf16[16,48,128]{2,1,0:T(8,128)(2,1)S(1)} collective-permute-done((bf16[16,48,128]{2,1,0:T(8,128)(2,1)S(1)}, bf16[16,48,128]{2,1,0:T(8,128)(2,1)S(1)}, u32[]{:S(2)}, u32[]{:S(2)}) %collective-permute-start) | collective-permute-done | bytes 196640 | tf_op jit(solution)/shard_map/ppermute | solution.py:232
  3.5 0.0 copy-done.1
  3.5 0.0 copy-done.2
  3.5 0.0 copy-done.3
  3.6 13.6 %all_to_all.10.pieces_ref = bf16[16,48,128]{2,1,0:T(8,128)(2,1)S(1)} all-to-all(bf16[16,48,128]{2,1,0:T(8,128)(2,1)S(1)} %get-tuple-element.22), channel_id=1, replica_groups={{22,20,18,16,30,28,26,24,6,4,2,0,14,12,10,8},{23,31,7,15,21,29,5,13,19,..., dimensions={0} | all-to-all | bytes 393216 | tf_op jit(solution)/shard_map/all_to_all | solution.py:236
  17.2 0.4 %shard_map.86 = (f32[48,128]{1,0:T(8,128)S(1)}, f32[48,128]{1,0:T(8,128)S(1)}, f32[48,128]{1,0:T(8,128)S(1)}, bf16[16,24,256]{2,1,0:T(8,128)(2,1)S(1)}) custom-call(s32[1,24]{1,0:T(1,128)S(1)} %get-tuple-element.21.position_ref, bf16[16,48,128]{2,1,0:T(8,128)(2,1)S(1)} %all_to_all.10.pieces_ref, f32[48,128]{1,0:T(8,128)S(1)} %get-tuple-element.23.master_ref, ...), custom_call_target="tpu_custom_call" | custom-call | tf_op jit(solution)/shard_map/pallas_call | solution.py:141
  17.6 11.9 %all_to_all.11.own_ref = bf16[16,24,256]{2,1,0:T(8,128)(2,1)S(1)} all-to-all(bf16[16,24,256]{2,1,0:T(8,128)(2,1)S(1)} %get-tuple-element.29), channel_id=1, replica_groups={{14,12,10,8,6,4,2,0,30,28,26,24,22,20,18,16},{15,7,31,23,13,5,29,21,11,..., dimensions={0} | all-to-all | bytes 393216 | tf_op jit(solution)/shard_map/all_to_all | solution.py:239
  29.5 0.0 collective-permute-start.1
  29.5 1.4 %collective-permute-done.1.other_ref = bf16[16,24,256]{2,1,0:T(8,128)(2,1)S(1)} collective-permute-done((bf16[16,24,256]{2,1,0:T(8,128)(2,1)S(1)}, bf16[16,24,256]{2,1,0:T(8,128)(2,1)S(1)}, u32[]{:S(2)}, u32[]{:S(2)}) %collective-permute-start.1) | collective-permute-done | bytes 196640 | tf_op jit(solution)/shard_map/ppermute | solution.py:240
  30.9 0.9 %shard_map.87 = (f32[48,128]{1,0:T(8,128)}, f32[48,128]{1,0:T(8,128)}, f32[48,128]{1,0:T(8,128)}, bf16[24,8192]{1,0:T(8,128)(2,1)}) custom-call(s32[1,24]{1,0:T(1,128)S(1)} %get-tuple-element.21.position_ref, f32[48,128]{1,0:T(8,128)S(1)} %get-tuple-element.26.new_first_ref, f32[48,128]{1,0:T(8,128)S(1)} %get-tuple-element.27.new_second_ref, ...), custom_call_target="tpu_custom_call" | custom-call | tf_op jit(solution)/shard_map/pallas_call | solution.py:198
  (1 shorter events, 0.0 us)
Async XLA Ops:
  0.6 1.1 %copy-start = (bf16[1,196608]{1,0:T(2,128)(2,1)S(1)}, bf16[1,196608]{1,0:T(2,128)(2,1)}, u32[]{:S(2)}) copy-start(bf16[1,196608]{1,0:T(2,128)(2,1)} %grads_ref.1) | copy-start | bytes 1179652
  1.8 1.8 %copy-start.1 = (f32[6144]{0:T(1024)S(1)}, f32[6144]{0:T(1024)}, u32[]{:S(2)}) copy-start(f32[6144]{0:T(1024)} %param.6) | copy-start | bytes 73732
  1.8 1.8 %copy-start.2 = (f32[6144]{0:T(1024)S(1)}, f32[6144]{0:T(1024)}, u32[]{:S(2)}) copy-start(f32[6144]{0:T(1024)} %param.7) | copy-start | bytes 73732
  1.8 1.8 %copy-start.3 = (f32[6144]{0:T(1024)S(1)}, f32[6144]{0:T(1024)}, u32[]{:S(2)}) copy-start(f32[6144]{0:T(1024)} %param.8) | copy-start | bytes 73732
  1.9 0.7 %copy-start.4 = (s32[24]{0:T(128)S(1)}, s32[24]{0:T(128)}, u32[]{:S(2)}) copy-start(s32[24]{0:T(128)} %param.9) | copy-start | bytes 292
  1.9 1.6 %collective-permute-start = (bf16[16,48,128]{2,1,0:T(8,128)(2,1)S(1)}, bf16[16,48,128]{2,1,0:T(8,128)(2,1)S(1)}, u32[]{:S(2)}, u32[]{:S(2)}) collective-permute-start(bf16[16,48,128]{2,1,0:T(8,128)(2,1)S(1)} %get-tuple-element.20), channel_id=1, source_target_pairs={{0,1},{1,0},{2,3},{3,2},{4,5},{5,4},{6,7},{7,6},{8,9},{9,8},{10,11... | collective-permute-start | bytes 589832 | tf_op jit(solution)/shard_map/ppermute | solution.py:232
  29.5 1.4 %collective-permute-start.1 = (bf16[16,24,256]{2,1,0:T(8,128)(2,1)S(1)}, bf16[16,24,256]{2,1,0:T(8,128)(2,1)S(1)}, u32[]{:S(2)}, u32[]{:S(2)}) collective-permute-start(bf16[16,24,256]{2,1,0:T(8,128)(2,1)S(1)} %all_to_all.11.own_ref), channel_id=1, source_target_pairs={{0,1},{1,0},{2,3},{3,2},{4,5},{5,4},{6,7},{7,6},{8,9},{9,8},{10,11... | collective-permute-start | bytes 589832 | tf_op jit(solution)/shard_map/ppermute | solution.py:240

commit v19 on v17

--- a/solution.py
+++ b/solution.py
@@ -18,6 +18,7 @@
 AXES = ("shard", "replica")
 LANES = 128
 FIRST = 11
+BY_LAYER = (True, False)
 PLANE = 4
 
 
@@ -41,22 +42,22 @@
     return pltpu.CompilerParams(vmem_limit_bytes=6 * 2**20, **more)
 
 
-def place_of(chip):
+def place_of(chip, step):
     by_layer = chip ^ FIRST
     by_column = by_layer % PLANE * PLANE + by_layer // PLANE
-    return by_column, by_column
-
-
-def groups(chips):
+    return by_layer if BY_LAYER[step] else by_column, by_column
+
+
+def groups(chips, step):
     lists = [[0] * chips, [0] * chips]
     for chip in range(chips):
-        for core, place in enumerate(place_of(chip)):
+        for core, place in enumerate(place_of(chip, step)):
             lists[core][place] = 2 * chip + core
     return lists
 
 
-def slot(chip, core):
-    places = place_of(chip)
+def slot(chip, core, step):
+    places = place_of(chip, step)
     return jnp.where(core == 0, places[0], places[1])
 
 
@@ -68,7 +69,7 @@
         for ref, place in ((kept_ref, core), (sent_ref, 1 - core)):
             start = pl.multiple_of((2 * k + place) * width, width)
             row = grads_ref[:, pl.ds(start, width)].astype(jnp.float32)
-            ref[slot(k, place)] = row.reshape(lines, lanes).astype(jnp.bfloat16)
+            ref[slot(k, place, 0)] = row.reshape(lines, lanes).astype(jnp.bfloat16)
 
 
 def pack(grads, chips, lines):
@@ -170,7 +171,7 @@
         for k in range(p * each, (p + 1) * each):
             for ref, place in ((own_ref, core), (other_ref, 1 - core)):
                 start = pl.multiple_of((2 * k + place) * width, width)
-                scaled = ref[slot(k, place)].astype(jnp.float32) * factor
+                scaled = ref[slot(k, place, 1)].astype(jnp.float32) * factor
                 scaled_ref[:, pl.ds(start, width)] = scaled.astype(jnp.bfloat16)
         part = pl.ds(p * 2 * each * width, 2 * each * width)
         copies.append(pltpu.make_async_copy(scaled_ref.at[:, part], copy_out.at[:, part], sems.at[3 + p]))
@@ -233,9 +234,9 @@
         taken = lax.ppermute(sent, "replica", [(0, 1), (1, 0)])
         states = (master, first_moment, second_moment)
         position, *states, pairs = add_pairs(kept, taken, flat_positions(owners), states)
-        pieces = lax.all_to_all(pairs, AXES, 0, 0, tiled=True, axis_index_groups=groups(shards))
+        pieces = lax.all_to_all(pairs, AXES, 0, 0, tiled=True, axis_index_groups=groups(shards, 0))
         *updated, copies = middle(position, pieces, states, devices)
-        own = lax.all_to_all(copies, AXES, 0, 0, tiled=True, axis_index_groups=groups(shards))
+        own = lax.all_to_all(copies, AXES, 0, 0, tiled=True, axis_index_groups=groups(shards, 1))
         other = lax.ppermute(own, "replica", [(0, 1), (1, 0)])
         *flat, model_copy = finish(position, *updated, own, other)
         return (*(x.reshape(-1) for x in flat), model_copy)

time: 31 us -> 31 us (level)
    all_to_all x1, blocking collectives: 14 us -> 13.6 us  [on_device(): lax.all_to_all(pairs, AXES, 0, 0, tiled=True, axis_index_groups=groups(sh...]
    all_to_all x1, blocking collectives: 10.3 us -> 10.7 us  [on_device(): lax.all_to_all(copies, AXES, 0, 0, tiled=True, axis_index_groups=groups(s...]
where the time goes in v19:
time: 31 us; the launch traced here: 30.7 us
  blocking collectives  24.3 us (78%)
  waiting for transfers between devices  2.2 us (7%)
  Pallas kernels  1.56 us (5%)
  local copies, waits for them, and re-layouts  1.27 us (4%)
  between operations  0.67 us (2%)
  starting transfers between devices  0.52 us (2%)
    all_to_all x1, blocking collectives, on_device(): lax.all_to_all(pairs, AXES, 0, 0, tiled=True, axis_index_groups=groups(sh...  13.6 us
    all_to_all x1, blocking collectives, on_device(): lax.all_to_all(copies, AXES, 0, 0, tiled=True, axis_index_groups=groups(s...  10.7 us
    ppermute x1, waiting for transfers between devices, on_device(): other = lax.ppermute(own, 'replica', [(0, 1), (1, 0)])  1.44 us
    unnamed x10, local copies, waits for them, and re-layouts  1.27 us
    pallas_call x1, Pallas kernels, finish(): pl.pallas_call(finish_kernel, in_specs=[pl.BlockSpec(memory_space=pltpu.V...  0.93 us
    ppermute x1, waiting for transfers between devices, on_device(): taken = lax.ppermute(sent, 'replica', [(0, 1), (1, 0)])  0.76 us
  transfers between devices with their start and end apart: 2, of which 2 were waited for; matrix products, arithmetic and copies ran while one was open for 1% of the time, Pallas kernels for 0%

profile of v19, /device:TPU:0, one launch (start us, length us, event | category | flops | bytes accessed | tf_op | source)
XLA Modules:
  0.0 30.7 jit_solution(7903080072722124338)
XLA Ops:
  0.6 0.0 copy-start
  0.6 1.1 %copy-done = bf16[1,196608]{1,0:T(2,128)(2,1)S(1)} copy-done((bf16[1,196608]{1,0:T(2,128)(2,1)S(1)}, bf16[1,196608]{1,0:T(2,128)(2,1)}, u32[]{:S(2)}) %copy-start) | copy-done | bytes 393240
  1.8 0.0 copy-start.1
  1.8 0.0 copy-start.2
  1.8 0.0 copy-start.3
  1.8 0.1 shard_map.84
  1.9 0.0 copy-start.4
  1.9 0.5 %collective-permute-start = (bf16[16,48,128]{2,1,0:T(8,128)(2,1)S(1)}, bf16[16,48,128]{2,1,0:T(8,128)(2,1)S(1)}, u32[]{:S(2)}, u32[]{:S(2)}) collective-permute-start(bf16[16,48,128]{2,1,0:T(8,128)(2,1)S(1)} %get-tuple-element.20), channel_id=1, source_target_pairs={{0,1},{1,0},{2,3},{3,2},{4,5},{5,4},{6,7},{7,6},{8,9},{9,8},{10,11... | collective-permute-start | bytes 589832 | tf_op jit(solution)/shard_map/ppermute | solution.py:234
  2.5 0.1 copy-done.4
  2.6 0.2 convert_reduce_fusion
  2.8 0.8 %collective-permute-done.taken_ref = bf16[16,48,128]{2,1,0:T(8,128)(2,1)S(1)} collective-permute-done((bf16[16,48,128]{2,1,0:T(8,128)(2,1)S(1)}, bf16[16,48,128]{2,1,0:T(8,128)(2,1)S(1)}, u32[]{:S(2)}, u32[]{:S(2)}) %collective-permute-start) | collective-permute-done | bytes 196640 | tf_op jit(solution)/shard_map/ppermute | solution.py:234
  3.5 0.0 copy-done.1
  3.5 0.0 copy-done.2
  3.5 0.0 copy-done.3
  3.6 13.6 %all_to_all.10.pieces_ref = bf16[16,48,128]{2,1,0:T(8,128)(2,1)S(1)} all-to-all(bf16[16,48,128]{2,1,0:T(8,128)(2,1)S(1)} %get-tuple-element.22), channel_id=1, replica_groups={{22,20,18,16,30,28,26,24,6,4,2,0,14,12,10,8},{23,31,7,15,21,29,5,13,19,..., dimensions={0} | all-to-all | bytes 393216 | tf_op jit(solution)/shard_map/all_to_all | solution.py:237
  17.2 0.4 %shard_map.86 = (f32[48,128]{1,0:T(8,128)S(1)}, f32[48,128]{1,0:T(8,128)S(1)}, f32[48,128]{1,0:T(8,128)S(1)}, bf16[16,24,256]{2,1,0:T(8,128)(2,1)S(1)}) custom-call(s32[1,24]{1,0:T(1,128)S(1)} %get-tuple-element.21.position_ref, bf16[16,48,128]{2,1,0:T(8,128)(2,1)S(1)} %all_to_all.10.pieces_ref, f32[48,128]{1,0:T(8,128)S(1)} %get-tuple-element.23.master_ref, ...), custom_call_target="tpu_custom_call" | custom-call | tf_op jit(solution)/shard_map/pallas_call | solution.py:143
  17.6 10.7 %all_to_all.11.own_ref = bf16[16,24,256]{2,1,0:T(8,128)(2,1)S(1)} all-to-all(bf16[16,24,256]{2,1,0:T(8,128)(2,1)S(1)} %get-tuple-element.29), channel_id=1, replica_groups={{22,30,6,14,20,28,4,12,18,26,2,10,16,24,0,8},{23,31,7,15,21,29,5,13,19,..., dimensions={0} | all-to-all | bytes 393216 | tf_op jit(solution)/shard_map/all_to_all | solution.py:239
  28.3 0.0 collective-permute-start.1
  28.3 1.4 %collective-permute-done.1.other_ref = bf16[16,24,256]{2,1,0:T(8,128)(2,1)S(1)} collective-permute-done((bf16[16,24,256]{2,1,0:T(8,128)(2,1)S(1)}, bf16[16,24,256]{2,1,0:T(8,128)(2,1)S(1)}, u32[]{:S(2)}, u32[]{:S(2)}) %collective-permute-start.1) | collective-permute-done | bytes 196640 | tf_op jit(solution)/shard_map/ppermute | solution.py:240
  29.8 0.9 %shard_map.87 = (f32[48,128]{1,0:T(8,128)}, f32[48,128]{1,0:T(8,128)}, f32[48,128]{1,0:T(8,128)}, bf16[24,8192]{1,0:T(8,128)(2,1)}) custom-call(s32[1,24]{1,0:T(1,128)S(1)} %get-tuple-element.21.position_ref, f32[48,128]{1,0:T(8,128)S(1)} %get-tuple-element.26.new_first_ref, f32[48,128]{1,0:T(8,128)S(1)} %get-tuple-element.27.new_second_ref, ...), custom_call_target="tpu_custom_call" | custom-call | tf_op jit(solution)/shard_map/pallas_call | solution.py:200
  (1 shorter events, 0.0 us)
Async XLA Ops:
  0.6 1.1 %copy-start = (bf16[1,196608]{1,0:T(2,128)(2,1)S(1)}, bf16[1,196608]{1,0:T(2,128)(2,1)}, u32[]{:S(2)}) copy-start(bf16[1,196608]{1,0:T(2,128)(2,1)} %grads_ref.1) | copy-start | bytes 1179652
  1.8 1.8 %copy-start.1 = (f32[6144]{0:T(1024)S(1)}, f32[6144]{0:T(1024)}, u32[]{:S(2)}) copy-start(f32[6144]{0:T(1024)} %param.6) | copy-start | bytes 73732
  1.8 1.8 %copy-start.2 = (f32[6144]{0:T(1024)S(1)}, f32[6144]{0:T(1024)}, u32[]{:S(2)}) copy-start(f32[6144]{0:T(1024)} %param.7) | copy-start | bytes 73732
  1.8 1.8 %copy-start.3 = (f32[6144]{0:T(1024)S(1)}, f32[6144]{0:T(1024)}, u32[]{:S(2)}) copy-start(f32[6144]{0:T(1024)} %param.8) | copy-start | bytes 73732
  1.9 0.7 %copy-start.4 = (s32[24]{0:T(128)S(1)}, s32[24]{0:T(128)}, u32[]{:S(2)}) copy-start(s32[24]{0:T(128)} %param.9) | copy-start | bytes 292
  1.9 1.6 %collective-permute-start = (bf16[16,48,128]{2,1,0:T(8,128)(2,1)S(1)}, bf16[16,48,128]{2,1,0:T(8,128)(2,1)S(1)}, u32[]{:S(2)}, u32[]{:S(2)}) collective-permute-start(bf16[16,48,128]{2,1,0:T(8,128)(2,1)S(1)} %get-tuple-element.20), channel_id=1, source_target_pairs={{0,1},{1,0},{2,3},{3,2},{4,5},{5,4},{6,7},{7,6},{8,9},{9,8},{10,11... | collective-permute-start | bytes 589832 | tf_op jit(solution)/shard_map/ppermute | solution.py:234
  28.3 1.4 %collective-permute-start.1 = (bf16[16,24,256]{2,1,0:T(8,128)(2,1)S(1)}, bf16[16,24,256]{2,1,0:T(8,128)(2,1)S(1)}, u32[]{:S(2)}, u32[]{:S(2)}) collective-permute-start(bf16[16,24,256]{2,1,0:T(8,128)(2,1)S(1)} %all_to_all.11.own_ref), channel_id=1, source_target_pairs={{0,1},{1,0},{2,3},{3,2},{4,5},{5,4},{6,7},{7,6},{8,9},{9,8},{10,11... | collective-permute-start | bytes 589832 | tf_op jit(solution)/shard_map/ppermute | solution.py:240

commit v20 on v18

--- a/solution.py
+++ b/solution.py
@@ -17,7 +17,7 @@
 second_correction = 1.0 - 0.95**20
 AXES = ("shard", "replica")
 LANES = 128
-FIRST = (11, 7)
+FIRST = (11, 10)
 PLANE = 4
 
 

time: 32.2 us -> 31.7 us (0.984)
  blocking collectives: 25.5 us -> 24.9 us
    all_to_all x1, blocking collectives: 11.9 us -> 11.3 us  [on_device(): lax.all_to_all(copies, AXES, 0, 0, tiled=True, axis_index_groups=lists)]
where the time goes in v20:
time: 31.7 us; the launch traced here: 31.4 us
  blocking collectives  24.9 us (79%)
  waiting for transfers between devices  2.2 us (7%)
  Pallas kernels  1.59 us (5%)
  local copies, waits for them, and re-layouts  1.27 us (4%)
  between operations  0.67 us (2%)
  starting transfers between devices  0.52 us (2%)
    all_to_all x1, blocking collectives, on_device(): lax.all_to_all(pairs, AXES, 0, 0, tiled=True, axis_index_groups=lists)  13.6 us
    all_to_all x1, blocking collectives, on_device(): lax.all_to_all(copies, AXES, 0, 0, tiled=True, axis_index_groups=lists)  11.3 us
    ppermute x1, waiting for transfers between devices, on_device(): other = lax.ppermute(own, 'replica', [(0, 1), (1, 0)])  1.44 us
    unnamed x10, local copies, waits for them, and re-layouts  1.27 us
    pallas_call x1, Pallas kernels, finish(): pl.pallas_call(finish_kernel, in_specs=[pl.BlockSpec(memory_space=pltpu.V...  0.95 us
    ppermute x1, waiting for transfers between devices, on_device(): taken = lax.ppermute(sent, 'replica', [(0, 1), (1, 0)])  0.76 us
  transfers between devices with their start and end apart: 2, of which 2 were waited for; matrix products, arithmetic and copies ran while one was open for 1% of the time, Pallas kernels for 0%

profile of v20, /device:TPU:0, one launch (start us, length us, event | category | flops | bytes accessed | tf_op | source)
XLA Modules:
  0.0 31.4 jit_solution(2666601721766718573)
XLA Ops:
  0.6 0.0 copy-start
  0.6 1.1 %copy-done = bf16[1,196608]{1,0:T(2,128)(2,1)S(1)} copy-done((bf16[1,196608]{1,0:T(2,128)(2,1)S(1)}, bf16[1,196608]{1,0:T(2,128)(2,1)}, u32[]{:S(2)}) %copy-start) | copy-done | bytes 393240
  1.8 0.0 copy-start.1
  1.8 0.0 copy-start.2
  1.8 0.0 copy-start.3
  1.8 0.1 shard_map.84
  1.9 0.0 copy-start.4
  1.9 0.5 %collective-permute-start = (bf16[16,48,128]{2,1,0:T(8,128)(2,1)S(1)}, bf16[16,48,128]{2,1,0:T(8,128)(2,1)S(1)}, u32[]{:S(2)}, u32[]{:S(2)}) collective-permute-start(bf16[16,48,128]{2,1,0:T(8,128)(2,1)S(1)} %get-tuple-element.20), channel_id=1, source_target_pairs={{0,1},{1,0},{2,3},{3,2},{4,5},{5,4},{6,7},{7,6},{8,9},{9,8},{10,11... | collective-permute-start | bytes 589832 | tf_op jit(solution)/shard_map/ppermute | solution.py:232
  2.5 0.1 copy-done.4
  2.6 0.2 convert_reduce_fusion
  2.8 0.8 %collective-permute-done.taken_ref = bf16[16,48,128]{2,1,0:T(8,128)(2,1)S(1)} collective-permute-done((bf16[16,48,128]{2,1,0:T(8,128)(2,1)S(1)}, bf16[16,48,128]{2,1,0:T(8,128)(2,1)S(1)}, u32[]{:S(2)}, u32[]{:S(2)}) %collective-permute-start) | collective-permute-done | bytes 196640 | tf_op jit(solution)/shard_map/ppermute | solution.py:232
  3.5 0.0 copy-done.1
  3.5 0.0 copy-done.2
  3.5 0.0 copy-done.3
  3.6 13.6 %all_to_all.10.pieces_ref = bf16[16,48,128]{2,1,0:T(8,128)(2,1)S(1)} all-to-all(bf16[16,48,128]{2,1,0:T(8,128)(2,1)S(1)} %get-tuple-element.22), channel_id=1, replica_groups={{22,20,18,16,30,28,26,24,6,4,2,0,14,12,10,8},{23,31,7,15,21,29,5,13,19,..., dimensions={0} | all-to-all | bytes 393216 | tf_op jit(solution)/shard_map/all_to_all | solution.py:236
  17.2 0.4 %shard_map.86 = (f32[48,128]{1,0:T(8,128)S(1)}, f32[48,128]{1,0:T(8,128)S(1)}, f32[48,128]{1,0:T(8,128)S(1)}, bf16[16,24,256]{2,1,0:T(8,128)(2,1)S(1)}) custom-call(s32[1,24]{1,0:T(1,128)S(1)} %get-tuple-element.21.position_ref, bf16[16,48,128]{2,1,0:T(8,128)(2,1)S(1)} %all_to_all.10.pieces_ref, f32[48,128]{1,0:T(8,128)S(1)} %get-tuple-element.23.master_ref, ...), custom_call_target="tpu_custom_call" | custom-call | tf_op jit(solution)/shard_map/pallas_call | solution.py:141
  17.6 11.3 %all_to_all.11.own_ref = bf16[16,24,256]{2,1,0:T(8,128)(2,1)S(1)} all-to-all(bf16[16,24,256]{2,1,0:T(8,128)(2,1)S(1)} %get-tuple-element.29), channel_id=1, replica_groups={{20,22,16,18,28,30,24,26,4,6,0,2,12,14,8,10},{21,29,5,13,23,31,7,15,17,..., dimensions={0} | all-to-all | bytes 393216 | tf_op jit(solution)/shard_map/all_to_all | solution.py:239
  29.0 0.0 collective-permute-start.1
  29.0 1.4 %collective-permute-done.1.other_ref = bf16[16,24,256]{2,1,0:T(8,128)(2,1)S(1)} collective-permute-done((bf16[16,24,256]{2,1,0:T(8,128)(2,1)S(1)}, bf16[16,24,256]{2,1,0:T(8,128)(2,1)S(1)}, u32[]{:S(2)}, u32[]{:S(2)}) %collective-permute-start.1) | collective-permute-done | bytes 196640 | tf_op jit(solution)/shard_map/ppermute | solution.py:240
  30.4 1.0 %shard_map.87 = (f32[48,128]{1,0:T(8,128)}, f32[48,128]{1,0:T(8,128)}, f32[48,128]{1,0:T(8,128)}, bf16[24,8192]{1,0:T(8,128)(2,1)}) custom-call(s32[1,24]{1,0:T(1,128)S(1)} %get-tuple-element.21.position_ref, f32[48,128]{1,0:T(8,128)S(1)} %get-tuple-element.26.new_first_ref, f32[48,128]{1,0:T(8,128)S(1)} %get-tuple-element.27.new_second_ref, ...), custom_call_target="tpu_custom_call" | custom-call | tf_op jit(solution)/shard_map/pallas_call | solution.py:198
  (1 shorter events, 0.0 us)
Async XLA Ops:
  0.6 1.1 %copy-start = (bf16[1,196608]{1,0:T(2,128)(2,1)S(1)}, bf16[1,196608]{1,0:T(2,128)(2,1)}, u32[]{:S(2)}) copy-start(bf16[1,196608]{1,0:T(2,128)(2,1)} %grads_ref.1) | copy-start | bytes 1179652
  1.8 1.8 %copy-start.1 = (f32[6144]{0:T(1024)S(1)}, f32[6144]{0:T(1024)}, u32[]{:S(2)}) copy-start(f32[6144]{0:T(1024)} %param.6) | copy-start | bytes 73732
  1.8 1.8 %copy-start.2 = (f32[6144]{0:T(1024)S(1)}, f32[6144]{0:T(1024)}, u32[]{:S(2)}) copy-start(f32[6144]{0:T(1024)} %param.7) | copy-start | bytes 73732
  1.8 1.8 %copy-start.3 = (f32[6144]{0:T(1024)S(1)}, f32[6144]{0:T(1024)}, u32[]{:S(2)}) copy-start(f32[6144]{0:T(1024)} %param.8) | copy-start | bytes 73732
  1.9 0.7 %copy-start.4 = (s32[24]{0:T(128)S(1)}, s32[24]{0:T(128)}, u32[]{:S(2)}) copy-start(s32[24]{0:T(128)} %param.9) | copy-start | bytes 292
  1.9 1.6 %collective-permute-start = (bf16[16,48,128]{2,1,0:T(8,128)(2,1)S(1)}, bf16[16,48,128]{2,1,0:T(8,128)(2,1)S(1)}, u32[]{:S(2)}, u32[]{:S(2)}) collective-permute-start(bf16[16,48,128]{2,1,0:T(8,128)(2,1)S(1)} %get-tuple-element.20), channel_id=1, source_target_pairs={{0,1},{1,0},{2,3},{3,2},{4,5},{5,4},{6,7},{7,6},{8,9},{9,8},{10,11... | collective-permute-start | bytes 589832 | tf_op jit(solution)/shard_map/ppermute | solution.py:232
  29.0 1.4 %collective-permute-start.1 = (bf16[16,24,256]{2,1,0:T(8,128)(2,1)S(1)}, bf16[16,24,256]{2,1,0:T(8,128)(2,1)S(1)}, u32[]{:S(2)}, u32[]{:S(2)}) collective-permute-start(bf16[16,24,256]{2,1,0:T(8,128)(2,1)S(1)} %all_to_all.11.own_ref), channel_id=1, source_target_pairs={{0,1},{1,0},{2,3},{3,2},{4,5},{5,4},{6,7},{7,6},{8,9},{9,8},{10,11... | collective-permute-start | bytes 589832 | tf_op jit(solution)/shard_map/ppermute | solution.py:240
